TPU v7x, 32 devices: a whole 2x2x4 slice. The times are simulated.
32 devices in a mesh: seq: 8 (over z, x), tp: 4 (over y, core).
Axes of the slice: x: 2, y: 2, z: 4, core: 2. Of those that a mesh axis runs over, the one named last changes fastest.
Arguments:
- residual: bfloat16 [1536, 8192], P('seq', 'tp'), may hold values from -6 to 6
- attention: bfloat16 [384, 8192], P('seq'), may hold values from -6 to 6
- quantized_codes: int32 [8192, 8192], P('seq', 'tp'), may hold values from 0 to 15
- absmax: float32 [8192, 128], P('seq', 'tp'), may hold values from 0.005 to 0.05
- adapter_down: bfloat16 [8192, 64], P('seq'), may hold values from -0.0625 to 0.0625
- adapter_up: bfloat16 [64, 8192], P(None, 'tp'), may hold values from -0.75 to 0.75
- routed_slot_gate: float32 [384], P('seq'), may hold values from 0.2 to 1
- selected: int32 [384], P('seq'), may hold values from 0 to 191, as said below
- counts: int32 [8], P('seq'), may hold values from 1 to 48, 192 in all
- cotangent: bfloat16 [1536, 8192], P('seq', 'tp'), may hold values from -0.59765625 to 0.59765625
Outputs:
- outgoing_residual: bfloat16 [1536, 8192], P('seq', 'tp')
- attention_output_grad: bfloat16 [384, 8192], P(None, 'seq')
- adapter_down_gradient: float32 [8192, 64], P('seq')
- adapter_up_gradient: float32 [64, 8192], P(None, 'tp')
- router_gate_gradient: float32 [384], P('seq')
Inputs may be any that keep to these rules, and one draw needn't show every extreme that they name: `counts`: every shard has at least one live slot, all shards together have 192, and some shard has all 48 slots live. `selected`: within each shard's 48 slots the entries are distinct token positions of that shard; only the first counts entries of a shard are live.
All inputs are finite; a program needn't handle non-finite values.
Results may differ from a plain program's by a relative error of at most 0.0058.
Values may be sent and summed in bfloat16 or wider, within the bound.
No kernel may reach another device: no remote copies, remote signals or barrier semaphores. Data moves between devices by JAX's collectives and lax.ppermute only.
A program may use at most 128 MiB of HBM per device.

v0:
```python
import jax
import jax.numpy as jnp
from jax import lax
from jax.sharding import PartitionSpec as P

LEVELS = (
    -1.0,
    -0.6961928009986877,
    -0.5250730514526367,
    -0.39491748809814453,
    -0.28444138169288635,
    -0.18477343022823334,
    -0.09105003625154495,
    0.0,
    0.07958029955625534,
    0.16093020141124725,
    0.24611230194568634,
    0.33791524171829224,
    0.44070982933044434,
    0.5626170039176941,
    0.7229568362236023,
    1.0,
)
adapter_scale = 0.25


def precise_matmul(left, right):
    return jnp.dot(left, right, precision=lax.Precision.HIGHEST, preferred_element_type=jnp.float32)


def dequantize(quantized_codes, absmax):
    quantile_levels = jnp.zeros(quantized_codes.shape, jnp.float32)
    for level_code in range(16):
        quantile_levels = quantile_levels + jnp.where(
            quantized_codes == level_code, LEVELS[level_code], 0.0
        )
    block_size = quantized_codes.shape[1] // absmax.shape[1]
    scales = jnp.repeat(absmax, block_size, axis=1)
    return (quantile_levels * scales).astype(jnp.bfloat16)


def body(
    residual,
    attention,
    quantized_codes,
    absmax,
    adapter_down,
    adapter_up,
    routed_slot_gate,
    selected,
    counts,
    cotangent,
):
    projection_weight = dequantize(quantized_codes, absmax)
    adapter_up_single32 = adapter_up.astype(jnp.float32)
    home_slots = attention.shape[0]
    live_slot = jnp.arange(home_slots, dtype=jnp.int32) < counts[0]
    target = jnp.where(live_slot, selected, residual.shape[0])
    full_w, full_a = (
        lax.all_gather(projection_weight, "seq", axis=0, tiled=True),
        lax.all_gather(adapter_down, "seq", axis=0, tiled=True),
    )
    adapter_product = jnp.dot(attention, full_a, preferred_element_type=jnp.float32)
    block_output = jnp.dot(
        attention, full_w, preferred_element_type=jnp.float32
    ) + adapter_scale * precise_matmul(adapter_product, adapter_up_single32)
    picked = residual[selected].astype(jnp.float32)
    updated = (picked + routed_slot_gate[:, None] * block_output).astype(jnp.bfloat16)
    outgoing_residual = residual.at[target].set(updated, mode="drop")
    upstream = jnp.where(live_slot[:, None], cotangent[selected].astype(jnp.float32), 0.0)
    gate_part = jnp.sum(upstream * block_output, axis=1)
    output_gradient = (routed_slot_gate[:, None] * upstream).astype(jnp.bfloat16)
    head_part = jnp.dot(output_gradient, full_w.T, preferred_element_type=jnp.float32)
    adapter_rank_piece = adapter_scale * jnp.dot(
        output_gradient, adapter_up.T, preferred_element_type=jnp.float32
    )
    head_full, rank_full, router_gate_gradient = lax.psum(
        (head_part, adapter_rank_piece, gate_part), "tp"
    )
    adapter_rank_gradient = rank_full.astype(jnp.bfloat16)
    home_grad = (
        head_full + jnp.dot(adapter_rank_gradient, full_a.T, preferred_element_type=jnp.float32)
    ).astype(jnp.bfloat16)
    attention_output_grad = lax.all_to_all(
        home_grad, "seq", split_axis=1, concat_axis=0, tiled=True
    )
    adapter_down_gradient = lax.psum_scatter(
        jnp.dot(attention.T, adapter_rank_gradient, preferred_element_type=jnp.float32),
        "seq",
        scatter_dimension=0,
        tiled=True,
    )
    up_factor_piece = adapter_scale * precise_matmul(
        adapter_product.T, output_gradient.astype(jnp.float32)
    )
    adapter_up_gradient = lax.psum(up_factor_piece, "seq")
    return (
        outgoing_residual,
        attention_output_grad,
        adapter_down_gradient,
        adapter_up_gradient,
        router_gate_gradient,
    )


def solution(mesh):
    return jax.shard_map(
        body,
        mesh=mesh,
        in_specs=(
            P("seq", "tp"),
            P("seq", None),
            P("seq", "tp"),
            P("seq", "tp"),
            P("seq", None),
            P(None, "tp"),
            P("seq"),
            P("seq"),
            P("seq"),
            P("seq", "tp"),
        ),
        out_specs=(P("seq", "tp"), P(None, "seq"), P("seq", None), P(None, "tp"), P("seq")),
        check_vma=False,
    )
```

profile of v0, /device:TPU:0, one launch (start us, length us, event | category | flops | bytes accessed | tf_op | source)
XLA Modules:
  0.0 922.6 jit_solution(5490296936160284484)
XLA Ops:
  7.2 0.0 all-gather.3.cloned.1.call-start
  7.2 9.4 %copy.33 = s32[1024,2048]{0,1:T(8,128)} copy(s32[1024,2048]{1,0:T(8,128)} %param.12) | data formatting | bytes 16777216 | tf_op args[2]
  16.6 14.7 %fusion.1 = bf16[1024,2048]{0,1:T(8,128)(2,1)} fusion(s32[1024,2048]{0,1:T(8,128)} %copy.33, f32[1024,32]{0,1:T(8,128)S(1)} %copy-done.6), kind=kLoop, calls=%fused_computation.7 | loop fusion | flops 96468992 | bytes 12713984 | tf_op jit(solution)/shard_map/convert_element_type | solution.py:39
  31.4 0.0 all-gather.3.cloned.1.call-update
  31.4 0.0 all-gather.5.cloned.1.call-start
  31.4 0.7 all-gather.5.cloned.1.call-update
  32.1 0.0 all-reduce.4.cloned.1.call-start
  32.9 0.7 gather_fusion
  33.6 638.4 %all-gather.3.cloned.1.call-done = bf16[8192,2048]{0,1:T(8,128)(2,1)} async-done(((bf16[1024,2048]{0,1:T(8,128)(2,1)}), bf16[8192,2048]{0,1:T(8,128)(2,1)}) %all-gather.3.cloned.1.call-update) | async-done | bytes 33554448 | tf_op jit(solution)/shard_map/all_gather | solution.py:60
  672.0 14.9 %fusion.8 = f32[48,8192]{1,0:T(8,128)} fusion(bf16[8192,2048]{0,1:T(8,128)(2,1)} %all-gather.3.cloned.1.call-done, bf16[48,2048]{1,0:T(8,128)(2,1)S(1)} %gather_fusion, f32[48]{0:T(128)S(1)} %copy-done.7, pred[48]{0:T(512)(128)(4,1)S(1)} %iota_compare_fusion), kind=kOutput, calls=%fused_computation.27 | convolution fusion | flops 1611005952 | bytes 35324144 | tf_op jit(solution)/shard_map/dot_general | solution.py:73
  686.8 0.0 all-reduce.4.cloned.1.call-update
  686.9 0.0 all-reduce.6.cloned.1.call-start
  686.9 0.3 convolution_multiply_fusion.2
  687.2 27.1 %all-gather.5.cloned.1.call-done = bf16[8192,64]{0,1:T(8,128)(2,1)} async-done(((bf16[1024,64]{0,1:T(8,128)(2,1)}), bf16[8192,64]{0,1:T(8,128)(2,1)}) %all-gather.5.cloned.1.call-update) | async-done | bytes 1048592 | tf_op jit(solution)/shard_map/all_gather | solution.py:61
  714.4 1.6 fusion.9
  716.0 1.2 convolution_multiply_fusion
  717.2 0.0 all-reduce.6.cloned.1.call-update
  717.3 0.0 reduce-scatter.2.cloned.1.call-start
  717.3 16.4 %convolution_bitcast_fusion.1 = f32[48,2048]{1,0:T(8,128)S(1)} fusion(bf16[8192,2048]{0,1:T(8,128)(2,1)} %all-gather.3.cloned.1.call-done, bf16[48,8192]{1,0:T(8,128)(2,1)S(1)} %copy-done), kind=kOutput, calls=%fused_computation.11 | convolution fusion | flops 1610612736 | bytes 34734080 | tf_op jit(solution)/shard_map/dot_general | solution.py:64
  733.8 0.4 multiply_reduce_fusion
  734.2 10.8 %all-reduce = (bf16[48,64]{1,0:T(8,128)(2,1)S(1)}, f32[48]{0:T(128)}) all-reduce(f32[48,64]{1,0:T(8,128)S(1)} %convolution_multiply_fusion.2, f32[48]{0:T(128)S(1)} %get-tuple-element.9), channel_id=1, replica_groups=mesh['seq'=8,'tp'=4] {'tp'}, use_global_device_ids=true, to_apply=%region_2.3 | all-reduce | flops 3120 | bytes 18816 | tf_op jit(solution)/shard_map/psum | solution.py:77
  745.0 1.8 convolution_bitcast_fusion
  746.8 11.5 %all-reduce.4.cloned.1.call-done = f32[48,8192]{1,0:T(8,128)} async-done(((f32[48,8192]{1,0:T(8,128)}), f32[48,8192]{1,0:T(8,128)}) %all-reduce.4.cloned.1.call-update) | async-done | bytes 1572880 | tf_op jit(solution)/shard_map/psum | solution.py:77
  758.4 1.8 fusion
  760.1 0.9 copy.51
  761.1 5.5 all-to-all-start
  766.6 2.0 scatter_custom_fusion
  768.7 23.7 %all-to-all-done = bf16[48,8,1024]{2,0,1:T(8,128)(2,1)S(1)} async-done(((bf16[48,8,1024]{2,0,1:T(8,128)(2,1)}), bf16[48,8,1024]{2,0,1:T(8,128)(2,1)S(1)}, u32[]{:S(2)}, u32[]{:S(2)}) %all-to-all-start) | async-done | bytes 786464 | tf_op jit(solution)/shard_map/all_to_all | solution.py:84
  792.4 49.4 %all-reduce.6.cloned.1.call-done = f32[64,2048]{1,0:T(8,128)} async-done(((f32[64,2048]{1,0:T(8,128)}), f32[64,2048]{1,0:T(8,128)}) %all-reduce.6.cloned.1.call-update) | async-done | bytes 524304 | tf_op jit(solution)/shard_map/psum | solution.py:96
  841.7 71.6 %reduce-scatter.2.cloned.1.call-done = f32[1024,64]{0,1:T(8,128)} async-done(((f32[8192,64]{0,1:T(8,128)}), f32[1024,64]{0,1:T(8,128)}) %reduce-scatter.2.cloned.1.call-update) | async-done | bytes 262160 | tf_op jit(solution)/shard_map/reduce_scatter | solution.py:87
  913.3 0.9 copy.59
  914.2 1.9 copy.60
  (22 shorter events, 0.1 us)
Async XLA Ops:
  7.2 707.2 %copy-start = (bf16[48,8192]{1,0:T(8,128)(2,1)S(1)}, bf16[48,8192]{1,0:T(8,128)(2,1)}, u32[]{:S(2)}) copy-start(bf16[48,8192]{1,0:T(8,128)(2,1)} %param.11) | copy-start | bytes 2359300
  7.2 664.8 %all-gather.3.cloned.1.call-start = ((), (), s32[]{:S(2)}) async-start(), calls=%async_computation.2 | async-start | bytes 37748736 | tf_op jit(solution)/shard_map/all_gather | solution.py:60
  7.2 9.4 %copy-start.6 = (f32[1024,32]{0,1:T(8,128)S(1)}, f32[1024,32]{0,1:T(8,128)}, u32[]{:S(2)}) copy-start(f32[1024,32]{0,1:T(8,128)} %param.13) | copy-start | bytes 393220
  16.6 16.2 %copy-start.8 = (s32[48]{0:T(128)S(1)}, s32[48]{0:T(128)}, u32[]{:S(2)}) copy-start(s32[48]{0:T(128)} %param.17) | copy-start | bytes 580
  16.6 16.3 %copy-start.4 = (bf16[192,2048]{1,0:T(8,128)(2,1)S(1)}, bf16[192,2048]{1,0:T(8,128)(2,1)}, u32[]{:S(2)}) copy-start(bf16[192,2048]{1,0:T(8,128)(2,1)} %param.19) | copy-start | bytes 2359300
  16.6 655.4 %copy-start.7 = (f32[48]{0:T(128)S(1)}, f32[48]{0:T(128)}, u32[]{:S(2)}) copy-start(f32[48]{0:T(128)} %param.16) | copy-start | bytes 580
  31.4 683.0 %all-gather.5.cloned.1.call-start = ((), (), s32[]{:S(2)}) async-start(), calls=%async_computation.3 | async-start | bytes 1179648 | tf_op jit(solution)/shard_map/all_gather | solution.py:61
  32.1 726.2 %all-reduce.4.cloned.1.call-start = ((), (), s32[]{:S(2)}) async-start(), calls=%async_computation.4 | async-start | bytes 3145728 | tf_op jit(solution)/shard_map/psum | solution.py:77
  33.6 653.3 %copy-start.5 = (bf16[64,2048]{1,0:T(8,128)(2,1)S(1)}, bf16[64,2048]{1,0:T(8,128)(2,1)}, u32[]{:S(2)}) copy-start(bf16[64,2048]{1,0:T(8,128)(2,1)} %param.15) | copy-start | bytes 786436
  686.9 154.9 %all-reduce.6.cloned.1.call-start = ((), (), s32[]{:S(2)}) async-start(), calls=%async_computation.6 | async-start | bytes 1048576 | tf_op jit(solution)/shard_map/psum | solution.py:96
  717.3 41.1 %copy-start.1 = (bf16[8192,64]{0,1:T(8,128)(2,1)S(1)}, bf16[8192,64]{0,1:T(8,128)(2,1)}, u32[]{:S(2)}) copy-start(bf16[8192,64]{0,1:T(8,128)(2,1)} %all-gather.5.cloned.1.call-done) | copy-start | bytes 3145732
  717.3 196.1 %reduce-scatter.2.cloned.1.call-start = ((), (), s32[]{:S(2)}) async-start(), calls=%async_computation.5 | async-start | bytes 2359296 | tf_op jit(solution)/shard_map/reduce_scatter | solution.py:87
  733.8 32.8 %copy-start.3 = (bf16[192,2048]{1,0:T(8,128)(2,1)S(1)}, bf16[192,2048]{1,0:T(8,128)(2,1)}, u32[]{:S(2)}) copy-start(bf16[192,2048]{1,0:T(8,128)(2,1)} %param.10) | copy-start | bytes 2359300
  761.1 31.3 %all-to-all-start = ((bf16[48,8,1024]{2,0,1:T(8,128)(2,1)}), bf16[48,8,1024]{2,0,1:T(8,128)(2,1)S(1)}, u32[]{:S(2)}, u32[]{:S(2)}) async-start(bf16[48,8,1024]{2,0,1:T(8,128)(2,1)} %bitcast.32), calls=%async_computation | async-start | bytes 1572864 | tf_op jit(solution)/shard_map/all_to_all | solution.py:84
  768.6 147.4 %copy-start.2 = (bf16[192,2048]{1,0:T(8,128)(2,1)}, bf16[192,2048]{1,0:T(8,128)(2,1)S(1)}, u32[]{:S(2)}) copy-start(bf16[192,2048]{1,0:T(8,128)(2,1)S(1)} %scatter_custom_fusion) | copy-start | bytes 2359300
Sparse Core Ops, SparseCore 0:
  31.5 640.4 all-gather.2
  674.1 40.1 all-gather.4
  716.7 41.5 all-reduce.3
  762.2 79.4 all-reduce.5
  846.1 67.1 reduce-scatter.1
where the time goes:
time: 923 us
  waiting for transfers between devices  822 us (89%)
  matrix products  38.5 us (4%)
  other arithmetic  16.8 us (2%)
  between operations  14.6 us (2%)
  local copies, waits for them, and re-layouts  13.8 us (1%)
  blocking collectives  10.8 us (1%)
    all_gather x1, waiting for transfers between devices, body(): lax.all_gather(projection_weight, 'seq', axis=0, tiled=True)  638 us
    reduce_scatter x1, waiting for transfers between devices, body(): lax.psum_scatter(jnp.dot(attention.T, adapter_rank_gradient, preferred_el...  71.6 us
    psum x1, waiting for transfers between devices, body(): adapter_up_gradient = lax.psum(up_factor_piece, 'seq')  49.4 us
    all_gather x1, waiting for transfers between devices, body(): lax.all_gather(adapter_down, 'seq', axis=0, tiled=True)  27.1 us
    all_to_all x1, waiting for transfers between devices, body(): lax.all_to_all(home_grad, 'seq', split_axis=1, concat_axis=0, tiled=True)  23.7 us
  transfers between devices with their start and end apart: 6, of which 6 were waited for; matrix products, arithmetic and copies ran while one was open for 5% of the time, Pallas kernels for 0%

commit v1 on v0

v1 whole, which is shorter than its diff:
```python
import jax
import jax.numpy as jnp
from jax import lax
from jax.experimental import pallas as pl
from jax.experimental.pallas import tpu as pltpu
from jax.sharding import PartitionSpec as P

LEVELS = (
    -1.0,
    -0.6961928009986877,
    -0.5250730514526367,
    -0.39491748809814453,
    -0.28444138169288635,
    -0.18477343022823334,
    -0.09105003625154495,
    0.0,
    0.07958029955625534,
    0.16093020141124725,
    0.24611230194568634,
    0.33791524171829224,
    0.44070982933044434,
    0.5626170039176941,
    0.7229568362236023,
    1.0,
)
adapter_scale = 0.25
BF, F32, I32 = jnp.bfloat16, jnp.float32, jnp.int32
VMEM_LIMIT = 48 * 2**20


def dot(a, b, ca=1, cb=0):
    return lax.dot_general(a, b, (((ca,), (cb,)), ((), ())), preferred_element_type=F32)


def split2(x):
    hi = x.astype(BF)
    return hi, (x - hi.astype(F32)).astype(BF)


def split3(x):
    hi = x.astype(BF)
    rest = x - hi.astype(F32)
    mid = rest.astype(BF)
    return hi, mid, (rest - mid.astype(F32)).astype(BF)


def call(kernel, outs, *args, flops=0, scratch=(), in_specs=None, name=None):
    nbytes = sum(a.size * a.dtype.itemsize for a in args) + sum(
        o.size * o.dtype.itemsize for o in outs
    )
    whole = pl.BlockSpec(memory_space=pltpu.VMEM)
    return pl.pallas_call(
        kernel,
        out_shape=tuple(outs),
        in_specs=in_specs or [whole] * len(args),
        out_specs=tuple([whole] * len(outs)),
        scratch_shapes=list(scratch),
        compiler_params=pltpu.CompilerParams(vmem_limit_bytes=VMEM_LIMIT),
        cost_estimate=pl.CostEstimate(flops=flops, bytes_accessed=nbytes, transcendentals=0),
        name=name,
    )(*args)


def shape(dims, dtype):
    return jax.ShapeDtypeStruct(tuple(dims), dtype)


def column(row):
    k = row.shape[1]
    eye = lax.broadcasted_iota(I32, (k, k), 0) == lax.broadcasted_iota(I32, (k, k), 1)
    return jnp.sum(jnp.where(eye, row, jnp.zeros_like(row)), axis=1, keepdims=True)


def row_of(col):
    k = col.shape[0]
    eye = lax.broadcasted_iota(I32, (k, k), 0) == lax.broadcasted_iota(I32, (k, k), 1)
    return jnp.sum(jnp.where(eye, col, jnp.zeros_like(col)), axis=0, keepdims=True)


def tree_levels(codes):
    values = list(LEVELS)
    for bit in range(4):
        odd = (codes & (1 << bit)) != 0
        values = [jnp.where(odd, values[2 * i + 1], values[2 * i]) for i in range(len(values) // 2)]
    return values[0]


def dequant_kernel(codes_ref, absmax_ref, table_ref, weight_ref):
    rows, cols = codes_ref.shape
    blocks = absmax_ref.shape[1]
    parts = jnp.concatenate(split3(absmax_ref[...]), axis=1)
    spread = lax.broadcasted_iota(I32, (3 * blocks, cols), 0) % blocks == lax.broadcasted_iota(
        I32, (3 * blocks, cols), 1
    ) // (cols // blocks)
    scales = dot(parts, jnp.where(spread, 1.0, 0.0).astype(BF))
    table = jnp.broadcast_to(table_ref[0:1, :], (rows, 128))
    for c in range(cols // 128):
        part = slice(c * 128, c * 128 + 128)
        codes = codes_ref[:, part]
        if c % 3:
            level = jnp.take_along_axis(table, codes, axis=1, mode="promise_in_bounds")
        else:
            level = tree_levels(codes)
        weight_ref[:, part] = (level * scales[:, part]).astype(BF)


def dequantize(codes, absmax, table, part, parts):
    rows, cols = codes.shape
    own = rows // parts
    block = min(128, own)
    steps = own // block
    return pl.pallas_call(
        dequant_kernel,
        grid=(steps,),
        out_shape=shape((own, cols), BF),
        in_specs=[
            pl.BlockSpec((block, cols), lambda i: (part * steps + i, 0)),
            pl.BlockSpec((block, absmax.shape[1]), lambda i: (part * steps + i, 0)),
            pl.BlockSpec((8, 128), lambda i: (0, 0)),
        ],
        out_specs=pl.BlockSpec((block, cols), lambda i: (i, 0)),
        compiler_params=pltpu.CompilerParams(vmem_limit_bytes=VMEM_LIMIT),
        cost_estimate=pl.CostEstimate(
            flops=own * cols * 100, bytes_accessed=own * cols * 6, transcendentals=0
        ),
        name="dequantize",
    )(codes, absmax, table)


def solution(mesh):
    n, tp = mesh.shape["seq"], mesh.shape["tp"]
    half = n // 2
    order = list(range(0, n, 2)) + list(range(n - 1, 0, -2))

    def ring(step):
        return [(order[i], order[(i + step) % n]) for i in range(n)]

    def flip(size, bit):
        return [(i, i ^ bit) for i in range(size)]

    def place(shard):
        return jnp.where(shard % 2 == 0, shard // 2, n - 1 - shard // 2)

    def shard_at(position):
        position = lax.rem(position + 2 * n, n)
        return jnp.where(position < half, 2 * position, 2 * (n - 1 - position) + 1)

    def body(
        residual,
        attention,
        quantized_codes,
        absmax,
        adapter_down,
        adapter_up,
        routed_slot_gate,
        selected,
        counts,
        cotangent,
    ):
        cap, all_heads = attention.shape
        tokens, cols = residual.shape
        heads = all_heads // n
        rank = adapter_up.shape[0]
        sub = heads // 2
        slots = n * cap
        side = 2 * rank
        gate_row = routed_slot_gate.reshape(1, cap)
        selected_row = selected.reshape(1, cap)
        table = jnp.asarray([list(LEVELS) * 8] * 8, F32)
        smem = pl.BlockSpec(memory_space=pltpu.SMEM)
        vmem = pl.BlockSpec(memory_space=pltpu.VMEM)

        def me():
            return lax.axis_index("seq"), lax.axis_index("tp") % 2

        def live_row(counts_ref):
            return lax.broadcasted_iota(I32, (1, cap), 1) < counts_ref[0]

        def pick(counts_ref, selected_ref):
            at = lax.broadcasted_iota(I32, (tokens, cap), 0) == selected_ref[...]
            return jnp.where(at & live_row(counts_ref), 1.0, 0.0).astype(BF)

        def prepare(counts_ref, selected_ref, gate_ref, attention_ref, cot_ref, send_ref, own_ref, grad_ref, up_ref):
            seq, core = me()
            for k in range(half):
                for ref, flipped in ((send_ref, 1), (own_ref, 0)):
                    at = (seq ^ (2 * k + flipped)) * heads + core * sub
                    ref[k] = attention_ref[:, pl.ds(pl.multiple_of(at, 128), sub)]
            upstream = dot(pick(counts_ref, selected_ref), cot_ref[...], 0, 0)
            up_ref[...] = upstream.astype(BF)
            grad_ref[...] = (column(gate_ref[...]) * upstream).astype(BF)

        send, own, grad, upstream = call(
            prepare,
            [shape((half, cap, sub), BF)] * 2 + [shape((cap, cols), BF)] * 2,
            counts, selected_row, gate_row, attention, cotangent,
            in_specs=[smem] + [vmem] * 4, name="prepare",
        )

        across = lax.ppermute(send, "seq", flip(n, 1))
        pairs = jnp.stack([own, across], axis=1)
        fetched = [pairs[0]] + [lax.ppermute(pairs[k], "seq", flip(n, 2 * k)) for k in range(1, half)]
        slots_own = jnp.concatenate(fetched).reshape(slots, sub)
        slots_other = lax.ppermute(slots_own, "tp", flip(tp, 1))

        gathered = {0: (grad,)}
        going, coming = grad, grad
        for step in range(1, half):
            going, coming = lax.ppermute(going, "seq", ring(1)), lax.ppermute(coming, "seq", ring(-1))
            gathered[n - step], gathered[step] = (going,), (coming,)
        mid = cap // 2
        gathered[half] = (
            lax.ppermute(going[:mid], "seq", ring(1)),
            lax.ppermute(coming[mid:], "seq", ring(-1)),
        )

        parts = 4
        weight = [dequantize(quantized_codes, absmax, table, i, parts) for i in range(parts)]
        per = heads // parts

        def forward(own_ref, other_ref, down_ref, up_ref, *refs):
            w_refs, (out_ref, low_ref) = refs[:parts], refs[parts:]
            seq, core = me()
            a, b = own_ref[...], other_ref[...]
            att = jnp.concatenate([jnp.where(core == 0, a, b), jnp.where(core == 0, b, a)], axis=1)
            low = dot(att, down_ref[...])
            thrice = jnp.concatenate(split3(adapter_scale * low), axis=1)
            low_pad = jnp.concatenate([low, jnp.zeros_like(low)], axis=1)
            for j in range(n):
                low_ref[seq ^ j] = low_pad[j * cap : (j + 1) * cap]
            spots = [lax.rem(place(seq ^ j) - place(seq) + n, n) for j in range(n)]
            tile = min(512, cols)
            for c in range(cols // tile):
                part = slice(c * tile, (c + 1) * tile)
                ups = up_ref[:, part]
                acc = dot(thrice, jnp.concatenate([ups] * 3, axis=0))
                for i in range(parts):
                    acc += dot(att[:, i * per : (i + 1) * per], w_refs[i][:, part])
                acc = acc.astype(BF)
                for j in range(n):
                    out_ref[spots[j], :, part] = acc[j * cap : (j + 1) * cap]

        partial, low = call(
            forward,
            [shape((n, cap, cols), BF), shape((n, cap, 2 * rank), F32)],
            slots_own, slots_other, adapter_down, adapter_up, *weight,
            flops=2 * slots * heads * cols, name="forward",
        )

        bit = 1
        while bit < n:
            low = low + lax.ppermute(low, "seq", flip(n, bit))
            bit *= 2

        def plus(a, b):
            return (a.astype(F32) + b.astype(F32)).astype(BF)

        going = lax.ppermute(partial[half, :mid], "seq", ring(1))
        coming = lax.ppermute(partial[half, mid:], "seq", ring(-1))
        for step in range(half - 1, 0, -1):
            here, there = partial[step], partial[n - step]
            if step == half - 1:
                here = jnp.concatenate([plus(here[:mid], going), here[mid:]])
                there = jnp.concatenate([there[:mid], plus(there[mid:], coming)])
            else:
                here, there = plus(here, going), plus(there, coming)
            going = lax.ppermute(here, "seq", ring(1))
            coming = lax.ppermute(there, "seq", ring(-1))

        def home(counts_ref, selected_ref, gate_ref, res_ref, own_ref, going_ref, coming_ref, up_ref, out_ref, gate_out_ref):
            chosen = pick(counts_ref, selected_ref)
            block = own_ref[...].astype(F32) + going_ref[...].astype(F32) + coming_ref[...].astype(F32)
            gate_out_ref[...] = row_of(jnp.sum(up_ref[...].astype(F32) * block, axis=1, keepdims=True))
            res = res_ref[...]
            picked = dot(chosen, res, 0, 0)
            updated = (picked + column(gate_ref[...]) * block).astype(BF)
            hit = jnp.sum(chosen.astype(F32), axis=1, keepdims=True) > 0
            out_ref[...] = jnp.where(hit, dot(chosen, updated), res.astype(F32)).astype(BF)

        outgoing_residual, gate_part = call(
            home,
            [shape((tokens, cols), BF), shape((1, cap), F32)],
            counts, selected_row, gate_row, residual, partial[0], going, coming, upstream,
            in_specs=[smem] + [vmem] * 7, name="home",
        )
        bit = 1
        while bit < tp:
            gate_part = gate_part + lax.ppermute(gate_part, "tp", flip(tp, bit))
            bit *= 2

        spots = [r for r in range(n) if r != half]
        some = slots // 2

        def backward(up_ref, *refs):
            w_refs, refs = refs[:parts], refs[parts:]
            first_ref, second_ref, refs = refs[0], refs[1], refs[2:]
            g_refs, (keep_ref, send_ref, all_ref, sums) = refs[: n - 1], refs[n - 1 :]
            seq, core = me()
            for r, ref in zip(spots, g_refs):
                all_ref[shard_at(place(seq) + r)] = ref[...]
            all_ref[shard_at(place(seq) + half)] = jnp.concatenate([first_ref[...], second_ref[...]])
            g = all_ref[...].reshape(slots, cols)
            for i in range(parts):
                sums[:, i * per : (i + 1) * per] = dot(g, w_refs[i][...], 1, 1)
            hi, lo = split2(adapter_scale * dot(g, up_ref[...], 1, 1))
            sums[:, heads:] = jnp.concatenate([hi, lo], axis=1).astype(F32)
            keep_ref[...] = sums[pl.ds(pl.multiple_of(core * some, 8), some), :]
            send_ref[...] = sums[pl.ds(pl.multiple_of((1 - core) * some, 8), some), :].astype(BF)

        wide = heads + side
        keep, send, grad_all = call(
            backward,
            [shape((some, wide), F32), shape((some, wide), BF), shape((n, cap, cols), BF)],
            adapter_up, *weight, *gathered[half], *[gathered[r][0] for r in spots],
            flops=2 * slots * heads * cols, scratch=[pltpu.VMEM((slots, wide), F32)], name="backward",
        )

        def ranks(a, b):
            return (a[:, heads : heads + rank].astype(F32) + b[:, heads : heads + rank].astype(F32)) + (
                a[:, heads + rank :].astype(F32) + b[:, heads + rank :].astype(F32)
            )

        def add(a_ref, b_ref, out_ref):
            a, b = a_ref[...], b_ref[...]
            out_ref[:, :heads] = (a[:, :heads].astype(F32) + b[:, :heads].astype(F32)).astype(BF)
            out_ref[:, heads:] = jnp.concatenate(split2(ranks(a, b)), axis=1)

        mine = call(add, [shape((some, wide), BF)], keep, lax.ppermute(send, "tp", flip(tp, 1)), name="add")[0]
        bit = 2
        while 2 * bit < tp:
            mine = call(add, [shape((some, wide), BF)], mine, lax.ppermute(mine, "tp", flip(tp, bit)), name="add")[0]
            bit *= 2

        def finish(a_ref, b_ref, down_ref, out_ref):
            a, b = a_ref[...], b_ref[...]
            rank_grad = ranks(a, b).astype(BF)
            tail = dot(rank_grad, down_ref[...], 1, 1)
            out_ref[:, :heads] = (a[:, :heads].astype(F32) + b[:, :heads].astype(F32) + tail).astype(BF)
            out_ref[:, heads:] = jnp.concatenate([rank_grad, jnp.zeros_like(rank_grad)], axis=1)

        done = call(
            finish, [shape((some, wide), BF)], mine, lax.ppermute(mine, "tp", flip(tp, bit)), adapter_down, name="finish"
        )[0]
        other_done = lax.ppermute(done, "tp", flip(tp, 1))

        def last(a_ref, b_ref, own_ref, other_ref, grad_ref, down_grad_ref, rank_ref):
            seq, core = me()
            for ref, at in ((a_ref, core), (b_ref, 1 - core)):
                grad_ref[pl.ds(pl.multiple_of(at * some, 16), some), :] = ref[:, :heads]
                for i in range(half):
                    rank_ref[at * half + i] = ref[i * cap : (i + 1) * cap, heads : heads + rank]
            rank_grad = jnp.concatenate([rank_ref[seq ^ j] for j in range(n)], axis=0)
            for ref, at in ((own_ref, core), (other_ref, 1 - core)):
                down_grad_ref[pl.ds(pl.multiple_of(at * sub, 8), sub), :] = dot(ref[...], rank_grad, 0, 0)

        attention_output_grad, adapter_down_gradient = call(
            last,
            [shape((slots, heads), BF), shape((heads, rank), F32)],
            done, other_done, slots_own, slots_other,
            scratch=[pltpu.VMEM((n, cap, rank), BF)], name="last",
        )

        def up_gradient(low_ref, g_ref, out_ref):
            low = low_ref[...].reshape(slots, 2 * rank)[:, :rank]
            thrice = dot(jnp.concatenate(split3(low), axis=1), g_ref[...].reshape(slots, cols), 0, 0)
            out_ref[...] = adapter_scale * (
                thrice[:rank] + thrice[rank : 2 * rank] + thrice[2 * rank :]
            )

        adapter_up_gradient = call(
            up_gradient, [shape((rank, cols), F32)], low, grad_all, flops=6 * slots * rank * cols, name="up_gradient"
        )[0]
        return (
            outgoing_residual,
            attention_output_grad,
            adapter_down_gradient,
            adapter_up_gradient,
            gate_part.reshape(cap),
        )

    return jax.shard_map(
        body,
        mesh=mesh,
        in_specs=(
            P("seq", "tp"),
            P("seq", None),
            P("seq", "tp"),
            P("seq", "tp"),
            P("seq", None),
            P(None, "tp"),
            P("seq"),
            P("seq"),
            P("seq"),
            P("seq", "tp"),
        ),
        out_specs=(P("seq", "tp"), P(None, "seq"), P("seq", None), P(None, "tp"), P("seq")),
        check_vma=False,
    )
```

time: 923 us -> 100 us (0.11)
  waiting for transfers between devices: 822 us -> 31.3 us
  matrix products: 38.5 us -> 0 us
  starting transfers between devices: 5.72 us -> 33.7 us
  Pallas kernels: 0 us -> 25.4 us
  other arithmetic: 16.8 us -> 1.88 us
  between operations: 14.6 us -> 1.61 us
  blocking collectives: 10.8 us -> 0 us
    all_gather x2 -> x0, waiting for transfers between devices: 666 us -> none  [the longest x1 638 us: body(): lax.all_gather(projection_weight, 'seq', axis=0, tiled=True)]
    reduce_scatter x1 -> x0, waiting for transfers between devices: 71.6 us -> none  [body(): lax.psum_scatter(jnp.dot(attention.T, adapter_rank_gradient, preferred_el...]
    psum x2 -> x0, waiting for transfers between devices: 60.9 us -> none  [the longest x1 49.4 us: body(): adapter_up_gradient = lax.psum(up_factor_piece, 'seq')]
    dot_general x8 -> x0, matrix products: 38.5 us -> none  [the longest x1 16.4 us: body(): jnp.dot(attention, full_w, preferred_element_type=jnp.float32)]
    ppermute x0 -> x29, starting transfers between devices: none -> 33.7 us  [the longest x3 4.48 us: body(): lax.ppermute(pairs[k], 'seq', flip(n, 2 * k))]
    ppermute x0 -> x29, waiting for transfers between devices: none -> 31.3 us  [the longest x1 7.86 us: body(): lax.ppermute(mine, 'tp', flip(tp, bit))]
    pallas_call x0 -> x12, Pallas kernels: none -> 25.4 us  [the longest x8 13.5 us: call(): pl.pallas_call(kernel, out_shape=tuple(outs), in_specs=in_specs or [whole...]
    all_to_all x1 -> x0, waiting for transfers between devices: 23.7 us -> none  [body(): lax.all_to_all(home_grad, 'seq', split_axis=1, concat_axis=0, tiled=True)]
  transfers between devices with their start and end apart: 6 -> 29, of which waited for: 6 -> 9; matrix products, arithmetic and copies ran while one was open for 5% -> 3% of each run, Pallas kernels for 0% -> 24%
where the time goes in v1:
time: 100 us
  starting transfers between devices  33.7 us (34%)
  waiting for transfers between devices  31.3 us (31%)
  Pallas kernels  25.4 us (25%)
  local copies, waits for them, and re-layouts  6.08 us (6%)
  other arithmetic  1.88 us (2%)
  between operations  1.61 us (2%)
    pallas_call x8, Pallas kernels, call(): pl.pallas_call(kernel, out_shape=tuple(outs), in_specs=in_specs or [whole...  13.5 us
    pallas_call x4, Pallas kernels, dequantize(): pl.pallas_call(dequant_kernel, grid=(steps,), out_shape=shape((own, cols)...  11.9 us
    ppermute x1, waiting for transfers between devices, body(): lax.ppermute(mine, 'tp', flip(tp, bit))  7.86 us
    ppermute x3, waiting for transfers between devices, body(): lax.ppermute(pairs[k], 'seq', flip(n, 2 * k))  6.84 us
    ppermute x3, waiting for transfers between devices, body(): low = low + lax.ppermute(low, 'seq', flip(n, bit))  5.13 us
    ppermute x1, waiting for transfers between devices, body(): across = lax.ppermute(send, 'seq', flip(n, 1))  4.9 us
    unnamed x33, local copies, waits for them, and re-layouts  4.87 us
    ppermute x3, starting transfers between devices, body(): lax.ppermute(pairs[k], 'seq', flip(n, 2 * k))  4.48 us
  transfers between devices with their start and end apart: 29, of which 9 were waited for; matrix products, arithmetic and copies ran while one was open for 3% of the time, Pallas kernels for 24%

profile of v1, /device:TPU:0, one launch (start us, length us, event | category | flops | bytes accessed | tf_op | source)
XLA Modules:
  0.0 100.0 jit_solution(9063133992658695435)
XLA Ops:
  5.2 3.0 %collective-permute-start = (bf16[4,48,512]{2,1,0:T(8,128)(2,1)S(1)}, bf16[4,48,512]{2,1,0:T(8,128)(2,1)S(1)}, u32[]{:S(2)}, u32[]{:S(2)}) collective-permute-start(bf16[4,48,512]{2,1,0:T(8,128)(2,1)S(1)} %get-tuple-element.19), channel_id=1, source_target_pairs={{0,4},{4,0},{8,12},{12,8},{16,20},{20,16},{24,28},{28,24},{1,5},{5... | collective-permute-start | bytes 589832 | tf_op jit(solution)/shard_map/ppermute | solution.py:200
  8.2 4.9 %collective-permute-done = bf16[4,48,512]{2,1,0:T(8,128)(2,1)S(1)} collective-permute-done((bf16[4,48,512]{2,1,0:T(8,128)(2,1)S(1)}, bf16[4,48,512]{2,1,0:T(8,128)(2,1)S(1)}, u32[]{:S(2)}, u32[]{:S(2)}) %collective-permute-start) | collective-permute-done | bytes 196640 | tf_op jit(solution)/shard_map/ppermute | solution.py:200
  13.1 1.9 %collective-permute-start.1 = (bf16[2,48,512]{2,1,0:T(8,128)(2,1)S(1)}, bf16[2,48,512]{2,1,0:T(8,128)(2,1)S(1)}, u32[]{:S(2)}, u32[]{:S(2)}) collective-permute-start(bf16[2,48,512]{2,1,0:T(8,128)(2,1)S(1)} %get-tuple-element.45), channel_id=1, source_target_pairs={{0,8},{4,12},{8,0},{12,4},{16,24},{20,28},{24,16},{28,20},{1,9},{5... | collective-permute-start | bytes 294920 | tf_op jit(solution)/shard_map/ppermute | solution.py:202
  15.0 2.5 %collective-permute-start.3 = (bf16[2,48,512]{2,1,0:T(8,128)(2,1)S(1)}, bf16[2,48,512]{2,1,0:T(8,128)(2,1)S(1)}, u32[]{:S(2)}, u32[]{:S(2)}) collective-permute-start(bf16[2,48,512]{2,1,0:T(8,128)(2,1)S(1)} %get-tuple-element.46), channel_id=1, source_target_pairs={{0,24},{4,28},{8,16},{12,20},{16,8},{20,12},{24,0},{28,4},{1,25},{... | collective-permute-start | bytes 294920 | tf_op jit(solution)/shard_map/ppermute | solution.py:202
  17.6 1.5 %collective-permute-start.17 = (bf16[48,2048]{1,0:T(8,128)(2,1)S(1)}, bf16[48,2048]{1,0:T(8,128)(2,1)S(1)}, u32[]{:S(2)}, u32[]{:S(2)}) collective-permute-start(bf16[48,2048]{1,0:T(8,128)(2,1)S(1)} %get-tuple-element.23.refs_6_), channel_id=1, source_target_pairs={{0,4},{8,0},{16,8},{24,16},{28,24},{20,28},{12,20},{4,12},{1,5},{9... | collective-permute-start | bytes 589832 | tf_op jit(solution)/shard_map/ppermute | solution.py:209
  19.6 3.4 %collective-permute-done.3 = bf16[2,48,512]{2,1,0:T(8,128)(2,1)S(1)} collective-permute-done((bf16[2,48,512]{2,1,0:T(8,128)(2,1)S(1)}, bf16[2,48,512]{2,1,0:T(8,128)(2,1)S(1)}, u32[]{:S(2)}, u32[]{:S(2)}) %collective-permute-start.3) | collective-permute-done | bytes 98336 | tf_op jit(solution)/shard_map/ppermute | solution.py:202
  23.1 3.4 %collective-permute-done.2 = bf16[2,48,512]{2,1,0:T(8,128)(2,1)S(1)} collective-permute-done((bf16[2,48,512]{2,1,0:T(8,128)(2,1)S(1)}, bf16[2,48,512]{2,1,0:T(8,128)(2,1)S(1)}, u32[]{:S(2)}, u32[]{:S(2)}) %collective-permute-start.2) | collective-permute-done | bytes 98336 | tf_op jit(solution)/shard_map/ppermute | solution.py:202
  26.6 1.5 %collective-permute-start.18 = (bf16[48,2048]{1,0:T(8,128)(2,1)S(1)}, bf16[48,2048]{1,0:T(8,128)(2,1)S(1)}, u32[]{:S(2)}, u32[]{:S(2)}) collective-permute-start(bf16[48,2048]{1,0:T(8,128)(2,1)S(1)} %collective-permute-done.17.refs_7_), channel_id=1, source_target_pairs={{0,4},{8,0},{16,8},{24,16},{28,24},{20,28},{12,20},{4,12},{1,5},{9... | collective-permute-start | bytes 589832 | tf_op jit(solution)/shard_map/ppermute | solution.py:209
  28.2 2.2 %collective-permute-start.14 = (bf16[48,2048]{1,0:T(8,128)(2,1)S(1)}, bf16[48,2048]{1,0:T(8,128)(2,1)S(1)}, u32[]{:S(2)}, u32[]{:S(2)}) collective-permute-start(bf16[48,2048]{1,0:T(8,128)(2,1)S(1)} %collective-permute-done.13.refs_12_), channel_id=1, source_target_pairs={{0,8},{8,16},{16,24},{24,28},{28,20},{20,12},{12,4},{4,0},{1,9},{9... | collective-permute-start | bytes 589832 | tf_op jit(solution)/shard_map/ppermute | solution.py:209
  30.7 2.8 %dequantize.7.refs_3_ = bf16[256,2048]{1,0:T(8,128)(2,1)S(1)} custom-call(s32[1024,2048]{1,0:T(8,128)} %codes_ref.7, f32[1024,32]{1,0:T(8,128)S(1)} %copy.19.absmax_ref, f32[8,128]{1,0:T(8,128)S(1)} %copy-done.7), custom_call_target="tpu_custom_call" | custom-call | flops 52428800 | bytes 3145728 | tf_op jit(solution)/shard_map/dequantize/pallas_call | solution.py:112
  33.5 3.1 %dequantize.6.refs_2_ = bf16[256,2048]{1,0:T(8,128)(2,1)S(1)} custom-call(s32[1024,2048]{1,0:T(8,128)} %codes_ref.7, f32[1024,32]{1,0:T(8,128)S(1)} %copy.19.absmax_ref, f32[8,128]{1,0:T(8,128)S(1)} %copy-done.7), custom_call_target="tpu_custom_call" | custom-call | flops 52428800 | bytes 3145728 | tf_op jit(solution)/shard_map/dequantize/pallas_call | solution.py:112
  36.7 3.1 %dequantize.5.refs_1_ = bf16[256,2048]{1,0:T(8,128)(2,1)S(1)} custom-call(s32[1024,2048]{1,0:T(8,128)} %codes_ref.7, f32[1024,32]{1,0:T(8,128)S(1)} %copy.19.absmax_ref, f32[8,128]{1,0:T(8,128)S(1)} %copy-done.7), custom_call_target="tpu_custom_call" | custom-call | flops 52428800 | bytes 3145728 | tf_op jit(solution)/shard_map/dequantize/pallas_call | solution.py:112
  39.9 2.8 %dequantize.4.refs_0_ = bf16[256,2048]{1,0:T(8,128)(2,1)S(1)} custom-call(s32[1024,2048]{1,0:T(8,128)} %codes_ref.7, f32[1024,32]{1,0:T(8,128)S(1)} %copy.19.absmax_ref, f32[8,128]{1,0:T(8,128)S(1)} %copy-done.7), custom_call_target="tpu_custom_call" | custom-call | flops 52428800 | bytes 3145728 | tf_op jit(solution)/shard_map/dequantize/pallas_call | solution.py:112
  43.5 1.3 %collective-permute-start.15 = (bf16[48,2048]{1,0:T(8,128)(2,1)S(1)}, bf16[48,2048]{1,0:T(8,128)(2,1)S(1)}, u32[]{:S(2)}, u32[]{:S(2)}) collective-permute-start(bf16[48,2048]{1,0:T(8,128)(2,1)S(1)} %collective-permute-done.14.refs_11_), channel_id=1, source_target_pairs={{0,8},{8,16},{16,24},{24,28},{28,20},{20,12},{12,4},{4,0},{1,9},{9... | collective-permute-start | bytes 589832 | tf_op jit(solution)/shard_map/ppermute | solution.py:209
  44.8 3.7 %forward.1 = (bf16[8,48,2048]{2,1,0:T(8,128)(2,1)}, f32[8,48,128]{2,1,0:T(8,128)S(1)}) custom-call(bf16[384,512]{1,0:T(8,128)(2,1)S(1)} %bitcast.50, bf16[384,512]{1,0:T(8,128)(2,1)S(1)} %collective-permute-done.4.other_ref, bf16[1024,64]{1,0:T(8,128)(2,1)S(1)} %copy.23.down_ref, bf16[64,2048]{1,0:T(8,128)(2,1)S(1)} %copy-done.6, ...), custom_call_target="tpu_custom_call" | custom-call | flops 1610612736 | bytes 7143424 | tf_op jit(solution)/shard_map/forward/pallas_call | solution.py:52
  49.7 1.3 %collective-permute-start.9 = (bf16[24,2048]{1,0:T(8,128)(2,1)S(1)}, bf16[24,2048]{1,0:T(8,128)(2,1)S(1)}, u32[]{:S(2)}, u32[]{:S(2)}) collective-permute-start(bf16[24,2048]{1,0:T(8,128)(2,1)S(1)} %get-tuple-element.39), channel_id=1, source_target_pairs={{0,4},{8,0},{16,8},{24,16},{28,24},{20,28},{12,20},{4,12},{1,5},{9... | collective-permute-start | bytes 294920 | tf_op jit(solution)/shard_map/ppermute | solution.py:259
  51.8 1.3 %collective-permute-start.20 = (bf16[24,2048]{1,0:T(8,128)(2,1)S(1)}, bf16[24,2048]{1,0:T(8,128)(2,1)S(1)}, u32[]{:S(2)}, u32[]{:S(2)}) collective-permute-start(bf16[24,2048]{1,0:T(8,128)(2,1)S(1)} %slice.91), channel_id=1, source_target_pairs={{0,4},{8,0},{16,8},{24,16},{28,24},{20,28},{12,20},{4,12},{1,5},{9... | collective-permute-start | bytes 294920 | tf_op jit(solution)/shard_map/ppermute | solution.py:214
  53.9 1.3 %collective-permute-start.24 = (f32[8,48,128]{2,1,0:T(8,128)S(1)}, f32[8,48,128]{2,1,0:T(8,128)S(1)}, u32[]{:S(2)}, u32[]{:S(2)}) collective-permute-start(f32[8,48,128]{2,1,0:T(8,128)S(1)} %get-tuple-element.28), channel_id=1, source_target_pairs={{0,4},{4,0},{8,12},{12,8},{16,20},{20,16},{24,28},{28,24},{1,5},{5... | collective-permute-start | bytes 589832 | tf_op jit(solution)/shard_map/ppermute | solution.py:252
  55.2 1.5 %collective-permute-done.5 = bf16[24,2048]{1,0:T(8,128)(2,1)S(1)} collective-permute-done((bf16[24,2048]{1,0:T(8,128)(2,1)S(1)}, bf16[24,2048]{1,0:T(8,128)(2,1)S(1)}, u32[]{:S(2)}, u32[]{:S(2)}) %collective-permute-start.5) | collective-permute-done | bytes 98336 | tf_op jit(solution)/shard_map/ppermute | solution.py:258
  59.8 3.7 %collective-permute-done.10 = bf16[48,2048]{1,0:T(8,128)(2,1)S(1)} collective-permute-done((bf16[48,2048]{1,0:T(8,128)(2,1)S(1)}, bf16[48,2048]{1,0:T(8,128)(2,1)S(1)}, u32[]{:S(2)}, u32[]{:S(2)}) %collective-permute-start.10) | collective-permute-done | bytes 196640 | tf_op jit(solution)/shard_map/ppermute | solution.py:268
  63.6 1.5 %collective-permute-start.11 = (bf16[48,2048]{1,0:T(8,128)(2,1)S(1)}, bf16[48,2048]{1,0:T(8,128)(2,1)S(1)}, u32[]{:S(2)}, u32[]{:S(2)}) collective-permute-start(bf16[48,2048]{1,0:T(8,128)(2,1)S(1)} %fusion), channel_id=1, source_target_pairs={{0,4},{8,0},{16,8},{24,16},{28,24},{20,28},{12,20},{4,12},{1,5},{9... | collective-permute-start | bytes 589832 | tf_op jit(solution)/shard_map/ppermute | solution.py:268
  65.2 4.8 %backward.1 = (f32[192,1152]{1,0:T(8,128)S(1)}, bf16[192,1152]{1,0:T(8,128)(2,1)S(1)}, bf16[8,48,2048]{2,1,0:T(8,128)(2,1)}) custom-call(bf16[64,2048]{1,0:T(8,128)(2,1)S(1)} %copy-done.6, bf16[256,2048]{1,0:T(8,128)(2,1)S(1)} %dequantize.4.refs_0_, bf16[256,2048]{1,0:T(8,128)(2,1)S(1)} %dequantize.5.refs_1_, bf16[256,2048]{1,0:T(8,128)(2,1)} %copy-done.1, ...), custom_call_target="tpu_custom_call" | custom-call | flops 1610612736 | bytes 8929280 | tf_op jit(solution)/shard_map/backward/pallas_call | solution.py:52
  70.7 1.5 %collective-permute-start.7 = (bf16[48,2048]{1,0:T(8,128)(2,1)S(1)}, bf16[48,2048]{1,0:T(8,128)(2,1)S(1)}, u32[]{:S(2)}, u32[]{:S(2)}) collective-permute-start(bf16[48,2048]{1,0:T(8,128)(2,1)S(1)} %get-tuple-element.37), channel_id=1, source_target_pairs={{0,8},{8,16},{16,24},{24,28},{28,20},{20,12},{12,4},{4,0},{1,9},{9... | collective-permute-start | bytes 589832 | tf_op jit(solution)/shard_map/ppermute | solution.py:267
  72.3 5.1 %collective-permute-done.25 = f32[8,48,128]{2,1,0:T(8,128)S(1)} collective-permute-done((f32[8,48,128]{2,1,0:T(8,128)S(1)}, f32[8,48,128]{2,1,0:T(8,128)S(1)}, u32[]{:S(2)}, u32[]{:S(2)}) %collective-permute-start.25) | collective-permute-done | bytes 196640 | tf_op jit(solution)/shard_map/ppermute | solution.py:252
  77.4 1.2 %collective-permute-start.26 = (f32[8,48,128]{2,1,0:T(8,128)S(1)}, f32[8,48,128]{2,1,0:T(8,128)S(1)}, u32[]{:S(2)}, u32[]{:S(2)}) collective-permute-start(f32[8,48,128]{2,1,0:T(8,128)S(1)} %add.41), channel_id=1, source_target_pairs={{0,16},{4,20},{8,24},{12,28},{16,0},{20,4},{24,8},{28,12},{1,17},{... | collective-permute-start | bytes 589832 | tf_op jit(solution)/shard_map/ppermute | solution.py:252
  78.9 1.6 %collective-permute-start.22 = (bf16[192,1152]{1,0:T(8,128)(2,1)S(1)}, bf16[192,1152]{1,0:T(8,128)(2,1)S(1)}, u32[]{:S(2)}, u32[]{:S(2)}) collective-permute-start(bf16[192,1152]{1,0:T(8,128)(2,1)S(1)} %add.64.a_ref), channel_id=1, source_target_pairs={{0,2},{1,3},{2,0},{3,1},{4,6},{5,7},{6,4},{7,5},{8,10},{9,11},{10,... | collective-permute-start | bytes 1327112 | tf_op jit(solution)/shard_map/ppermute | solution.py:342
  80.5 1.3 %collective-permute-start.12 = (bf16[48,2048]{1,0:T(8,128)(2,1)S(1)}, bf16[48,2048]{1,0:T(8,128)(2,1)S(1)}, u32[]{:S(2)}, u32[]{:S(2)}) collective-permute-start(bf16[48,2048]{1,0:T(8,128)(2,1)S(1)} %get-tuple-element.36), channel_id=1, source_target_pairs={{0,4},{8,0},{16,8},{24,16},{28,24},{20,28},{12,20},{4,12},{1,5},{9... | collective-permute-start | bytes 589832 | tf_op jit(solution)/shard_map/ppermute | solution.py:268
  82.7 7.9 %collective-permute-done.22.b_ref = bf16[192,1152]{1,0:T(8,128)(2,1)S(1)} collective-permute-done((bf16[192,1152]{1,0:T(8,128)(2,1)S(1)}, bf16[192,1152]{1,0:T(8,128)(2,1)S(1)}, u32[]{:S(2)}, u32[]{:S(2)}) %collective-permute-start.22) | collective-permute-done | bytes 442400 | tf_op jit(solution)/shard_map/ppermute | solution.py:342
  91.0 1.5 %home.1 = (bf16[192,2048]{1,0:T(8,128)(2,1)}, f32[1,48]{1,0:T(1,128)S(1)}) custom-call(s32[1]{0:T(128)S(6)} %copy.29.counts_ref, s32[1,48]{1,0:T(1,128)S(1)} %bitcast.54, f32[1,48]{1,0:T(1,128)S(1)} %bitcast.56, bf16[192,2048]{1,0:T(8,128)(2,1)S(1)} %copy-done.5, bf16[48,2048]{1,0:T(8,128)(2,1)S(1)} %slice_bitcast_fusion.own_ref, ...), custom_call_target="tpu_custom_call" | custom-call | bytes 2359876 | tf_op jit(solution)/shard_map/home/pallas_call | solution.py:52
  93.8 1.5 %collective-permute-start.28 = (f32[1,48]{1,0:T(1,128)S(1)}, f32[1,48]{1,0:T(1,128)S(1)}, u32[]{:S(2)}, u32[]{:S(2)}) collective-permute-start(f32[1,48]{1,0:T(1,128)S(1)} %add.43), channel_id=1, source_target_pairs={{0,2},{1,3},{2,0},{3,1},{4,6},{5,7},{6,4},{7,5},{8,10},{9,11},{10,... | collective-permute-start | bytes 584 | tf_op jit(solution)/shard_map/ppermute | solution.py:288
  95.3 1.5 %up_gradient.1 = f32[64,2048]{1,0:T(8,128)} custom-call(f32[8,48,128]{2,1,0:T(8,128)S(1)} %add.42.low_ref, bf16[8,48,2048]{2,1,0:T(8,128)(2,1)S(1)} %copy-done.2), custom_call_target="tpu_custom_call" | custom-call | flops 301989888 | bytes 2293760 | tf_op jit(solution)/shard_map/up_gradient/pallas_call | solution.py:52
  97.8 1.3 %last.1 = (bf16[384,1024]{1,0:T(8,128)(2,1)}, f32[1024,64]{1,0:T(8,128)S(1)}) custom-call(bf16[192,1152]{1,0:T(8,128)(2,1)S(1)} %finish.1.a_ref, bf16[192,1152]{1,0:T(8,128)(2,1)S(1)} %collective-permute-done.23.b_ref, bf16[384,512]{1,0:T(8,128)(2,1)S(1)} %bitcast.51, bf16[384,512]{1,0:T(8,128)(2,1)S(1)} %collective-permute-done.4.other_ref), custom_call_target="tpu_custom_call" | custom-call | bytes 2719744 | tf_op jit(solution)/shard_map/last/pallas_call | solution.py:52
  (88 shorter events, 17.5 us)
Async XLA Ops:
  4.9 25.5 %copy-start.13 = (bf16[1024,64]{0,1:T(8,128)(2,1)S(1)}, bf16[1024,64]{0,1:T(8,128)(2,1)}, u32[]{:S(2)}) copy-start(bf16[1024,64]{0,1:T(8,128)(2,1)} %param.15) | copy-start | bytes 393220
  4.9 25.7 %copy-start.14 = (f32[1024,32]{0,1:T(8,128)S(1)}, f32[1024,32]{0,1:T(8,128)}, u32[]{:S(2)}) copy-start(f32[1024,32]{0,1:T(8,128)} %param.14) | copy-start | bytes 393220
  5.2 25.6 %copy-start.7 = (f32[8,128]{1,0:T(8,128)S(1)}, f32[8,128]{1,0:T(8,128)}, u32[]{:S(2)}) copy-start(f32[8,128]{1,0:T(8,128)} %constant.2.clone.table_ref) | copy-start | bytes 12292
  5.2 7.9 %collective-permute-start = (bf16[4,48,512]{2,1,0:T(8,128)(2,1)S(1)}, bf16[4,48,512]{2,1,0:T(8,128)(2,1)S(1)}, u32[]{:S(2)}, u32[]{:S(2)}) collective-permute-start(bf16[4,48,512]{2,1,0:T(8,128)(2,1)S(1)} %get-tuple-element.19), channel_id=1, source_target_pairs={{0,4},{4,0},{8,12},{12,8},{16,20},{20,16},{24,28},{28,24},{1,5},{5... | collective-permute-start | bytes 589832 | tf_op jit(solution)/shard_map/ppermute | solution.py:200
  13.1 6.5 %collective-permute-start.1 = (bf16[2,48,512]{2,1,0:T(8,128)(2,1)S(1)}, bf16[2,48,512]{2,1,0:T(8,128)(2,1)S(1)}, u32[]{:S(2)}, u32[]{:S(2)}) collective-permute-start(bf16[2,48,512]{2,1,0:T(8,128)(2,1)S(1)} %get-tuple-element.45), channel_id=1, source_target_pairs={{0,8},{4,12},{8,0},{12,4},{16,24},{20,28},{24,16},{28,20},{1,9},{5... | collective-permute-start | bytes 294920 | tf_op jit(solution)/shard_map/ppermute | solution.py:202
  15.0 8.1 %collective-permute-start.3 = (bf16[2,48,512]{2,1,0:T(8,128)(2,1)S(1)}, bf16[2,48,512]{2,1,0:T(8,128)(2,1)S(1)}, u32[]{:S(2)}, u32[]{:S(2)}) collective-permute-start(bf16[2,48,512]{2,1,0:T(8,128)(2,1)S(1)} %get-tuple-element.46), channel_id=1, source_target_pairs={{0,24},{4,28},{8,16},{12,20},{16,8},{20,12},{24,0},{28,4},{1,25},{... | collective-permute-start | bytes 294920 | tf_op jit(solution)/shard_map/ppermute | solution.py:202
  17.5 9.0 %collective-permute-start.2 = (bf16[2,48,512]{2,1,0:T(8,128)(2,1)S(1)}, bf16[2,48,512]{2,1,0:T(8,128)(2,1)S(1)}, u32[]{:S(2)}, u32[]{:S(2)}) collective-permute-start(bf16[2,48,512]{2,1,0:T(8,128)(2,1)S(1)} %get-tuple-element.47), channel_id=1, source_target_pairs={{0,16},{4,20},{8,24},{12,28},{16,0},{20,4},{24,8},{28,12},{1,17},{... | collective-permute-start | bytes 294920 | tf_op jit(solution)/shard_map/ppermute | solution.py:202
  17.6 9.0 %collective-permute-start.17 = (bf16[48,2048]{1,0:T(8,128)(2,1)S(1)}, bf16[48,2048]{1,0:T(8,128)(2,1)S(1)}, u32[]{:S(2)}, u32[]{:S(2)}) collective-permute-start(bf16[48,2048]{1,0:T(8,128)(2,1)S(1)} %get-tuple-element.23.refs_6_), channel_id=1, source_target_pairs={{0,4},{8,0},{16,8},{24,16},{28,24},{20,28},{12,20},{4,12},{1,5},{9... | collective-permute-start | bytes 589832 | tf_op jit(solution)/shard_map/ppermute | solution.py:209
  19.1 9.1 %collective-permute-start.13 = (bf16[48,2048]{1,0:T(8,128)(2,1)S(1)}, bf16[48,2048]{1,0:T(8,128)(2,1)S(1)}, u32[]{:S(2)}, u32[]{:S(2)}) collective-permute-start(bf16[48,2048]{1,0:T(8,128)(2,1)S(1)} %get-tuple-element.23.refs_6_), channel_id=1, source_target_pairs={{0,8},{8,16},{16,24},{24,28},{28,20},{20,12},{12,4},{4,0},{1,9},{9... | collective-permute-start | bytes 589832 | tf_op jit(solution)/shard_map/ppermute | solution.py:209
  26.5 18.3 %collective-permute-start.4 = (bf16[384,512]{1,0:T(8,128)(2,1)S(1)}, bf16[384,512]{1,0:T(8,128)(2,1)S(1)}, u32[]{:S(2)}, u32[]{:S(2)}) collective-permute-start(bf16[384,512]{1,0:T(8,128)(2,1)S(1)} %bitcast.49), channel_id=1, source_target_pairs={{0,1},{1,0},{2,3},{3,2},{4,5},{5,4},{6,7},{7,6},{8,9},{9,8},{10,11... | collective-permute-start | bytes 1179656 | tf_op jit(solution)/shard_map/ppermute | solution.py:204
  26.6 16.0 %collective-permute-start.18 = (bf16[48,2048]{1,0:T(8,128)(2,1)S(1)}, bf16[48,2048]{1,0:T(8,128)(2,1)S(1)}, u32[]{:S(2)}, u32[]{:S(2)}) collective-permute-start(bf16[48,2048]{1,0:T(8,128)(2,1)S(1)} %collective-permute-done.17.refs_7_), channel_id=1, source_target_pairs={{0,4},{8,0},{16,8},{24,16},{28,24},{20,28},{12,20},{4,12},{1,5},{9... | collective-permute-start | bytes 589832 | tf_op jit(solution)/shard_map/ppermute | solution.py:209
  28.2 15.4 %collective-permute-start.14 = (bf16[48,2048]{1,0:T(8,128)(2,1)S(1)}, bf16[48,2048]{1,0:T(8,128)(2,1)S(1)}, u32[]{:S(2)}, u32[]{:S(2)}) collective-permute-start(bf16[48,2048]{1,0:T(8,128)(2,1)S(1)} %collective-permute-done.13.refs_12_), channel_id=1, source_target_pairs={{0,8},{8,16},{16,24},{24,28},{28,20},{20,12},{12,4},{4,0},{1,9},{9... | collective-permute-start | bytes 589832 | tf_op jit(solution)/shard_map/ppermute | solution.py:209
  42.7 9.1 %collective-permute-start.19 = (bf16[48,2048]{1,0:T(8,128)(2,1)S(1)}, bf16[48,2048]{1,0:T(8,128)(2,1)S(1)}, u32[]{:S(2)}, u32[]{:S(2)}) collective-permute-start(bf16[48,2048]{1,0:T(8,128)(2,1)S(1)} %collective-permute-done.18.refs_8_), channel_id=1, source_target_pairs={{0,4},{8,0},{16,8},{24,16},{28,24},{20,28},{12,20},{4,12},{1,5},{9... | collective-permute-start | bytes 589832 | tf_op jit(solution)/shard_map/ppermute | solution.py:209
  43.5 9.5 %collective-permute-start.15 = (bf16[48,2048]{1,0:T(8,128)(2,1)S(1)}, bf16[48,2048]{1,0:T(8,128)(2,1)S(1)}, u32[]{:S(2)}, u32[]{:S(2)}) collective-permute-start(bf16[48,2048]{1,0:T(8,128)(2,1)S(1)} %collective-permute-done.14.refs_11_), channel_id=1, source_target_pairs={{0,8},{8,16},{16,24},{24,28},{28,20},{20,12},{12,4},{4,0},{1,9},{9... | collective-permute-start | bytes 589832 | tf_op jit(solution)/shard_map/ppermute | solution.py:209
  49.7 5.5 %collective-permute-start.9 = (bf16[24,2048]{1,0:T(8,128)(2,1)S(1)}, bf16[24,2048]{1,0:T(8,128)(2,1)S(1)}, u32[]{:S(2)}, u32[]{:S(2)}) collective-permute-start(bf16[24,2048]{1,0:T(8,128)(2,1)S(1)} %get-tuple-element.39), channel_id=1, source_target_pairs={{0,4},{8,0},{16,8},{24,16},{28,24},{20,28},{12,20},{4,12},{1,5},{9... | collective-permute-start | bytes 294920 | tf_op jit(solution)/shard_map/ppermute | solution.py:259
  51.0 5.7 %collective-permute-start.5 = (bf16[24,2048]{1,0:T(8,128)(2,1)S(1)}, bf16[24,2048]{1,0:T(8,128)(2,1)S(1)}, u32[]{:S(2)}, u32[]{:S(2)}) collective-permute-start(bf16[24,2048]{1,0:T(8,128)(2,1)S(1)} %get-tuple-element.41), channel_id=1, source_target_pairs={{0,8},{8,16},{16,24},{24,28},{28,20},{20,12},{12,4},{4,0},{1,9},{9... | collective-permute-start | bytes 294920 | tf_op jit(solution)/shard_map/ppermute | solution.py:258
  51.8 13.4 %collective-permute-start.20 = (bf16[24,2048]{1,0:T(8,128)(2,1)S(1)}, bf16[24,2048]{1,0:T(8,128)(2,1)S(1)}, u32[]{:S(2)}, u32[]{:S(2)}) collective-permute-start(bf16[24,2048]{1,0:T(8,128)(2,1)S(1)} %slice.91), channel_id=1, source_target_pairs={{0,4},{8,0},{16,8},{24,16},{28,24},{20,28},{12,20},{4,12},{1,5},{9... | collective-permute-start | bytes 294920 | tf_op jit(solution)/shard_map/ppermute | solution.py:214
  53.1 12.1 %collective-permute-start.16 = (bf16[24,2048]{1,0:T(8,128)(2,1)S(1)}, bf16[24,2048]{1,0:T(8,128)(2,1)S(1)}, u32[]{:S(2)}, u32[]{:S(2)}) collective-permute-start(bf16[24,2048]{1,0:T(8,128)(2,1)S(1)} %slice.90), channel_id=1, source_target_pairs={{0,8},{8,16},{16,24},{24,28},{28,20},{20,12},{12,4},{4,0},{1,9},{9... | collective-permute-start | bytes 294920 | tf_op jit(solution)/shard_map/ppermute | solution.py:213
  53.9 16.1 %collective-permute-start.24 = (f32[8,48,128]{2,1,0:T(8,128)S(1)}, f32[8,48,128]{2,1,0:T(8,128)S(1)}, u32[]{:S(2)}, u32[]{:S(2)}) collective-permute-start(f32[8,48,128]{2,1,0:T(8,128)S(1)} %get-tuple-element.28), channel_id=1, source_target_pairs={{0,4},{4,0},{8,12},{12,8},{16,20},{20,16},{24,28},{28,24},{1,5},{5... | collective-permute-start | bytes 589832 | tf_op jit(solution)/shard_map/ppermute | solution.py:252
  57.7 5.9 %collective-permute-start.10 = (bf16[48,2048]{1,0:T(8,128)(2,1)S(1)}, bf16[48,2048]{1,0:T(8,128)(2,1)S(1)}, u32[]{:S(2)}, u32[]{:S(2)}) collective-permute-start(bf16[48,2048]{1,0:T(8,128)(2,1)S(1)} %pad_maximum_fusion.2), channel_id=1, source_target_pairs={{0,4},{8,0},{16,8},{24,16},{28,24},{20,28},{12,20},{4,12},{1,5},{9... | collective-permute-start | bytes 589832 | tf_op jit(solution)/shard_map/ppermute | solution.py:268
  58.7 12.0 %collective-permute-start.6 = (bf16[48,2048]{1,0:T(8,128)(2,1)S(1)}, bf16[48,2048]{1,0:T(8,128)(2,1)S(1)}, u32[]{:S(2)}, u32[]{:S(2)}) collective-permute-start(bf16[48,2048]{1,0:T(8,128)(2,1)S(1)} %pad_maximum_fusion.1), channel_id=1, source_target_pairs={{0,8},{8,16},{16,24},{24,28},{28,20},{20,12},{12,4},{4,0},{1,9},{9... | collective-permute-start | bytes 589832 | tf_op jit(solution)/shard_map/ppermute | solution.py:267
  63.6 7.0 %collective-permute-start.11 = (bf16[48,2048]{1,0:T(8,128)(2,1)S(1)}, bf16[48,2048]{1,0:T(8,128)(2,1)S(1)}, u32[]{:S(2)}, u32[]{:S(2)}) collective-permute-start(bf16[48,2048]{1,0:T(8,128)(2,1)S(1)} %fusion), channel_id=1, source_target_pairs={{0,4},{8,0},{16,8},{24,16},{28,24},{20,28},{12,20},{4,12},{1,5},{9... | collective-permute-start | bytes 589832 | tf_op jit(solution)/shard_map/ppermute | solution.py:268
  70.0 8.7 %collective-permute-start.21 = (bf16[192,1152]{1,0:T(8,128)(2,1)S(1)}, bf16[192,1152]{1,0:T(8,128)(2,1)S(1)}, u32[]{:S(2)}, u32[]{:S(2)}) collective-permute-start(bf16[192,1152]{1,0:T(8,128)(2,1)S(1)} %get-tuple-element.25), channel_id=1, source_target_pairs={{0,1},{1,0},{2,3},{3,2},{4,5},{5,4},{6,7},{7,6},{8,9},{9,8},{10,11... | collective-permute-start | bytes 1327112 | tf_op jit(solution)/shard_map/ppermute | solution.py:328
  70.0 7.4 %collective-permute-start.25 = (f32[8,48,128]{2,1,0:T(8,128)S(1)}, f32[8,48,128]{2,1,0:T(8,128)S(1)}, u32[]{:S(2)}, u32[]{:S(2)}) collective-permute-start(f32[8,48,128]{2,1,0:T(8,128)S(1)} %add.40), channel_id=1, source_target_pairs={{0,8},{4,12},{8,0},{12,4},{16,24},{20,28},{24,16},{28,20},{1,9},{5... | collective-permute-start | bytes 589832 | tf_op jit(solution)/shard_map/ppermute | solution.py:252
  70.7 11.0 %collective-permute-start.7 = (bf16[48,2048]{1,0:T(8,128)(2,1)S(1)}, bf16[48,2048]{1,0:T(8,128)(2,1)S(1)}, u32[]{:S(2)}, u32[]{:S(2)}) collective-permute-start(bf16[48,2048]{1,0:T(8,128)(2,1)S(1)} %get-tuple-element.37), channel_id=1, source_target_pairs={{0,8},{8,16},{16,24},{24,28},{28,20},{20,12},{12,4},{4,0},{1,9},{9... | collective-permute-start | bytes 589832 | tf_op jit(solution)/shard_map/ppermute | solution.py:267
  77.4 15.5 %collective-permute-start.26 = (f32[8,48,128]{2,1,0:T(8,128)S(1)}, f32[8,48,128]{2,1,0:T(8,128)S(1)}, u32[]{:S(2)}, u32[]{:S(2)}) collective-permute-start(f32[8,48,128]{2,1,0:T(8,128)S(1)} %add.41), channel_id=1, source_target_pairs={{0,16},{4,20},{8,24},{12,28},{16,0},{20,4},{24,8},{28,12},{1,17},{... | collective-permute-start | bytes 589832 | tf_op jit(solution)/shard_map/ppermute | solution.py:252
  78.9 11.6 %collective-permute-start.22 = (bf16[192,1152]{1,0:T(8,128)(2,1)S(1)}, bf16[192,1152]{1,0:T(8,128)(2,1)S(1)}, u32[]{:S(2)}, u32[]{:S(2)}) collective-permute-start(bf16[192,1152]{1,0:T(8,128)(2,1)S(1)} %add.64.a_ref), channel_id=1, source_target_pairs={{0,2},{1,3},{2,0},{3,1},{4,6},{5,7},{6,4},{7,5},{8,10},{9,11},{10,... | collective-permute-start | bytes 1327112 | tf_op jit(solution)/shard_map/ppermute | solution.py:342
  80.5 10.4 %collective-permute-start.12 = (bf16[48,2048]{1,0:T(8,128)(2,1)S(1)}, bf16[48,2048]{1,0:T(8,128)(2,1)S(1)}, u32[]{:S(2)}, u32[]{:S(2)}) collective-permute-start(bf16[48,2048]{1,0:T(8,128)(2,1)S(1)} %get-tuple-element.36), channel_id=1, source_target_pairs={{0,4},{8,0},{16,8},{24,16},{28,24},{20,28},{12,20},{4,12},{1,5},{9... | collective-permute-start | bytes 589832 | tf_op jit(solution)/shard_map/ppermute | solution.py:268
  81.8 9.1 %collective-permute-start.8 = (bf16[48,2048]{1,0:T(8,128)(2,1)S(1)}, bf16[48,2048]{1,0:T(8,128)(2,1)S(1)}, u32[]{:S(2)}, u32[]{:S(2)}) collective-permute-start(bf16[48,2048]{1,0:T(8,128)(2,1)S(1)} %fusion.3), channel_id=1, source_target_pairs={{0,8},{8,16},{16,24},{24,28},{28,20},{20,12},{12,4},{4,0},{1,9},{9... | collective-permute-start | bytes 589832 | tf_op jit(solution)/shard_map/ppermute | solution.py:267
  90.8 7.0 %collective-permute-start.23 = (bf16[192,1152]{1,0:T(8,128)(2,1)S(1)}, bf16[192,1152]{1,0:T(8,128)(2,1)S(1)}, u32[]{:S(2)}, u32[]{:S(2)}) collective-permute-start(bf16[192,1152]{1,0:T(8,128)(2,1)S(1)} %finish.1.a_ref), channel_id=1, source_target_pairs={{0,1},{1,0},{2,3},{3,2},{4,5},{5,4},{6,7},{7,6},{8,9},{9,8},{10,11... | collective-permute-start | bytes 1327112 | tf_op jit(solution)/shard_map/ppermute | solution.py:344
  92.5 1.3 %collective-permute-start.27 = (f32[1,48]{1,0:T(1,128)S(1)}, f32[1,48]{1,0:T(1,128)S(1)}, u32[]{:S(2)}, u32[]{:S(2)}) collective-permute-start(f32[1,48]{1,0:T(1,128)S(1)} %get-tuple-element.30), channel_id=1, source_target_pairs={{0,1},{1,0},{2,3},{3,2},{4,5},{5,4},{6,7},{7,6},{8,9},{9,8},{10,11... | collective-permute-start | bytes 584 | tf_op jit(solution)/shard_map/ppermute | solution.py:288
  93.8 3.5 %collective-permute-start.28 = (f32[1,48]{1,0:T(1,128)S(1)}, f32[1,48]{1,0:T(1,128)S(1)}, u32[]{:S(2)}, u32[]{:S(2)}) collective-permute-start(f32[1,48]{1,0:T(1,128)S(1)} %add.43), channel_id=1, source_target_pairs={{0,2},{1,3},{2,0},{3,1},{4,6},{5,7},{6,4},{7,5},{8,10},{9,11},{10,... | collective-permute-start | bytes 584 | tf_op jit(solution)/shard_map/ppermute | solution.py:288
  (12 other events, 83.8 us)

commit v2 on v1

v2 whole, which is shorter than its diff:
```python
import functools

import jax
import jax.numpy as jnp
from jax import lax
from jax.experimental import pallas as pl
from jax.experimental.pallas import tpu as pltpu
from jax.sharding import PartitionSpec as P

LEVELS = (
    -1.0,
    -0.6961928009986877,
    -0.5250730514526367,
    -0.39491748809814453,
    -0.28444138169288635,
    -0.18477343022823334,
    -0.09105003625154495,
    0.0,
    0.07958029955625534,
    0.16093020141124725,
    0.24611230194568634,
    0.33791524171829224,
    0.44070982933044434,
    0.5626170039176941,
    0.7229568362236023,
    1.0,
)
adapter_scale = 0.25
BF, F32, I32 = jnp.bfloat16, jnp.float32, jnp.int32
VMEM_LIMIT = 16 * 2**20
DEAD = 2.0


def dot(a, b, ca=1, cb=0):
    return lax.dot_general(a, b, (((ca,), (cb,)), ((), ())), preferred_element_type=F32)


def split2(x):
    hi = x.astype(BF)
    return hi, (x - hi.astype(F32)).astype(BF)


def split3(x):
    hi = x.astype(BF)
    rest = x - hi.astype(F32)
    mid = rest.astype(BF)
    return hi, mid, (rest - mid.astype(F32)).astype(BF)


def call(kernel, outs, *args, flops=0, scratch=(), in_specs=None, name=None):
    nbytes = sum(a.size * a.dtype.itemsize for a in args) + sum(
        o.size * o.dtype.itemsize for o in outs
    )
    whole = pl.BlockSpec(memory_space=pltpu.VMEM)
    return pl.pallas_call(
        kernel,
        out_shape=tuple(outs),
        in_specs=in_specs or [whole] * len(args),
        out_specs=tuple([whole] * len(outs)),
        scratch_shapes=list(scratch),
        compiler_params=pltpu.CompilerParams(vmem_limit_bytes=VMEM_LIMIT),
        cost_estimate=pl.CostEstimate(flops=flops, bytes_accessed=nbytes, transcendentals=0),
        name=name,
    )(*args)


def shape(dims, dtype):
    return jax.ShapeDtypeStruct(tuple(dims), dtype)


def column(row):
    k = row.shape[1]
    eye = lax.broadcasted_iota(I32, (k, k), 0) == lax.broadcasted_iota(I32, (k, k), 1)
    return jnp.sum(jnp.where(eye, row, jnp.zeros_like(row)), axis=1, keepdims=True)


def row_of(col):
    k = col.shape[0]
    eye = lax.broadcasted_iota(I32, (k, k), 0) == lax.broadcasted_iota(I32, (k, k), 1)
    return jnp.sum(jnp.where(eye, col, jnp.zeros_like(col)), axis=0, keepdims=True)


def tree_levels(codes):
    values = list(LEVELS)
    for bit in range(4):
        odd = (codes & (1 << bit)) != 0
        values = [jnp.where(odd, values[2 * i + 1], values[2 * i]) for i in range(len(values) // 2)]
    return values[0]


def dequant_kernel(first, codes_hbm, absmax_ref, weight_ref, token_ref, codes, sems):
    chunks, block, cols = codes.shape
    blocks = absmax_ref.shape[1]
    per = cols // blocks

    def copy(i):
        rows = pl.ds(first + i * block, block)
        return pltpu.make_async_copy(codes_hbm.at[rows], codes.at[i], sems.at[i])

    for i in range(chunks):
        copy(i).start()
    token_ref[...] = jnp.zeros_like(token_ref)
    column_block = lax.broadcasted_iota(I32, (block, 128), 1) // per

    @pl.loop(0, chunks)
    def _(i):
        rows = pl.ds(pl.multiple_of(i * block, block), block)
        absmax = absmax_ref[pl.ds(pl.multiple_of(first + i * block, block), block), :]
        absmax = jnp.concatenate([absmax] * (128 // blocks), axis=1)
        copy(i).wait()
        for c in range(cols // 128):
            part = slice(c * 128, c * 128 + 128)
            scale = jnp.take_along_axis(absmax, column_block + c * (128 // per), axis=1, mode="promise_in_bounds")
            weight_ref[rows, part] = (tree_levels(codes[i, :, part]) * scale).astype(BF)


def in_hbm(array):
    return pltpu.with_memory_space_constraint(array, pltpu.HBM)


def solution(mesh):
    n, tp = mesh.shape["seq"], mesh.shape["tp"]
    half = n // 2
    order = list(range(0, n, 2)) + list(range(n - 1, 0, -2))

    def ring(step):
        return [(order[i], order[(i + step) % n]) for i in range(n)]

    def flip(size, bit):
        return [(i, i ^ bit) for i in range(size)]

    def place(shard):
        return jnp.where(shard % 2 == 0, shard // 2, n - 1 - shard // 2)

    def shard_at(position):
        position = lax.rem(position + 2 * n, n)
        return jnp.where(position < half, 2 * position, 2 * (n - 1 - position) + 1)

    def body(
        residual,
        attention,
        quantized_codes,
        absmax,
        adapter_down,
        adapter_up,
        routed_slot_gate,
        selected,
        counts,
        cotangent,
    ):
        cap, all_heads = attention.shape
        tokens, cols = residual.shape
        heads = all_heads // n
        rank = adapter_up.shape[0]
        sub = heads // 2
        slots = n * cap
        side = 2 * rank
        down_t = adapter_down.T
        gate_row = routed_slot_gate.reshape(1, cap)
        selected_row = selected.reshape(1, cap)
        hbm = pl.BlockSpec(memory_space=pltpu.HBM)
        smem = pl.BlockSpec(memory_space=pltpu.SMEM)
        vmem = pl.BlockSpec(memory_space=pltpu.VMEM)

        def me():
            return lax.axis_index("seq"), lax.axis_index("tp") % 2

        def live_row(counts_ref):
            return lax.broadcasted_iota(I32, (1, cap), 1) < counts_ref[0]

        def pick(counts_ref, selected_ref):
            at = lax.broadcasted_iota(I32, (tokens, cap), 0) == selected_ref[...]
            return jnp.where(at & live_row(counts_ref), 1.0, 0.0).astype(BF)

        some = slots // 4
        live_slots = slots // 2

        def prepare(counts_ref, selected_ref, gate_ref, attention_ref, cot_ref, send_ref, own_ref, grad_ref, up_ref, chosen, gates, cots, sems):
            seq, core = me()
            first = [
                pltpu.make_async_copy(selected_ref, chosen, sems.at[0]),
                pltpu.make_async_copy(gate_ref, gates, sems.at[1]),
                pltpu.make_async_copy(cot_ref, cots, sems.at[2]),
            ]
            later = []
            for k in range(half):
                for ref, flipped in ((send_ref, 1), (own_ref, 0)):
                    at = pl.multiple_of((seq ^ (2 * k + flipped)) * heads + core * sub, 128)
                    sem = sems.at[3 + 2 * k + flipped]
                    later.append(pltpu.make_async_copy(attention_ref.at[:, pl.ds(at, sub)], ref.at[k], sem))
            for copy in first + later:
                copy.start()
            for copy in first:
                copy.wait()
            upstream = dot(pick(counts_ref, chosen), cots[...], 0, 0)
            up_ref[...] = upstream.astype(BF)
            live = column(jnp.where(live_row(counts_ref), 1.0, 0.0)) > 0
            grad_ref[...] = jnp.where(live, column(gates[...]) * upstream, DEAD).astype(BF)
            for copy in later:
                copy.wait()

        send, own, grad, upstream = call(
            prepare,
            [shape((half, cap, sub), BF)] * 2 + [shape((cap, cols), BF)] * 2,
            counts, in_hbm(selected_row), in_hbm(gate_row), in_hbm(attention), in_hbm(cotangent),
            in_specs=[smem] + [hbm] * 4,
            scratch=[
                pltpu.VMEM((1, cap), I32),
                pltpu.VMEM((1, cap), F32),
                pltpu.VMEM((tokens, cols), BF),
                pltpu.SemaphoreType.DMA((3 + n,)),
            ],
            name="prepare",
        )

        across = lax.ppermute(send, "seq", flip(n, 1))
        going, coming = lax.ppermute(grad, "seq", ring(1)), lax.ppermute(grad, "seq", ring(-1))
        block = min(64, sub)

        def dequantize(part, absmax):
            return call(
                functools.partial(dequant_kernel, part * sub), [shape((sub, cols), BF), shape((8, 128), F32)],
                in_hbm(quantized_codes), absmax,
                in_specs=[hbm, vmem], flops=sub * cols * 100, name="dequantize",
                scratch=[
                    pltpu.VMEM((sub // block, block, cols), I32),
                    pltpu.SemaphoreType.DMA((sub // block,)),
                ],
            )

        weights, marks = zip(dequantize(0, absmax), dequantize(1, absmax))
        across, going, coming, mark = lax.optimization_barrier((across, going, coming, marks[0]))

        gathered = {0: (grad,)}

        def hop(step, going, coming):
            gathered[n - step], gathered[step] = (going,), (coming,)
            return lax.ppermute(going, "seq", ring(1)), lax.ppermute(coming, "seq", ring(-1))

        def pair(own_ref, across_ref, token_ref, *refs):
            for k, ref in enumerate(refs):
                ref[0] = own_ref[k]
                ref[1] = across_ref[k]

        def join(*refs):
            *refs, token_ref, out_ref = refs
            for k, ref in enumerate(refs):
                out_ref[2 * k * cap : 2 * (k + 1) * cap, :] = ref[...].reshape(2 * cap, sub)

        pairs = call(pair, [shape((2, cap, sub), BF)] * half, own, across, mark, name="pair")
        fetched = [pairs[0]] + [lax.ppermute(pairs[k], "seq", flip(n, 2 * k)) for k in range(1, half)]
        going, coming = hop(1, going, coming)
        fetched, going, coming, mark = lax.optimization_barrier((fetched, going, coming, marks[1]))
        slots_own = call(join, [shape((slots, sub), BF)], *fetched, mark, name="join")[0]
        slots_other = lax.ppermute(slots_own, "tp", flip(tp, 1))
        for step in range(2, half - 1):
            going, coming = hop(step, going, coming)
        mid = cap // 2

        def forward(own_ref, other_ref, down_ref, up_ref, w0_ref, w1_ref, out_ref, low_ref):
            seq, core = me()
            a, b = own_ref[...], other_ref[...]
            att = jnp.concatenate([jnp.where(core == 0, a, b), jnp.where(core == 0, b, a)], axis=1)
            low = dot(att, down_ref[...], 1, 1)
            thrice = jnp.concatenate(split3(adapter_scale * low), axis=1)
            for j in range(n):
                low_ref[seq ^ j] = low[j * cap : (j + 1) * cap]
            spots = [lax.rem(place(seq ^ j) - place(seq) + n, n) for j in range(n)]
            tile = min(512, cols)
            for c in range(cols // tile):
                part = slice(c * tile, (c + 1) * tile)
                ups = up_ref[:, part]
                acc = dot(thrice, jnp.concatenate([ups] * 3, axis=0))
                acc = acc + dot(att[:, :sub], w0_ref[:, part]) + dot(att[:, sub:], w1_ref[:, part])
                acc = acc.astype(BF)
                for j in range(n):
                    out_ref[spots[j], :, part] = acc[j * cap : (j + 1) * cap]

        partial, low = call(
            forward,
            [shape((n, cap, cols), BF), shape((n, cap, rank), F32)],
            slots_own, slots_other, down_t, adapter_up, *weights,
            flops=2 * slots * heads * cols, name="forward",
        )

        going, coming, partial = lax.optimization_barrier((going, coming, partial))
        gathered[n - half + 1], gathered[half - 1] = (going,), (coming,)
        gathered[half] = (
            lax.ppermute(going[:mid], "seq", ring(1)),
            lax.ppermute(coming[mid:], "seq", ring(-1)),
        )

        spots = [r for r in range(n) if r != half]

        def backward(low_ref, up_ref, w0_ref, w1_ref, first_ref, second_ref, *refs):
            g_refs, (keep_ref, send_ref, live_ref, where_ref, low_out_ref, every, sums) = refs[: n - 1], refs[n - 1 :]
            seq, core = me()
            for r, ref in zip(spots, g_refs):
                every[shard_at(place(seq) + r)] = ref[...]
            every[shard_at(place(seq) + half)] = jnp.concatenate([first_ref[...], second_ref[...]])
            passed = jnp.zeros((1, 1), F32)
            row = lax.broadcasted_iota(I32, (cap, live_slots), 0).astype(F32)
            col = lax.broadcasted_iota(I32, (cap, live_slots), 1).astype(F32)
            for j in range(n):
                alive = jnp.where(every[j][:, :1].astype(F32) < 0.5 * (1 + DEAD), 1.0, 0.0)
                at = jnp.where((row + passed == col) & (alive > 0), 1.0, 0.0)
                where_ref[j * cap : (j + 1) * cap, :] = at.astype(BF)
                passed = passed + jnp.sum(alive, axis=0, keepdims=True)
            g = dot(where_ref[...], every[...].reshape(slots, cols), 0, 0).astype(BF)
            live_ref[...] = g
            tile = min(256, sub)
            for i in range(sub // tile):
                for at, ref in ((0, w0_ref), (sub, w1_ref)):
                    sums[:, at + i * tile : at + (i + 1) * tile] = dot(g, ref[i * tile : (i + 1) * tile, :], 1, 1)
            low = dot(where_ref[...], jnp.concatenate(split3(low_ref[...].reshape(slots, rank)), axis=1), 0, 0)
            low = low[:, :rank] + low[:, rank : 2 * rank] + low[:, 2 * rank :]
            low_out_ref[...] = jnp.concatenate([low[:some], low[some:]], axis=1)
            hi, lo = split2(adapter_scale * dot(g, up_ref[...], 1, 1))
            sums[:, heads:] = jnp.concatenate([hi, lo], axis=1).astype(F32)
            keep_ref[...] = sums[pl.ds(pl.multiple_of(core * some, 8), some), :]
            send_ref[...] = sums[pl.ds(pl.multiple_of((1 - core) * some, 8), some), :].astype(BF)

        wide = heads + side

        def back(*farthest):
            return call(
                backward,
                [
                    shape((some, wide), F32),
                    shape((some, wide), BF),
                    shape((live_slots, cols), BF),
                    shape((slots, live_slots), BF),
                    shape((some, side), F32),
                ],
                low, adapter_up, *weights, *farthest, *[gathered[r][0] for r in spots],
                flops=2 * live_slots * heads * cols,
                scratch=[pltpu.VMEM((n, cap, cols), BF), pltpu.VMEM((live_slots, wide), F32)],
                name="backward",
            )

        def ranks(a, b):
            return (a[:, heads : heads + rank].astype(F32) + b[:, heads : heads + rank].astype(F32)) + (
                a[:, heads + rank :].astype(F32) + b[:, heads + rank :].astype(F32)
            )

        def add(a_ref, b_ref, out_ref):
            a, b = a_ref[...], b_ref[...]
            out_ref[:, :heads] = (a[:, :heads].astype(F32) + b[:, :heads].astype(F32)).astype(BF)
            out_ref[:, heads:] = jnp.concatenate(split2(ranks(a, b)), axis=1)

        def finish(a_ref, b_ref, down_ref, out_ref):
            a, b = a_ref[...], b_ref[...]
            rank_grad = ranks(a, b).astype(BF)
            tail = dot(rank_grad, down_ref[...])
            out_ref[:, :heads] = (a[:, :heads].astype(F32) + b[:, :heads].astype(F32) + tail).astype(BF)
            out_ref[:, heads:] = jnp.concatenate([rank_grad, jnp.zeros_like(rank_grad)], axis=1)

        def plus(a, b):
            return (a.astype(F32) + b.astype(F32)).astype(BF)

        def sum_heads(keep, send):
            recv = yield lax.ppermute(send, "tp", flip(tp, 1))
            mine = call(add, [shape((some, wide), BF)], keep, recv, name="add")[0]
            bit = 2
            while 2 * bit < tp:
                recv = yield lax.ppermute(mine, "tp", flip(tp, bit))
                mine = call(add, [shape((some, wide), BF)], mine, recv, name="add")[0]
                bit *= 2
            recv = yield lax.ppermute(mine, "tp", flip(tp, bit))
            done = call(finish, [shape((some, wide), BF)], mine, recv, down_t, name="finish")[0]
            other_done = yield lax.ppermute(done, "tp", flip(tp, 1))
            return done, other_done

        def sum_low(total):
            bit = 1
            while bit < n:
                recv = yield lax.ppermute(total, "seq", flip(n, bit))
                total = total + recv
                bit *= 2
            return total

        def drain(steps, value):
            try:
                while True:
                    value = steps.send(value)
            except StopIteration as stop:
                return stop.value

        here, there = partial[half, :mid], partial[half, mid:]
        going, coming = lax.ppermute(here, "seq", ring(1)), lax.ppermute(there, "seq", ring(-1))
        for step in range(half - 1, 0, -1):
            here, there = partial[step], partial[n - step]
            if step == half - 1:
                here = jnp.concatenate([plus(here[:mid], going), here[mid:]])
                there = jnp.concatenate([there[:mid], plus(there[mid:], coming)])
            else:
                here, there = plus(here, going), plus(there, coming)
            if step == half - 1:
                here, there, *farthest = lax.optimization_barrier((here, there, *gathered[half]))
                keep, send, grad_live, where_live, low_live = back(*farthest)
            elif step == half - 2:
                here, there, send = lax.optimization_barrier((here, there, send))
                head_steps, head_value = sum_heads(keep, send), None
            else:
                here, there, head_value, low_live = lax.optimization_barrier((here, there, head_value, low_live))
            going = lax.ppermute(here, "seq", ring(1))
            coming = lax.ppermute(there, "seq", ring(-1))
            if half - 4 < step < half - 1:
                head_value = head_steps.send(head_value)
        low_steps = sum_low(low_live)
        low_value = low_steps.send(None)
        going, coming, head_value, low_value = lax.optimization_barrier((going, coming, head_value, low_value))
        done, other_done = drain(head_steps, head_value)
        going, coming, done = lax.optimization_barrier((going, coming, done))
        low_sum = drain(low_steps, low_value)

        def home(counts_ref, selected_ref, gate_ref, res_ref, own_ref, going_ref, coming_ref, up_ref, out_ref, gate_out_ref):
            chosen = pick(counts_ref, selected_ref)
            block = own_ref[...].astype(F32) + going_ref[...].astype(F32) + coming_ref[...].astype(F32)
            gate_out_ref[...] = row_of(jnp.sum(up_ref[...].astype(F32) * block, axis=1, keepdims=True))
            res = res_ref[...]
            picked = dot(chosen, res, 0, 0)
            updated = (picked + column(gate_ref[...]) * block).astype(BF)
            hit = jnp.sum(chosen.astype(F32), axis=1, keepdims=True) > 0
            out_ref[...] = jnp.where(hit, dot(chosen, updated), res.astype(F32)).astype(BF)

        outgoing_residual, gate_part = call(
            home,
            [shape((tokens, cols), BF), shape((1, cap), F32)],
            counts, selected_row, gate_row, residual, partial[0], going, coming, upstream,
            in_specs=[smem] + [vmem] * 7, name="home",
        )
        bit = 1
        while bit < tp:
            gate_part = gate_part + lax.ppermute(gate_part, "tp", flip(tp, bit))
            bit *= 2

        def last(a_ref, b_ref, where_ref, own_ref, other_ref, grad_ref, down_grad_ref, live, rank_ref):
            seq, core = me()
            for ref, at in ((a_ref, core), (b_ref, 1 - core)):
                live[pl.ds(pl.multiple_of(at * some, 16), some), :] = ref[...]
            every = dot(where_ref[...], live[...]).astype(BF)
            grad_ref[...] = every[:, :heads]
            for j in range(n):
                rank_ref[j] = every[j * cap : (j + 1) * cap, heads:]
            rank_grad = jnp.concatenate([rank_ref[seq ^ j] for j in range(n)], axis=0)[:, :rank]
            for ref, at in ((own_ref, core), (other_ref, 1 - core)):
                down_grad_ref[:, pl.ds(pl.multiple_of(at * sub, 128), sub)] = dot(rank_grad, ref[...], 0, 0)

        attention_output_grad, down_gradient = call(
            last,
            [shape((slots, heads), BF), shape((rank, heads), F32)],
            done, other_done, where_live, slots_own, slots_other,
            scratch=[pltpu.VMEM((live_slots, wide), BF), pltpu.VMEM((n, cap, side), BF)], name="last",
        )

        def up_gradient(low_ref, g_ref, out_ref):
            low = jnp.concatenate([low_ref[:, :rank], low_ref[:, rank:]], axis=0)
            thrice = dot(jnp.concatenate(split3(low), axis=1), g_ref[...], 0, 0)
            out_ref[...] = adapter_scale * (
                thrice[:rank] + thrice[rank : 2 * rank] + thrice[2 * rank :]
            )

        adapter_up_gradient = call(
            up_gradient, [shape((rank, cols), F32)], low_sum, grad_live,
            flops=6 * live_slots * rank * cols, name="up_gradient",
        )[0]
        return (
            outgoing_residual,
            attention_output_grad,
            down_gradient.T,
            adapter_up_gradient,
            gate_part.reshape(cap),
        )

    return jax.shard_map(
        body,
        mesh=mesh,
        in_specs=(
            P("seq", "tp"),
            P("seq", None),
            P("seq", "tp"),
            P("seq", "tp"),
            P("seq", None),
            P(None, "tp"),
            P("seq"),
            P("seq"),
            P("seq"),
            P("seq", "tp"),
        ),
        out_specs=(P("seq", "tp"), P(None, "seq"), P("seq", None), P(None, "tp"), P("seq")),
        check_vma=False,
    )
```

time: 100 us -> 82.3 us (0.82)
  waiting for transfers between devices: 31.3 us -> 23.7 us
  local copies, waits for them, and re-layouts: 6.08 us -> 0.28 us
  Pallas kernels: 25.4 us -> 22.2 us
  other arithmetic: 1.88 us -> 0.81 us
    pallas_call x4 -> x0, Pallas kernels: 11.9 us -> none  [dequantize(): pl.pallas_call(dequant_kernel, grid=(steps,), out_shape=shape((own, cols)...]
    pallas_call x8 -> x12, Pallas kernels: 13.5 us -> 22.2 us  [call(): pl.pallas_call(kernel, out_shape=tuple(outs), in_specs=in_specs or [whole...]
    ppermute x3, waiting for transfers between devices: 0.01 us -> 4.82 us  [body(): going = lax.ppermute(here, 'seq', ring(1))]
    unnamed x33 -> x13, local copies, waits for them, and re-layouts: 4.87 us -> 0.22 us
    ppermute x14, waiting for transfers between devices: 14.5 us -> 10.5 us  [the longest x3 4.88 us: sum_low(): recv = (yield lax.ppermute(total, 'seq', flip(n, bit)))]
    ppermute x1, waiting for transfers between devices: 4.9 us -> 1.53 us  [body(): across = lax.ppermute(send, 'seq', flip(n, 1))]
    ppermute x3, waiting for transfers between devices: 6.84 us -> 3.52 us  [body(): lax.ppermute(pairs[k], 'seq', flip(n, 2 * k))]
    ppermute x14, starting transfers between devices: 14.7 us -> 17.2 us  [the longest x3 5.83 us: sum_low(): recv = (yield lax.ppermute(total, 'seq', flip(n, bit)))]
  transfers between devices with their start and end apart: 29 -> 29, of which waited for: 9 -> 18; matrix products, arithmetic and copies ran while one was open for 3% -> 1% of each run, Pallas kernels for 24% -> 23%
where the time goes in v2:
time: 82.3 us; the launch traced here: 82.2 us
  starting transfers between devices  33.6 us (41%)
  waiting for transfers between devices  23.7 us (29%)
  Pallas kernels  22.2 us (27%)
  between operations  1.54 us (2%)
    pallas_call x12, Pallas kernels, call(): pl.pallas_call(kernel, out_shape=tuple(outs), in_specs=in_specs or [whole...  22.2 us
    ppermute x3, starting transfers between devices, sum_low(): recv = (yield lax.ppermute(total, 'seq', flip(n, bit)))  5.83 us
    ppermute x3, starting transfers between devices, body(): lax.ppermute(pairs[k], 'seq', flip(n, 2 * k))  5.7 us
    ppermute x3, waiting for transfers between devices, sum_low(): recv = (yield lax.ppermute(total, 'seq', flip(n, bit)))  4.88 us
    ppermute x3, waiting for transfers between devices, body(): going = lax.ppermute(here, 'seq', ring(1))  4.82 us
    ppermute x3, starting transfers between devices, body(): coming = lax.ppermute(there, 'seq', ring(-1))  4.26 us
    ppermute x3, waiting for transfers between devices, body(): lax.ppermute(pairs[k], 'seq', flip(n, 2 * k))  3.52 us
    ppermute x1, starting transfers between devices, body(): lax.ppermute(grad, 'seq', ring(1))  3.08 us
  transfers between devices with their start and end apart: 29, of which 18 were waited for; matrix products, arithmetic and copies ran while one was open for 1% of the time, Pallas kernels for 23%

profile of v2, /device:TPU:0, one launch (start us, length us, event | category | flops | bytes accessed | tf_op | source)
XLA Modules:
  0.0 82.2 jit_solution(7485769578242442355)
XLA Ops:
  1.3 1.6 %prepare.1 = (bf16[4,48,512]{2,1,0:T(8,128)(2,1)S(1)}, bf16[4,48,512]{2,1,0:T(8,128)(2,1)S(1)}, bf16[48,2048]{1,0:T(8,128)(2,1)S(1)}, bf16[48,2048]{1,0:T(8,128)(2,1)S(1)}) custom-call(s32[1]{0:T(128)S(6)} %copy.17.counts_ref, s32[1,48]{1,0:T(1,128)} %bitcast.36, f32[1,48]{1,0:T(1,128)} %bitcast.38, bf16[48,8192]{1,0:T(8,128)(2,1)} %attention_ref.1, ...), custom_call_target="tpu_custom_call" | custom-call | bytes 2359684 | tf_op jit(solution)/shard_map/prepare/pallas_call | solution.py:55
  2.9 3.1 %collective-permute-start.1 = (bf16[48,2048]{1,0:T(8,128)(2,1)S(1)}, bf16[48,2048]{1,0:T(8,128)(2,1)S(1)}, u32[]{:S(2)}, u32[]{:S(2)}) collective-permute-start(bf16[48,2048]{1,0:T(8,128)(2,1)S(1)} %get-tuple-element.62.refs_0_), channel_id=1, source_target_pairs={{0,8},{8,16},{16,24},{24,28},{28,20},{20,12},{12,4},{4,0},{1,9},{9... | collective-permute-start | bytes 589832 | tf_op jit(solution)/shard_map/ppermute | solution.py:217
  6.0 1.9 %collective-permute-start = (bf16[4,48,512]{2,1,0:T(8,128)(2,1)S(1)}, bf16[4,48,512]{2,1,0:T(8,128)(2,1)S(1)}, u32[]{:S(2)}, u32[]{:S(2)}) collective-permute-start(bf16[4,48,512]{2,1,0:T(8,128)(2,1)S(1)} %get-tuple-element.61), channel_id=1, source_target_pairs={{0,4},{4,0},{8,12},{12,8},{16,20},{20,16},{24,28},{28,24},{1,5},{5... | collective-permute-start | bytes 589832 | tf_op jit(solution)/shard_map/ppermute | solution.py:216
  8.1 5.3 %dequantize.2 = (bf16[512,2048]{1,0:T(8,128)(2,1)S(1)}, f32[8,128]{1,0:T(8,128)S(1)}) custom-call(s32[1024,2048]{1,0:T(8,128)} %codes_hbm.3, f32[1024,32]{1,0:T(8,128)S(1)} %copy.15.absmax_ref), custom_call_target="tpu_custom_call" | custom-call | flops 104857600 | bytes 10620928 | tf_op jit(solution)/shard_map/dequantize/pallas_call | solution.py:55
  13.5 1.5 %collective-permute-done.across_ref = bf16[4,48,512]{2,1,0:T(8,128)(2,1)S(1)} collective-permute-done((bf16[4,48,512]{2,1,0:T(8,128)(2,1)S(1)}, bf16[4,48,512]{2,1,0:T(8,128)(2,1)S(1)}, u32[]{:S(2)}, u32[]{:S(2)}) %collective-permute-start) | collective-permute-done | bytes 196640 | tf_op jit(solution)/shard_map/ppermute | solution.py:216
  15.1 1.9 %collective-permute-start.7 = (bf16[48,2048]{1,0:T(8,128)(2,1)S(1)}, bf16[48,2048]{1,0:T(8,128)(2,1)S(1)}, u32[]{:S(2)}, u32[]{:S(2)}) collective-permute-start(bf16[48,2048]{1,0:T(8,128)(2,1)S(1)} %collective-permute-done.2.refs_1_), channel_id=1, source_target_pairs={{0,4},{8,0},{16,8},{24,16},{28,24},{20,28},{12,20},{4,12},{1,5},{9... | collective-permute-start | bytes 589832 | tf_op jit(solution)/shard_map/ppermute | solution.py:238
  17.2 5.5 %collective-permute-start.4 = (bf16[2,48,512]{2,1,0:T(8,128)(2,1)S(1)}, bf16[2,48,512]{2,1,0:T(8,128)(2,1)S(1)}, u32[]{:S(2)}, u32[]{:S(2)}) collective-permute-start(bf16[2,48,512]{2,1,0:T(8,128)(2,1)S(1)} %get-tuple-element.68), channel_id=1, source_target_pairs={{0,16},{4,20},{8,24},{12,28},{16,0},{20,4},{24,8},{28,12},{1,17},{... | collective-permute-start | bytes 294920 | tf_op jit(solution)/shard_map/ppermute | solution.py:251
  22.8 5.4 %dequantize.3 = (bf16[512,2048]{1,0:T(8,128)(2,1)S(1)}, f32[8,128]{1,0:T(8,128)S(1)}) custom-call(s32[1024,2048]{1,0:T(8,128)} %codes_hbm.3, f32[1024,32]{1,0:T(8,128)S(1)} %copy.15.absmax_ref), custom_call_target="tpu_custom_call" | custom-call | flops 104857600 | bytes 10620928 | tf_op jit(solution)/shard_map/dequantize/pallas_call | solution.py:55
  28.2 1.2 %collective-permute-done.4.refs_2_ = bf16[2,48,512]{2,1,0:T(8,128)(2,1)S(1)} collective-permute-done((bf16[2,48,512]{2,1,0:T(8,128)(2,1)S(1)}, bf16[2,48,512]{2,1,0:T(8,128)(2,1)S(1)}, u32[]{:S(2)}, u32[]{:S(2)}) %collective-permute-start.4) | collective-permute-done | bytes 98336 | tf_op jit(solution)/shard_map/ppermute | solution.py:251
  29.3 2.3 %collective-permute-done.5.refs_3_ = bf16[2,48,512]{2,1,0:T(8,128)(2,1)S(1)} collective-permute-done((bf16[2,48,512]{2,1,0:T(8,128)(2,1)S(1)}, bf16[2,48,512]{2,1,0:T(8,128)(2,1)S(1)}, u32[]{:S(2)}, u32[]{:S(2)}) %collective-permute-start.5) | collective-permute-done | bytes 98336 | tf_op jit(solution)/shard_map/ppermute | solution.py:251
  31.8 1.4 %collective-permute-start.8 = (bf16[48,2048]{1,0:T(8,128)(2,1)S(1)}, bf16[48,2048]{1,0:T(8,128)(2,1)S(1)}, u32[]{:S(2)}, u32[]{:S(2)}) collective-permute-start(bf16[48,2048]{1,0:T(8,128)(2,1)S(1)} %collective-permute-done.6.refs_5_), channel_id=1, source_target_pairs={{0,8},{8,16},{16,24},{24,28},{28,20},{20,12},{12,4},{4,0},{1,9},{9... | collective-permute-start | bytes 589832 | tf_op jit(solution)/shard_map/ppermute | solution.py:238
  33.9 2.5 %forward.1 = (bf16[8,48,2048]{2,1,0:T(8,128)(2,1)S(1)}, f32[8,48,64]{2,1,0:T(8,128)S(1)}) custom-call(bf16[384,512]{1,0:T(8,128)(2,1)S(1)} %join.1.own_ref, bf16[384,512]{1,0:T(8,128)(2,1)S(1)} %collective-permute-done.10.other_ref, bf16[64,1024]{1,0:T(8,128)(2,1)S(1)} %bitcast.34, bf16[64,2048]{1,0:T(8,128)(2,1)S(1)} %copy-done.1, ...), custom_call_target="tpu_custom_call" | custom-call | flops 1610612736 | bytes 7045120 | tf_op jit(solution)/shard_map/forward/pallas_call | solution.py:55
  36.4 2.7 %collective-permute-done.8.refs_4_ = bf16[48,2048]{1,0:T(8,128)(2,1)S(1)} collective-permute-done((bf16[48,2048]{1,0:T(8,128)(2,1)S(1)}, bf16[48,2048]{1,0:T(8,128)(2,1)S(1)}, u32[]{:S(2)}, u32[]{:S(2)}) %collective-permute-start.8) | collective-permute-done | bytes 196640 | tf_op jit(solution)/shard_map/ppermute | solution.py:238
  39.1 1.1 %collective-permute-done.9.refs_3_ = bf16[48,2048]{1,0:T(8,128)(2,1)S(1)} collective-permute-done((bf16[48,2048]{1,0:T(8,128)(2,1)S(1)}, bf16[48,2048]{1,0:T(8,128)(2,1)S(1)}, u32[]{:S(2)}, u32[]{:S(2)}) %collective-permute-start.9) | collective-permute-done | bytes 196640 | tf_op jit(solution)/shard_map/ppermute | solution.py:238
  40.6 1.7 %collective-permute-start.12 = (bf16[24,2048]{1,0:T(8,128)(2,1)S(1)}, bf16[24,2048]{1,0:T(8,128)(2,1)S(1)}, u32[]{:S(2)}, u32[]{:S(2)}) collective-permute-start(bf16[24,2048]{1,0:T(8,128)(2,1)S(1)} %get-tuple-element.120), channel_id=1, source_target_pairs={{0,4},{8,0},{16,8},{24,16},{28,24},{20,28},{12,20},{4,12},{1,5},{9... | collective-permute-start | bytes 294920 | tf_op jit(solution)/shard_map/ppermute | solution.py:390
  42.7 1.8 %collective-permute-start.14 = (bf16[24,2048]{1,0:T(8,128)(2,1)S(1)}, bf16[24,2048]{1,0:T(8,128)(2,1)S(1)}, u32[]{:S(2)}, u32[]{:S(2)}) collective-permute-start(bf16[24,2048]{1,0:T(8,128)(2,1)S(1)} %slice.65), channel_id=1, source_target_pairs={{0,4},{8,0},{16,8},{24,16},{28,24},{20,28},{12,20},{4,12},{1,5},{9... | collective-permute-start | bytes 294920 | tf_op jit(solution)/shard_map/ppermute | solution.py:290
  44.4 1.4 %collective-permute-done.11 = bf16[24,2048]{1,0:T(8,128)(2,1)S(1)} collective-permute-done((bf16[24,2048]{1,0:T(8,128)(2,1)S(1)}, bf16[24,2048]{1,0:T(8,128)(2,1)S(1)}, u32[]{:S(2)}, u32[]{:S(2)}) %collective-permute-start.11) | collective-permute-done | bytes 98336 | tf_op jit(solution)/shard_map/ppermute | solution.py:390
  47.6 1.7 %collective-permute-start.16 = (bf16[48,2048]{1,0:T(8,128)(2,1)S(1)}, bf16[48,2048]{1,0:T(8,128)(2,1)S(1)}, u32[]{:S(2)}, u32[]{:S(2)}) collective-permute-start(bf16[48,2048]{1,0:T(8,128)(2,1)S(1)} %get-tuple-element.87), channel_id=1, source_target_pairs={{0,4},{8,0},{16,8},{24,16},{28,24},{20,28},{12,20},{4,12},{1,5},{9... | collective-permute-start | bytes 589832 | tf_op jit(solution)/shard_map/ppermute | solution.py:407
  49.3 2.6 %backward.1 = (f32[96,1152]{1,0:T(8,128)S(1)}, bf16[96,1152]{1,0:T(8,128)(2,1)S(1)}, bf16[192,2048]{1,0:T(8,128)(2,1)S(1)}, bf16[384,192]{1,0:T(8,128)(2,1)S(1)}, f32[96,128]{1,0:T(8,128)S(1)}) custom-call(f32[8,48,64]{2,1,0:T(8,128)S(1)} %get-tuple-element.88.low_ref, bf16[64,2048]{1,0:T(8,128)(2,1)S(1)} %copy-done.1, ...), custom_call_target="tpu_custom_call" | custom-call | flops 805306368 | bytes 7774208 | tf_op jit(solution)/shard_map/backward/pallas_call | solution.py:55
  52.0 1.2 %collective-permute-done.15 = bf16[48,2048]{1,0:T(8,128)(2,1)S(1)} collective-permute-done((bf16[48,2048]{1,0:T(8,128)(2,1)S(1)}, bf16[48,2048]{1,0:T(8,128)(2,1)S(1)}, u32[]{:S(2)}, u32[]{:S(2)}) %collective-permute-start.15) | collective-permute-done | bytes 196640 | tf_op jit(solution)/shard_map/ppermute | solution.py:406
  53.6 1.9 %collective-permute-start.18 = (bf16[48,2048]{1,0:T(8,128)(2,1)S(1)}, bf16[48,2048]{1,0:T(8,128)(2,1)S(1)}, u32[]{:S(2)}, u32[]{:S(2)}) collective-permute-start(bf16[48,2048]{1,0:T(8,128)(2,1)S(1)} %get-tuple-element.93), channel_id=1, source_target_pairs={{0,4},{8,0},{16,8},{24,16},{28,24},{20,28},{12,20},{4,12},{1,5},{9... | collective-permute-start | bytes 589832 | tf_op jit(solution)/shard_map/ppermute | solution.py:407
  55.5 3.6 %collective-permute-done.17 = bf16[48,2048]{1,0:T(8,128)(2,1)S(1)} collective-permute-done((bf16[48,2048]{1,0:T(8,128)(2,1)S(1)}, bf16[48,2048]{1,0:T(8,128)(2,1)S(1)}, u32[]{:S(2)}, u32[]{:S(2)}) %collective-permute-start.17) | collective-permute-done | bytes 196640 | tf_op jit(solution)/shard_map/ppermute | solution.py:406
  59.6 1.6 %collective-permute-start.22 = (bf16[96,1152]{1,0:T(8,128)(2,1)S(1)}, bf16[96,1152]{1,0:T(8,128)(2,1)S(1)}, u32[]{:S(2)}, u32[]{:S(2)}) collective-permute-start(bf16[96,1152]{1,0:T(8,128)(2,1)S(1)} %add.64.a_ref), channel_id=1, source_target_pairs={{0,2},{1,3},{2,0},{3,1},{4,6},{5,7},{6,4},{7,5},{8,10},{9,11},{10,... | collective-permute-start | bytes 663560 | tf_op jit(solution)/shard_map/ppermute | solution.py:369
  61.2 1.4 %collective-permute-start.20 = (bf16[48,2048]{1,0:T(8,128)(2,1)S(1)}, bf16[48,2048]{1,0:T(8,128)(2,1)S(1)}, u32[]{:S(2)}, u32[]{:S(2)}) collective-permute-start(bf16[48,2048]{1,0:T(8,128)(2,1)S(1)} %get-tuple-element.96), channel_id=1, source_target_pairs={{0,8},{8,16},{16,24},{24,28},{28,20},{20,12},{12,4},{4,0},{1,9},{9... | collective-permute-start | bytes 589832 | tf_op jit(solution)/shard_map/ppermute | solution.py:406
  63.2 1.9 %collective-permute-start.23 = (f32[96,128]{1,0:T(8,128)S(1)}, f32[96,128]{1,0:T(8,128)S(1)}, u32[]{:S(2)}, u32[]{:S(2)}) collective-permute-start(f32[96,128]{1,0:T(8,128)S(1)} %get-tuple-element.100), channel_id=1, source_target_pairs={{0,4},{4,0},{8,12},{12,8},{16,20},{20,16},{24,28},{28,24},{1,5},{5... | collective-permute-start | bytes 147464 | tf_op jit(solution)/shard_map/ppermute | solution.py:377
  65.1 2.3 %collective-permute-done.23 = f32[96,128]{1,0:T(8,128)S(1)} collective-permute-done((f32[96,128]{1,0:T(8,128)S(1)}, f32[96,128]{1,0:T(8,128)S(1)}, u32[]{:S(2)}, u32[]{:S(2)}) %collective-permute-start.23) | collective-permute-done | bytes 49184 | tf_op jit(solution)/shard_map/ppermute | solution.py:377
  67.4 1.4 %collective-permute-done.21.coming_ref = bf16[48,2048]{1,0:T(8,128)(2,1)S(1)} collective-permute-done((bf16[48,2048]{1,0:T(8,128)(2,1)S(1)}, bf16[48,2048]{1,0:T(8,128)(2,1)S(1)}, u32[]{:S(2)}, u32[]{:S(2)}) %collective-permute-start.21) | collective-permute-done | bytes 196640 | tf_op jit(solution)/shard_map/ppermute | solution.py:407
  69.6 1.5 %home.1 = (bf16[192,2048]{1,0:T(8,128)(2,1)}, f32[1,48]{1,0:T(1,128)S(1)}) custom-call(s32[1]{0:T(128)S(6)} %copy.17.counts_ref, s32[1,48]{1,0:T(1,128)S(1)} %bitcast.37, f32[1,48]{1,0:T(1,128)S(1)} %bitcast.39, bf16[192,2048]{1,0:T(8,128)(2,1)S(1)} %copy-done, bf16[48,2048]{1,0:T(8,128)(2,1)S(1)} %slice_bitcast_fusion.own_ref, ...), custom_call_target="tpu_custom_call" | custom-call | bytes 2359876 | tf_op jit(solution)/shard_map/home/pallas_call | solution.py:55
  72.9 3.4 %collective-permute-start.26 = (f32[96,128]{1,0:T(8,128)S(1)}, f32[96,128]{1,0:T(8,128)S(1)}, u32[]{:S(2)}, u32[]{:S(2)}) collective-permute-start(f32[96,128]{1,0:T(8,128)S(1)} %add.41), channel_id=1, source_target_pairs={{0,16},{4,20},{8,24},{12,28},{16,0},{20,4},{24,8},{28,12},{1,17},{... | collective-permute-start | bytes 147464 | tf_op jit(solution)/shard_map/ppermute | solution.py:377
  76.9 2.3 %collective-permute-done.26 = f32[96,128]{1,0:T(8,128)S(1)} collective-permute-done((f32[96,128]{1,0:T(8,128)S(1)}, f32[96,128]{1,0:T(8,128)S(1)}, u32[]{:S(2)}, u32[]{:S(2)}) %collective-permute-start.26) | collective-permute-done | bytes 49184 | tf_op jit(solution)/shard_map/ppermute | solution.py:377
  79.2 1.3 %up_gradient.1 = f32[64,2048]{1,0:T(8,128)} custom-call(f32[96,128]{1,0:T(8,128)S(1)} %add.42.low_ref, bf16[192,2048]{1,0:T(8,128)(2,1)S(1)} %get-tuple-element.113.g_ref), custom_call_target="tpu_custom_call" | custom-call | flops 150994944 | bytes 1359872 | tf_op jit(solution)/shard_map/up_gradient/pallas_call | solution.py:55
  80.6 1.6 %last.1 = (bf16[384,1024]{1,0:T(8,128)(2,1)}, f32[64,1024]{1,0:T(8,128)}) custom-call(bf16[96,1152]{1,0:T(8,128)(2,1)S(1)} %finish.1.a_ref, bf16[96,1152]{1,0:T(8,128)(2,1)S(1)} %collective-permute-done.24.b_ref, bf16[384,192]{1,0:T(8,128)(2,1)S(1)} %get-tuple-element.109.where_ref, bf16[384,512]{1,0:T(8,128)(2,1)S(1)} %join.1.own_ref, ...), custom_call_target="tpu_custom_call" | custom-call | bytes 2424832 | tf_op jit(solution)/shard_map/last/pallas_call | solution.py:55
  (64 shorter events, 8.5 us)
Async XLA Ops:
  2.9 10.6 %collective-permute-start.1 = (bf16[48,2048]{1,0:T(8,128)(2,1)S(1)}, bf16[48,2048]{1,0:T(8,128)(2,1)S(1)}, u32[]{:S(2)}, u32[]{:S(2)}) collective-permute-start(bf16[48,2048]{1,0:T(8,128)(2,1)S(1)} %get-tuple-element.62.refs_0_), channel_id=1, source_target_pairs={{0,8},{8,16},{16,24},{24,28},{28,20},{20,12},{12,4},{4,0},{1,9},{9... | collective-permute-start | bytes 589832 | tf_op jit(solution)/shard_map/ppermute | solution.py:217
  6.0 7.5 %collective-permute-start.2 = (bf16[48,2048]{1,0:T(8,128)(2,1)S(1)}, bf16[48,2048]{1,0:T(8,128)(2,1)S(1)}, u32[]{:S(2)}, u32[]{:S(2)}) collective-permute-start(bf16[48,2048]{1,0:T(8,128)(2,1)S(1)} %get-tuple-element.62.refs_0_), channel_id=1, source_target_pairs={{0,4},{8,0},{16,8},{24,16},{28,24},{20,28},{12,20},{4,12},{1,5},{9... | collective-permute-start | bytes 589832 | tf_op jit(solution)/shard_map/ppermute | solution.py:217
  6.0 9.0 %collective-permute-start = (bf16[4,48,512]{2,1,0:T(8,128)(2,1)S(1)}, bf16[4,48,512]{2,1,0:T(8,128)(2,1)S(1)}, u32[]{:S(2)}, u32[]{:S(2)}) collective-permute-start(bf16[4,48,512]{2,1,0:T(8,128)(2,1)S(1)} %get-tuple-element.61), channel_id=1, source_target_pairs={{0,4},{4,0},{8,12},{12,8},{16,20},{20,16},{24,28},{28,24},{1,5},{5... | collective-permute-start | bytes 589832 | tf_op jit(solution)/shard_map/ppermute | solution.py:216
  15.0 16.7 %collective-permute-start.6 = (bf16[48,2048]{1,0:T(8,128)(2,1)S(1)}, bf16[48,2048]{1,0:T(8,128)(2,1)S(1)}, u32[]{:S(2)}, u32[]{:S(2)}) collective-permute-start(bf16[48,2048]{1,0:T(8,128)(2,1)S(1)} %collective-permute-done.1.refs_6_), channel_id=1, source_target_pairs={{0,8},{8,16},{16,24},{24,28},{28,20},{20,12},{12,4},{4,0},{1,9},{9... | collective-permute-start | bytes 589832 | tf_op jit(solution)/shard_map/ppermute | solution.py:238
  15.1 16.6 %collective-permute-start.7 = (bf16[48,2048]{1,0:T(8,128)(2,1)S(1)}, bf16[48,2048]{1,0:T(8,128)(2,1)S(1)}, u32[]{:S(2)}, u32[]{:S(2)}) collective-permute-start(bf16[48,2048]{1,0:T(8,128)(2,1)S(1)} %collective-permute-done.2.refs_1_), channel_id=1, source_target_pairs={{0,4},{8,0},{16,8},{24,16},{28,24},{20,28},{12,20},{4,12},{1,5},{9... | collective-permute-start | bytes 589832 | tf_op jit(solution)/shard_map/ppermute | solution.py:238
  17.1 11.1 %collective-permute-start.3 = (bf16[2,48,512]{2,1,0:T(8,128)(2,1)S(1)}, bf16[2,48,512]{2,1,0:T(8,128)(2,1)S(1)}, u32[]{:S(2)}, u32[]{:S(2)}) collective-permute-start(bf16[2,48,512]{2,1,0:T(8,128)(2,1)S(1)} %get-tuple-element.67), channel_id=1, source_target_pairs={{0,8},{4,12},{8,0},{12,4},{16,24},{20,28},{24,16},{28,20},{1,9},{5... | collective-permute-start | bytes 294920 | tf_op jit(solution)/shard_map/ppermute | solution.py:251
  17.2 12.1 %collective-permute-start.4 = (bf16[2,48,512]{2,1,0:T(8,128)(2,1)S(1)}, bf16[2,48,512]{2,1,0:T(8,128)(2,1)S(1)}, u32[]{:S(2)}, u32[]{:S(2)}) collective-permute-start(bf16[2,48,512]{2,1,0:T(8,128)(2,1)S(1)} %get-tuple-element.68), channel_id=1, source_target_pairs={{0,16},{4,20},{8,24},{12,28},{16,0},{20,4},{24,8},{28,12},{1,17},{... | collective-permute-start | bytes 294920 | tf_op jit(solution)/shard_map/ppermute | solution.py:251
  22.8 8.9 %collective-permute-start.5 = (bf16[2,48,512]{2,1,0:T(8,128)(2,1)S(1)}, bf16[2,48,512]{2,1,0:T(8,128)(2,1)S(1)}, u32[]{:S(2)}, u32[]{:S(2)}) collective-permute-start(bf16[2,48,512]{2,1,0:T(8,128)(2,1)S(1)} %get-tuple-element.69), channel_id=1, source_target_pairs={{0,24},{4,28},{8,16},{12,20},{16,8},{20,12},{24,0},{28,4},{1,25},{... | collective-permute-start | bytes 294920 | tf_op jit(solution)/shard_map/ppermute | solution.py:251
  31.7 2.2 %collective-permute-start.10 = (bf16[384,512]{1,0:T(8,128)(2,1)S(1)}, bf16[384,512]{1,0:T(8,128)(2,1)S(1)}, u32[]{:S(2)}, u32[]{:S(2)}) collective-permute-start(bf16[384,512]{1,0:T(8,128)(2,1)S(1)} %join.1.own_ref), channel_id=1, source_target_pairs={{0,1},{1,0},{2,3},{3,2},{4,5},{5,4},{6,7},{7,6},{8,9},{9,8},{10,11... | collective-permute-start | bytes 1179656 | tf_op jit(solution)/shard_map/ppermute | solution.py:255
  31.8 7.3 %collective-permute-start.8 = (bf16[48,2048]{1,0:T(8,128)(2,1)S(1)}, bf16[48,2048]{1,0:T(8,128)(2,1)S(1)}, u32[]{:S(2)}, u32[]{:S(2)}) collective-permute-start(bf16[48,2048]{1,0:T(8,128)(2,1)S(1)} %collective-permute-done.6.refs_5_), channel_id=1, source_target_pairs={{0,8},{8,16},{16,24},{24,28},{28,20},{20,12},{12,4},{4,0},{1,9},{9... | collective-permute-start | bytes 589832 | tf_op jit(solution)/shard_map/ppermute | solution.py:238
  33.2 7.0 %collective-permute-start.9 = (bf16[48,2048]{1,0:T(8,128)(2,1)S(1)}, bf16[48,2048]{1,0:T(8,128)(2,1)S(1)}, u32[]{:S(2)}, u32[]{:S(2)}) collective-permute-start(bf16[48,2048]{1,0:T(8,128)(2,1)S(1)} %collective-permute-done.7.refs_2_), channel_id=1, source_target_pairs={{0,4},{8,0},{16,8},{24,16},{28,24},{20,28},{12,20},{4,12},{1,5},{9... | collective-permute-start | bytes 589832 | tf_op jit(solution)/shard_map/ppermute | solution.py:238
  40.2 5.6 %collective-permute-start.11 = (bf16[24,2048]{1,0:T(8,128)(2,1)S(1)}, bf16[24,2048]{1,0:T(8,128)(2,1)S(1)}, u32[]{:S(2)}, u32[]{:S(2)}) collective-permute-start(bf16[24,2048]{1,0:T(8,128)(2,1)S(1)} %get-tuple-element.122), channel_id=1, source_target_pairs={{0,8},{8,16},{16,24},{24,28},{28,20},{20,12},{12,4},{4,0},{1,9},{9... | collective-permute-start | bytes 294920 | tf_op jit(solution)/shard_map/ppermute | solution.py:390
  40.6 5.7 %collective-permute-start.12 = (bf16[24,2048]{1,0:T(8,128)(2,1)S(1)}, bf16[24,2048]{1,0:T(8,128)(2,1)S(1)}, u32[]{:S(2)}, u32[]{:S(2)}) collective-permute-start(bf16[24,2048]{1,0:T(8,128)(2,1)S(1)} %get-tuple-element.120), channel_id=1, source_target_pairs={{0,4},{8,0},{16,8},{24,16},{28,24},{20,28},{12,20},{4,12},{1,5},{9... | collective-permute-start | bytes 294920 | tf_op jit(solution)/shard_map/ppermute | solution.py:390
  42.3 4.7 %collective-permute-start.13 = (bf16[24,2048]{1,0:T(8,128)(2,1)S(1)}, bf16[24,2048]{1,0:T(8,128)(2,1)S(1)}, u32[]{:S(2)}, u32[]{:S(2)}) collective-permute-start(bf16[24,2048]{1,0:T(8,128)(2,1)S(1)} %slice.64), channel_id=1, source_target_pairs={{0,8},{8,16},{16,24},{24,28},{28,20},{20,12},{12,4},{4,0},{1,9},{9... | collective-permute-start | bytes 294920 | tf_op jit(solution)/shard_map/ppermute | solution.py:289
  42.7 4.7 %collective-permute-start.14 = (bf16[24,2048]{1,0:T(8,128)(2,1)S(1)}, bf16[24,2048]{1,0:T(8,128)(2,1)S(1)}, u32[]{:S(2)}, u32[]{:S(2)}) collective-permute-start(bf16[24,2048]{1,0:T(8,128)(2,1)S(1)} %slice.65), channel_id=1, source_target_pairs={{0,4},{8,0},{16,8},{24,16},{28,24},{20,28},{12,20},{4,12},{1,5},{9... | collective-permute-start | bytes 294920 | tf_op jit(solution)/shard_map/ppermute | solution.py:290
  47.3 5.8 %collective-permute-start.15 = (bf16[48,2048]{1,0:T(8,128)(2,1)S(1)}, bf16[48,2048]{1,0:T(8,128)(2,1)S(1)}, u32[]{:S(2)}, u32[]{:S(2)}) collective-permute-start(bf16[48,2048]{1,0:T(8,128)(2,1)S(1)} %get-tuple-element.86), channel_id=1, source_target_pairs={{0,8},{8,16},{16,24},{24,28},{28,20},{20,12},{12,4},{4,0},{1,9},{9... | collective-permute-start | bytes 589832 | tf_op jit(solution)/shard_map/ppermute | solution.py:406
  47.6 5.7 %collective-permute-start.16 = (bf16[48,2048]{1,0:T(8,128)(2,1)S(1)}, bf16[48,2048]{1,0:T(8,128)(2,1)S(1)}, u32[]{:S(2)}, u32[]{:S(2)}) collective-permute-start(bf16[48,2048]{1,0:T(8,128)(2,1)S(1)} %get-tuple-element.87), channel_id=1, source_target_pairs={{0,4},{8,0},{16,8},{24,16},{28,24},{20,28},{12,20},{4,12},{1,5},{9... | collective-permute-start | bytes 589832 | tf_op jit(solution)/shard_map/ppermute | solution.py:407
  53.4 16.2 %copy-start = (bf16[192,2048]{1,0:T(8,128)(2,1)S(1)}, bf16[192,2048]{1,0:T(8,128)(2,1)}, u32[]{:S(2)}) copy-start(bf16[192,2048]{1,0:T(8,128)(2,1)} %res_ref.1) | copy-start | bytes 2359300
  53.4 16.2 %copy-start.3 = (s32[48]{0:T(128)S(1)}, s32[48]{0:T(128)}, u32[]{:S(2)}) copy-start(s32[48]{0:T(128)} %param.17) | copy-start | bytes 580
  53.4 16.2 %copy-start.4 = (f32[48]{0:T(128)S(1)}, f32[48]{0:T(128)}, u32[]{:S(2)}) copy-start(f32[48]{0:T(128)} %param.16) | copy-start | bytes 580
  53.4 5.7 %collective-permute-start.17 = (bf16[48,2048]{1,0:T(8,128)(2,1)S(1)}, bf16[48,2048]{1,0:T(8,128)(2,1)S(1)}, u32[]{:S(2)}, u32[]{:S(2)}) collective-permute-start(bf16[48,2048]{1,0:T(8,128)(2,1)S(1)} %get-tuple-element.92), channel_id=1, source_target_pairs={{0,8},{8,16},{16,24},{24,28},{28,20},{20,12},{12,4},{4,0},{1,9},{9... | collective-permute-start | bytes 589832 | tf_op jit(solution)/shard_map/ppermute | solution.py:406
  53.6 5.7 %collective-permute-start.18 = (bf16[48,2048]{1,0:T(8,128)(2,1)S(1)}, bf16[48,2048]{1,0:T(8,128)(2,1)S(1)}, u32[]{:S(2)}, u32[]{:S(2)}) collective-permute-start(bf16[48,2048]{1,0:T(8,128)(2,1)S(1)} %get-tuple-element.93), channel_id=1, source_target_pairs={{0,4},{8,0},{16,8},{24,16},{28,24},{20,28},{12,20},{4,12},{1,5},{9... | collective-permute-start | bytes 589832 | tf_op jit(solution)/shard_map/ppermute | solution.py:407
  55.5 3.9 %collective-permute-start.19 = (bf16[96,1152]{1,0:T(8,128)(2,1)S(1)}, bf16[96,1152]{1,0:T(8,128)(2,1)S(1)}, u32[]{:S(2)}, u32[]{:S(2)}) collective-permute-start(bf16[96,1152]{1,0:T(8,128)(2,1)S(1)} %get-tuple-element.94), channel_id=1, source_target_pairs={{0,1},{1,0},{2,3},{3,2},{4,5},{5,4},{6,7},{7,6},{8,9},{9,8},{10,11... | collective-permute-start | bytes 663560 | tf_op jit(solution)/shard_map/ppermute | solution.py:362
  59.6 9.2 %collective-permute-start.22 = (bf16[96,1152]{1,0:T(8,128)(2,1)S(1)}, bf16[96,1152]{1,0:T(8,128)(2,1)S(1)}, u32[]{:S(2)}, u32[]{:S(2)}) collective-permute-start(bf16[96,1152]{1,0:T(8,128)(2,1)S(1)} %add.64.a_ref), channel_id=1, source_target_pairs={{0,2},{1,3},{2,0},{3,1},{4,6},{5,7},{6,4},{7,5},{8,10},{9,11},{10,... | collective-permute-start | bytes 663560 | tf_op jit(solution)/shard_map/ppermute | solution.py:369
  61.2 6.2 %collective-permute-start.20 = (bf16[48,2048]{1,0:T(8,128)(2,1)S(1)}, bf16[48,2048]{1,0:T(8,128)(2,1)S(1)}, u32[]{:S(2)}, u32[]{:S(2)}) collective-permute-start(bf16[48,2048]{1,0:T(8,128)(2,1)S(1)} %get-tuple-element.96), channel_id=1, source_target_pairs={{0,8},{8,16},{16,24},{24,28},{28,20},{20,12},{12,4},{4,0},{1,9},{9... | collective-permute-start | bytes 589832 | tf_op jit(solution)/shard_map/ppermute | solution.py:406
  62.6 6.2 %collective-permute-start.21 = (bf16[48,2048]{1,0:T(8,128)(2,1)S(1)}, bf16[48,2048]{1,0:T(8,128)(2,1)S(1)}, u32[]{:S(2)}, u32[]{:S(2)}) collective-permute-start(bf16[48,2048]{1,0:T(8,128)(2,1)S(1)} %get-tuple-element.97), channel_id=1, source_target_pairs={{0,4},{8,0},{16,8},{24,16},{28,24},{20,28},{12,20},{4,12},{1,5},{9... | collective-permute-start | bytes 589832 | tf_op jit(solution)/shard_map/ppermute | solution.py:407
  63.2 4.2 %collective-permute-start.23 = (f32[96,128]{1,0:T(8,128)S(1)}, f32[96,128]{1,0:T(8,128)S(1)}, u32[]{:S(2)}, u32[]{:S(2)}) collective-permute-start(f32[96,128]{1,0:T(8,128)S(1)} %get-tuple-element.100), channel_id=1, source_target_pairs={{0,4},{4,0},{8,12},{12,8},{16,20},{20,16},{24,28},{28,24},{1,5},{5... | collective-permute-start | bytes 147464 | tf_op jit(solution)/shard_map/ppermute | solution.py:377
  68.8 4.2 %collective-permute-start.25 = (f32[96,128]{1,0:T(8,128)S(1)}, f32[96,128]{1,0:T(8,128)S(1)}, u32[]{:S(2)}, u32[]{:S(2)}) collective-permute-start(f32[96,128]{1,0:T(8,128)S(1)} %add.40), channel_id=1, source_target_pairs={{0,8},{4,12},{8,0},{12,4},{16,24},{20,28},{24,16},{28,20},{1,9},{5... | collective-permute-start | bytes 147464 | tf_op jit(solution)/shard_map/ppermute | solution.py:377
  71.1 1.1 %collective-permute-start.27 = (f32[1,48]{1,0:T(1,128)S(1)}, f32[1,48]{1,0:T(1,128)S(1)}, u32[]{:S(2)}, u32[]{:S(2)}) collective-permute-start(f32[1,48]{1,0:T(1,128)S(1)} %get-tuple-element.114), channel_id=1, source_target_pairs={{0,1},{1,0},{2,3},{3,2},{4,5},{5,4},{6,7},{7,6},{8,9},{9,8},{10,11... | collective-permute-start | bytes 584 | tf_op jit(solution)/shard_map/ppermute | solution.py:435
  71.1 9.5 %collective-permute-start.24 = (bf16[96,1152]{1,0:T(8,128)(2,1)S(1)}, bf16[96,1152]{1,0:T(8,128)(2,1)S(1)}, u32[]{:S(2)}, u32[]{:S(2)}) collective-permute-start(bf16[96,1152]{1,0:T(8,128)(2,1)S(1)} %finish.1.a_ref), channel_id=1, source_target_pairs={{0,1},{1,0},{2,3},{3,2},{4,5},{5,4},{6,7},{7,6},{8,9},{9,8},{10,11... | collective-permute-start | bytes 663560 | tf_op jit(solution)/shard_map/ppermute | solution.py:371
  72.2 4.2 %collective-permute-start.28 = (f32[1,48]{1,0:T(1,128)S(1)}, f32[1,48]{1,0:T(1,128)S(1)}, u32[]{:S(2)}, u32[]{:S(2)}) collective-permute-start(f32[1,48]{1,0:T(1,128)S(1)} %add.43), channel_id=1, source_target_pairs={{0,2},{1,3},{2,0},{3,1},{4,6},{5,7},{6,4},{7,5},{8,10},{9,11},{10,... | collective-permute-start | bytes 584 | tf_op jit(solution)/shard_map/ppermute | solution.py:435
  72.9 6.3 %collective-permute-start.26 = (f32[96,128]{1,0:T(8,128)S(1)}, f32[96,128]{1,0:T(8,128)S(1)}, u32[]{:S(2)}, u32[]{:S(2)}) collective-permute-start(f32[96,128]{1,0:T(8,128)S(1)} %add.41), channel_id=1, source_target_pairs={{0,16},{4,20},{8,24},{12,28},{16,0},{20,4},{24,8},{28,12},{1,17},{... | collective-permute-start | bytes 147464 | tf_op jit(solution)/shard_map/ppermute | solution.py:377
  (3 other events, 29.5 us)

commit v3 on v2

--- a/solution.py
+++ b/solution.py
@@ -88,7 +88,8 @@
     return values[0]
 
 
-def dequant_kernel(first, codes_hbm, absmax_ref, weight_ref, token_ref, codes, sems):
+def dequant_kernel(first, codes_hbm, absmax_ref, *refs):
+    weight_ref, token_ref, codes, sems = refs[-4:]
     chunks, block, cols = codes.shape
     blocks = absmax_ref.shape[1]
     per = cols // blocks
@@ -152,7 +153,9 @@
         tokens, cols = residual.shape
         heads = all_heads // n
         rank = adapter_up.shape[0]
-        sub = heads // 2
+        shares = 4 if tp % 4 == 0 and heads % 512 == 0 else 2
+        sub = heads // shares
+        wsub = heads // 2
         slots = n * cap
         side = 2 * rank
         down_t = adapter_down.T
@@ -165,6 +168,9 @@
         def me():
             return lax.axis_index("seq"), lax.axis_index("tp") % 2
 
+        def share():
+            return lax.axis_index("tp") % shares
+
         def live_row(counts_ref):
             return lax.broadcasted_iota(I32, (1, cap), 1) < counts_ref[0]
 
@@ -176,7 +182,7 @@
         live_slots = slots // 2
 
         def prepare(counts_ref, selected_ref, gate_ref, attention_ref, cot_ref, send_ref, own_ref, grad_ref, up_ref, chosen, gates, cots, sems):
-            seq, core = me()
+            seq, _ = me()
             first = [
                 pltpu.make_async_copy(selected_ref, chosen, sems.at[0]),
                 pltpu.make_async_copy(gate_ref, gates, sems.at[1]),
@@ -185,7 +191,7 @@
             later = []
             for k in range(half):
                 for ref, flipped in ((send_ref, 1), (own_ref, 0)):
-                    at = pl.multiple_of((seq ^ (2 * k + flipped)) * heads + core * sub, 128)
+                    at = pl.multiple_of((seq ^ (2 * k + flipped)) * heads + share() * sub, 128)
                     sem = sems.at[3 + 2 * k + flipped]
                     later.append(pltpu.make_async_copy(attention_ref.at[:, pl.ds(at, sub)], ref.at[k], sem))
             for copy in first + later:
@@ -215,21 +221,21 @@
 
         across = lax.ppermute(send, "seq", flip(n, 1))
         going, coming = lax.ppermute(grad, "seq", ring(1)), lax.ppermute(grad, "seq", ring(-1))
-        block = min(64, sub)
-
-        def dequantize(part, absmax):
+        block = min(64, wsub)
+
+        def dequantize(part, *after):
             return call(
-                functools.partial(dequant_kernel, part * sub), [shape((sub, cols), BF), shape((8, 128), F32)],
-                in_hbm(quantized_codes), absmax,
-                in_specs=[hbm, vmem], flops=sub * cols * 100, name="dequantize",
+                functools.partial(dequant_kernel, part * wsub), [shape((wsub, cols), BF), shape((8, 128), F32)],
+                in_hbm(quantized_codes), absmax, *after,
+                in_specs=[hbm, vmem] + [vmem] * len(after), flops=wsub * cols * 100, name="dequantize",
                 scratch=[
-                    pltpu.VMEM((sub // block, block, cols), I32),
-                    pltpu.SemaphoreType.DMA((sub // block,)),
+                    pltpu.VMEM((wsub // block, block, cols), I32),
+                    pltpu.SemaphoreType.DMA((wsub // block,)),
                 ],
             )
 
-        weights, marks = zip(dequantize(0, absmax), dequantize(1, absmax))
-        across, going, coming, mark = lax.optimization_barrier((across, going, coming, marks[0]))
+        weight0, mark = dequantize(0)
+        across, going, coming, mark = lax.optimization_barrier((across, going, coming, mark))
 
         gathered = {0: (grad,)}
 
@@ -237,63 +243,87 @@
             gathered[n - step], gathered[step] = (going,), (coming,)
             return lax.ppermute(going, "seq", ring(1)), lax.ppermute(coming, "seq", ring(-1))
 
-        def pair(own_ref, across_ref, token_ref, *refs):
+        def pair(own_ref, across_ref, going_ref, coming_ref, token_ref, *refs):
+            *refs, going_out_ref, coming_out_ref, token_out_ref = refs
             for k, ref in enumerate(refs):
                 ref[0] = own_ref[k]
                 ref[1] = across_ref[k]
+            going_out_ref[...] = going_ref[...]
+            coming_out_ref[...] = coming_ref[...]
+            token_out_ref[...] = token_ref[...]
 
         def join(*refs):
             *refs, token_ref, out_ref = refs
             for k, ref in enumerate(refs):
                 out_ref[2 * k * cap : 2 * (k + 1) * cap, :] = ref[...].reshape(2 * cap, sub)
 
-        pairs = call(pair, [shape((2, cap, sub), BF)] * half, own, across, mark, name="pair")
+        *pairs, going, coming, mark = call(
+            pair, [shape((2, cap, sub), BF)] * half + [shape((cap, cols), BF)] * 2 + [shape((8, 128), F32)],
+            own, across, going, coming, mark, name="pair",
+        )
         fetched = [pairs[0]] + [lax.ppermute(pairs[k], "seq", flip(n, 2 * k)) for k in range(1, half)]
         going, coming = hop(1, going, coming)
-        fetched, going, coming, mark = lax.optimization_barrier((fetched, going, coming, marks[1]))
-        slots_own = call(join, [shape((slots, sub), BF)], *fetched, mark, name="join")[0]
-        slots_other = lax.ppermute(slots_own, "tp", flip(tp, 1))
+        mid = cap // 2
+        mid = cap // 2
+        weight1, mark = dequantize(1, mark)
+        weights = weight0, weight1
+        fetched, going, coming, mark = lax.optimization_barrier((fetched, going, coming, mark))
+        pieces = list(call(join, [shape((slots, sub), BF)], *fetched, mark, name="join"))
         for step in range(2, half - 1):
             going, coming = hop(step, going, coming)
-        mid = cap // 2
-
-        def forward(own_ref, other_ref, down_ref, up_ref, w0_ref, w1_ref, out_ref, low_ref):
-            seq, core = me()
-            a, b = own_ref[...], other_ref[...]
-            att = jnp.concatenate([jnp.where(core == 0, a, b), jnp.where(core == 0, b, a)], axis=1)
+        if shares == 4:
+            pieces.append(lax.ppermute(pieces[0], "tp", flip(tp, 2)))
+        pieces, going, coming = lax.optimization_barrier((pieces, going, coming))
+        others = [lax.ppermute(piece, "tp", flip(tp, 1)) for piece in pieces]
+        pieces = [pieces[0], others[0]] + ([pieces[1], others[1]] if shares == 4 else [])
+        gathered[n - half + 1], gathered[half - 1] = (going,), (coming,)
+        gathered[half] = (
+            lax.ppermute(going[:mid], "seq", ring(1)),
+            lax.ppermute(coming[mid:], "seq", ring(-1)),
+        )
+
+        def natural(refs):
+            parts = [ref[...] for ref in refs]
+            for bit in (1, 2)[: shares // 2]:
+                unset = share() // bit % 2 == 0
+                parts = [jnp.where(unset, parts[k], parts[k ^ bit]) for k in range(shares)]
+            return jnp.concatenate(parts, axis=1)
+
+        def forward(down_ref, up_ref, w0_ref, w1_ref, *refs):
+            piece_refs, (out_ref, low_ref, every) = refs[:shares], refs[shares:]
+            seq, _ = me()
+            att = natural(piece_refs)
             low = dot(att, down_ref[...], 1, 1)
             thrice = jnp.concatenate(split3(adapter_scale * low), axis=1)
             for j in range(n):
-                low_ref[seq ^ j] = low[j * cap : (j + 1) * cap]
+                every[seq ^ j] = low[j * cap : (j + 1) * cap]
+            top, bottom = every[:half].reshape(live_slots, rank), every[half:].reshape(live_slots, rank)
+            low_ref[...] = jnp.concatenate([top, bottom], axis=1)
             spots = [lax.rem(place(seq ^ j) - place(seq) + n, n) for j in range(n)]
             tile = min(512, cols)
             for c in range(cols // tile):
                 part = slice(c * tile, (c + 1) * tile)
                 ups = up_ref[:, part]
                 acc = dot(thrice, jnp.concatenate([ups] * 3, axis=0))
-                acc = acc + dot(att[:, :sub], w0_ref[:, part]) + dot(att[:, sub:], w1_ref[:, part])
+                acc = acc + dot(att[:, :wsub], w0_ref[:, part]) + dot(att[:, wsub:], w1_ref[:, part])
                 acc = acc.astype(BF)
                 for j in range(n):
                     out_ref[spots[j], :, part] = acc[j * cap : (j + 1) * cap]
 
         partial, low = call(
             forward,
-            [shape((n, cap, cols), BF), shape((n, cap, rank), F32)],
-            slots_own, slots_other, down_t, adapter_up, *weights,
-            flops=2 * slots * heads * cols, name="forward",
-        )
-
-        going, coming, partial = lax.optimization_barrier((going, coming, partial))
-        gathered[n - half + 1], gathered[half - 1] = (going,), (coming,)
-        gathered[half] = (
-            lax.ppermute(going[:mid], "seq", ring(1)),
-            lax.ppermute(coming[mid:], "seq", ring(-1)),
-        )
-
+            [shape((n, cap, cols), BF), shape((live_slots, side), F32)],
+            down_t, adapter_up, *weights, *pieces,
+            flops=2 * slots * heads * cols, name="forward", scratch=[pltpu.VMEM((n, cap, rank), F32)],
+        )
+
+        here, there = partial[half, :mid], partial[half, mid:]
+        first_step = lax.ppermute(here, "seq", ring(1)), lax.ppermute(there, "seq", ring(-1))
+        low_across = lax.ppermute(low, "seq", flip(n, 1))
         spots = [r for r in range(n) if r != half]
 
-        def backward(low_ref, up_ref, w0_ref, w1_ref, first_ref, second_ref, *refs):
-            g_refs, (keep_ref, send_ref, live_ref, where_ref, low_out_ref, every, sums) = refs[: n - 1], refs[n - 1 :]
+        def backward(up_ref, w0_ref, w1_ref, first_ref, second_ref, *refs):
+            g_refs, (keep_ref, send_ref, live_ref, where_ref, every, sums) = refs[: n - 1], refs[n - 1 :]
             seq, core = me()
             for r, ref in zip(spots, g_refs):
                 every[shard_at(place(seq) + r)] = ref[...]
@@ -308,17 +338,21 @@
                 passed = passed + jnp.sum(alive, axis=0, keepdims=True)
             g = dot(where_ref[...], every[...].reshape(slots, cols), 0, 0).astype(BF)
             live_ref[...] = g
-            tile = min(256, sub)
-            for i in range(sub // tile):
-                for at, ref in ((0, w0_ref), (sub, w1_ref)):
+            tile = min(256, wsub)
+            for i in range(wsub // tile):
+                for at, ref in ((0, w0_ref), (wsub, w1_ref)):
                     sums[:, at + i * tile : at + (i + 1) * tile] = dot(g, ref[i * tile : (i + 1) * tile, :], 1, 1)
-            low = dot(where_ref[...], jnp.concatenate(split3(low_ref[...].reshape(slots, rank)), axis=1), 0, 0)
-            low = low[:, :rank] + low[:, rank : 2 * rank] + low[:, 2 * rank :]
-            low_out_ref[...] = jnp.concatenate([low[:some], low[some:]], axis=1)
             hi, lo = split2(adapter_scale * dot(g, up_ref[...], 1, 1))
             sums[:, heads:] = jnp.concatenate([hi, lo], axis=1).astype(F32)
             keep_ref[...] = sums[pl.ds(pl.multiple_of(core * some, 8), some), :]
             send_ref[...] = sums[pl.ds(pl.multiple_of((1 - core) * some, 8), some), :].astype(BF)
+
+        def compact(low_ref, low_across_ref, where_ref, out_ref):
+            low = low_ref[...] + low_across_ref[...]
+            low = jnp.concatenate([low[:, :rank], low[:, rank:]], axis=0)
+            low = dot(where_ref[...], jnp.concatenate(split3(low), axis=1), 0, 0)
+            low = low[:, :rank] + low[:, rank : 2 * rank] + low[:, 2 * rank :]
+            out_ref[...] = jnp.concatenate([low[: live_slots // 2], low[live_slots // 2 :]], axis=1)
 
         wide = heads + side
 
@@ -330,9 +364,8 @@
                     shape((some, wide), BF),
                     shape((live_slots, cols), BF),
                     shape((slots, live_slots), BF),
-                    shape((some, side), F32),
                 ],
-                low, adapter_up, *weights, *farthest, *[gathered[r][0] for r in spots],
+                adapter_up, *weights, *farthest, *[gathered[r][0] for r in spots],
                 flops=2 * live_slots * heads * cols,
                 scratch=[pltpu.VMEM((n, cap, cols), BF), pltpu.VMEM((live_slots, wide), F32)],
                 name="backward",
@@ -372,11 +405,11 @@
             return done, other_done
 
         def sum_low(total):
-            bit = 1
-            while bit < n:
+            bit = half
+            while bit > 1:
                 recv = yield lax.ppermute(total, "seq", flip(n, bit))
                 total = total + recv
-                bit *= 2
+                bit //= 2
             return total
 
         def drain(steps, value):
@@ -386,32 +419,32 @@
             except StopIteration as stop:
                 return stop.value
 
-        here, there = partial[half, :mid], partial[half, mid:]
-        going, coming = lax.ppermute(here, "seq", ring(1)), lax.ppermute(there, "seq", ring(-1))
+        going, coming = first_step
         for step in range(half - 1, 0, -1):
             here, there = partial[step], partial[n - step]
             if step == half - 1:
                 here = jnp.concatenate([plus(here[:mid], going), here[mid:]])
                 there = jnp.concatenate([there[:mid], plus(there[mid:], coming)])
+                keep, send, grad_live, where_live = back(*gathered[half])
+                here, there, send = lax.optimization_barrier((here, there, send))
             else:
                 here, there = plus(here, going), plus(there, coming)
-            if step == half - 1:
-                here, there, *farthest = lax.optimization_barrier((here, there, *gathered[half]))
-                keep, send, grad_live, where_live, low_live = back(*farthest)
-            elif step == half - 2:
-                here, there, send = lax.optimization_barrier((here, there, send))
-                head_steps, head_value = sum_heads(keep, send), None
-            else:
-                here, there, head_value, low_live = lax.optimization_barrier((here, there, head_value, low_live))
+                if step == half - 2:
+                    here, there, head_value, low_across = lax.optimization_barrier((here, there, head_value, low_across))
+                else:
+                    here, there = lax.optimization_barrier((here, there))
             going = lax.ppermute(here, "seq", ring(1))
             coming = lax.ppermute(there, "seq", ring(-1))
-            if half - 4 < step < half - 1:
+            if step == half - 1:
+                head_steps, head_value = sum_heads(keep, send), None
+            elif step == half - 2:
+                low_live = call(compact, [shape((some, side), F32)], low, low_across, where_live, name="compact")[0]
+                low_steps, low_value = sum_low(low_live), None
+                low_value = low_steps.send(None)
+            if step >= half - 2:
                 head_value = head_steps.send(head_value)
-        low_steps = sum_low(low_live)
-        low_value = low_steps.send(None)
-        going, coming, head_value, low_value = lax.optimization_barrier((going, coming, head_value, low_value))
         done, other_done = drain(head_steps, head_value)
-        going, coming, done = lax.optimization_barrier((going, coming, done))
+        going, coming, other_done, low_value = lax.optimization_barrier((going, coming, other_done, low_value))
         low_sum = drain(low_steps, low_value)
 
         def home(counts_ref, selected_ref, gate_ref, res_ref, own_ref, going_ref, coming_ref, up_ref, out_ref, gate_out_ref):
@@ -435,7 +468,8 @@
             gate_part = gate_part + lax.ppermute(gate_part, "tp", flip(tp, bit))
             bit *= 2
 
-        def last(a_ref, b_ref, where_ref, own_ref, other_ref, grad_ref, down_grad_ref, live, rank_ref):
+        def last(a_ref, b_ref, where_ref, *refs):
+            piece_refs, (grad_ref, down_grad_ref, live, rank_ref) = refs[:shares], refs[shares:]
             seq, core = me()
             for ref, at in ((a_ref, core), (b_ref, 1 - core)):
                 live[pl.ds(pl.multiple_of(at * some, 16), some), :] = ref[...]
@@ -444,13 +478,14 @@
             for j in range(n):
                 rank_ref[j] = every[j * cap : (j + 1) * cap, heads:]
             rank_grad = jnp.concatenate([rank_ref[seq ^ j] for j in range(n)], axis=0)[:, :rank]
-            for ref, at in ((own_ref, core), (other_ref, 1 - core)):
-                down_grad_ref[:, pl.ds(pl.multiple_of(at * sub, 128), sub)] = dot(rank_grad, ref[...], 0, 0)
+            for j, ref in enumerate(piece_refs):
+                at = pl.multiple_of((share() ^ j) * sub, 128)
+                down_grad_ref[:, pl.ds(at, sub)] = dot(rank_grad, ref[...], 0, 0)
 
         attention_output_grad, down_gradient = call(
             last,
             [shape((slots, heads), BF), shape((rank, heads), F32)],
-            done, other_done, where_live, slots_own, slots_other,
+            done, other_done, where_live, *pieces,
             scratch=[pltpu.VMEM((live_slots, wide), BF), pltpu.VMEM((n, cap, side), BF)], name="last",
         )
 

time: 82.3 us -> 77.3 us (0.939)
  waiting for transfers between devices: 23.7 us -> 19.4 us
  starting transfers between devices: 33.6 us -> 32.5 us
    ppermute x3 -> x2, waiting for transfers between devices: 4.88 us -> 0.01 us  [sum_low(): recv = (yield lax.ppermute(total, 'seq', flip(n, bit)))]
    ppermute x3, waiting for transfers between devices: 3.52 us -> 0.01 us  [body(): lax.ppermute(pairs[k], 'seq', flip(n, 2 * k))]
    ppermute x1 -> x4, waiting for transfers between devices: 0.01 us -> 3.08 us  [the longest x1 2.12 us: body(): pieces.append(lax.ppermute(pieces[0], 'tp', flip(tp, 2)))]
    ppermute x1, starting transfers between devices: 0.01 us -> 2.99 us  [body(): lax.ppermute(grad, 'seq', ring(-1))]
    ppermute x1, starting transfers between devices: 3.08 us -> 0.15 us  [body(): lax.ppermute(grad, 'seq', ring(1))]
    ppermute x1 -> x4, starting transfers between devices: 0.07 us -> 2.88 us  [the longest x1 1.59 us: body(): pieces.append(lax.ppermute(pieces[0], 'tp', flip(tp, 2)))]
    ppermute x3, waiting for transfers between devices: 1.68 us -> 4.25 us  [body(): coming = lax.ppermute(there, 'seq', ring(-1))]
    ppermute x1, waiting for transfers between devices: 0.01 us -> 2.35 us  [sum_heads(): recv = (yield lax.ppermute(mine, 'tp', flip(tp, bit)))]
  transfers between devices with their start and end apart: 29 -> 31, of which waited for: 18 -> 12; matrix products, arithmetic and copies ran while one was open for 1% -> 1% of each run, Pallas kernels for 23% -> 24%
where the time goes in v3:
time: 77.3 us; the launch traced here: 77.2 us
  starting transfers between devices  32.5 us (42%)
  Pallas kernels  22.6 us (29%)
  waiting for transfers between devices  19.4 us (25%)
  between operations  1.55 us (2%)
  other arithmetic  0.8 us (1%)
    pallas_call x13, Pallas kernels, call(): pl.pallas_call(kernel, out_shape=tuple(outs), in_specs=in_specs or [whole...  22.6 us
    ppermute x2, starting transfers between devices, sum_low(): recv = (yield lax.ppermute(total, 'seq', flip(n, bit)))  4.59 us
    ppermute x3, starting transfers between devices, body(): lax.ppermute(pairs[k], 'seq', flip(n, 2 * k))  4.39 us
    ppermute x3, waiting for transfers between devices, body(): coming = lax.ppermute(there, 'seq', ring(-1))  4.25 us
    ppermute x3, waiting for transfers between devices, body(): going = lax.ppermute(here, 'seq', ring(1))  4.11 us
    ppermute x2, starting transfers between devices, hop(): lax.ppermute(coming, 'seq', ring(-1))  3.35 us
    ppermute x3, starting transfers between devices, body(): coming = lax.ppermute(there, 'seq', ring(-1))  3.35 us
    ppermute x1, starting transfers between devices, body(): lax.ppermute(grad, 'seq', ring(-1))  2.99 us
  transfers between devices with their start and end apart: 31, of which 12 were waited for; matrix products, arithmetic and copies ran while one was open for 1% of the time, Pallas kernels for 24%

profile of v3, /device:TPU:0, one launch (start us, length us, event | category | flops | bytes accessed | tf_op | source)
XLA Modules:
  0.0 77.2 jit_solution(9359527826794831462)
XLA Ops:
  1.3 1.6 %prepare.1 = (bf16[4,48,256]{2,1,0:T(8,128)(2,1)S(1)}, bf16[4,48,256]{2,1,0:T(8,128)(2,1)S(1)}, bf16[48,2048]{1,0:T(8,128)(2,1)S(1)}, bf16[48,2048]{1,0:T(8,128)(2,1)S(1)}) custom-call(s32[1]{0:T(128)S(6)} %copy.17.counts_ref, s32[1,48]{1,0:T(1,128)} %bitcast.36, f32[1,48]{1,0:T(1,128)} %bitcast.38, bf16[48,8192]{1,0:T(8,128)(2,1)} %attention_ref.1, ...), custom_call_target="tpu_custom_call" | custom-call | bytes 2163076 | tf_op jit(solution)/shard_map/prepare/pallas_call | solution.py:55
  2.9 3.0 %collective-permute-start.2 = (bf16[48,2048]{1,0:T(8,128)(2,1)S(1)}, bf16[48,2048]{1,0:T(8,128)(2,1)S(1)}, u32[]{:S(2)}, u32[]{:S(2)}) collective-permute-start(bf16[48,2048]{1,0:T(8,128)(2,1)S(1)} %get-tuple-element.61.refs_0_), channel_id=1, source_target_pairs={{0,4},{8,0},{16,8},{24,16},{28,24},{20,28},{12,20},{4,12},{1,5},{9... | collective-permute-start | bytes 589832 | tf_op jit(solution)/shard_map/ppermute | solution.py:223
  6.0 1.9 %collective-permute-start = (bf16[4,48,256]{2,1,0:T(8,128)(2,1)S(1)}, bf16[4,48,256]{2,1,0:T(8,128)(2,1)S(1)}, u32[]{:S(2)}, u32[]{:S(2)}) collective-permute-start(bf16[4,48,256]{2,1,0:T(8,128)(2,1)S(1)} %get-tuple-element.60), channel_id=1, source_target_pairs={{0,4},{4,0},{8,12},{12,8},{16,20},{20,16},{24,28},{28,24},{1,5},{5... | collective-permute-start | bytes 294920 | tf_op jit(solution)/shard_map/ppermute | solution.py:222
  8.1 5.3 %dequantize.2 = (bf16[512,2048]{1,0:T(8,128)(2,1)S(1)}, f32[8,128]{1,0:T(8,128)S(1)}) custom-call(s32[1024,2048]{1,0:T(8,128)} %codes_hbm.3, f32[1024,32]{1,0:T(8,128)S(1)} %copy.15.absmax_ref), custom_call_target="tpu_custom_call" | custom-call | flops 104857600 | bytes 10620928 | tf_op jit(solution)/shard_map/dequantize/pallas_call | solution.py:55
  13.5 0.9 %collective-permute-done.across_ref = bf16[4,48,256]{2,1,0:T(8,128)(2,1)S(1)} collective-permute-done((bf16[4,48,256]{2,1,0:T(8,128)(2,1)S(1)}, bf16[4,48,256]{2,1,0:T(8,128)(2,1)S(1)}, u32[]{:S(2)}, u32[]{:S(2)}) %collective-permute-start) | collective-permute-done | bytes 98336 | tf_op jit(solution)/shard_map/ppermute | solution.py:222
  15.2 1.3 %collective-permute-start.7 = (bf16[48,2048]{1,0:T(8,128)(2,1)S(1)}, bf16[48,2048]{1,0:T(8,128)(2,1)S(1)}, u32[]{:S(2)}, u32[]{:S(2)}) collective-permute-start(bf16[48,2048]{1,0:T(8,128)(2,1)S(1)} %get-tuple-element.74.refs_1_), channel_id=1, source_target_pairs={{0,4},{8,0},{16,8},{24,16},{28,24},{20,28},{12,20},{4,12},{1,5},{9... | collective-permute-start | bytes 589832 | tf_op jit(solution)/shard_map/ppermute | solution.py:244
  17.2 2.6 %collective-permute-start.4 = (bf16[2,48,256]{2,1,0:T(8,128)(2,1)S(1)}, bf16[2,48,256]{2,1,0:T(8,128)(2,1)S(1)}, u32[]{:S(2)}, u32[]{:S(2)}) collective-permute-start(bf16[2,48,256]{2,1,0:T(8,128)(2,1)S(1)} %get-tuple-element.71), channel_id=1, source_target_pairs={{0,16},{4,20},{8,24},{12,28},{16,0},{20,4},{24,8},{28,12},{1,17},{... | collective-permute-start | bytes 147464 | tf_op jit(solution)/shard_map/ppermute | solution.py:264
  19.8 1.1 %collective-permute-start.5 = (bf16[2,48,256]{2,1,0:T(8,128)(2,1)S(1)}, bf16[2,48,256]{2,1,0:T(8,128)(2,1)S(1)}, u32[]{:S(2)}, u32[]{:S(2)}) collective-permute-start(bf16[2,48,256]{2,1,0:T(8,128)(2,1)S(1)} %get-tuple-element.72), channel_id=1, source_target_pairs={{0,24},{4,28},{8,16},{12,20},{16,8},{20,12},{24,0},{28,4},{1,25},{... | collective-permute-start | bytes 147464 | tf_op jit(solution)/shard_map/ppermute | solution.py:264
  20.9 5.4 %dequantize.3 = (bf16[512,2048]{1,0:T(8,128)(2,1)S(1)}, f32[8,128]{1,0:T(8,128)S(1)}) custom-call(s32[1024,2048]{1,0:T(8,128)} %codes_hbm.3, f32[1024,32]{1,0:T(8,128)S(1)} %copy.15.absmax_ref, f32[8,128]{1,0:T(8,128)S(1)} %get-tuple-element.67.refs_0_), custom_call_target="tpu_custom_call" | custom-call | flops 104857600 | bytes 10625024 | tf_op jit(solution)/shard_map/dequantize/pallas_call | solution.py:55
  26.3 1.6 %collective-permute-start.8 = (bf16[384,256]{1,0:T(8,128)(2,1)S(1)}, bf16[384,256]{1,0:T(8,128)(2,1)S(1)}, u32[]{:S(2)}, u32[]{:S(2)}) collective-permute-start(bf16[384,256]{1,0:T(8,128)(2,1)S(1)} %join.1.refs_0_), channel_id=1, source_target_pairs={{0,2},{1,3},{2,0},{3,1},{4,6},{5,7},{6,4},{7,5},{8,10},{9,11},{10,... | collective-permute-start | bytes 589832 | tf_op jit(solution)/shard_map/ppermute | solution.py:275
  27.9 2.0 %collective-permute-start.10 = (bf16[48,2048]{1,0:T(8,128)(2,1)S(1)}, bf16[48,2048]{1,0:T(8,128)(2,1)S(1)}, u32[]{:S(2)}, u32[]{:S(2)}) collective-permute-start(bf16[48,2048]{1,0:T(8,128)(2,1)S(1)} %collective-permute-done.7.refs_2_), channel_id=1, source_target_pairs={{0,4},{8,0},{16,8},{24,16},{28,24},{20,28},{12,20},{4,12},{1,5},{9... | collective-permute-start | bytes 589832 | tf_op jit(solution)/shard_map/ppermute | solution.py:244
  30.0 2.1 %collective-permute-done.8.refs_2_ = bf16[384,256]{1,0:T(8,128)(2,1)S(1)} collective-permute-done((bf16[384,256]{1,0:T(8,128)(2,1)S(1)}, bf16[384,256]{1,0:T(8,128)(2,1)S(1)}, u32[]{:S(2)}, u32[]{:S(2)}) %collective-permute-start.8) | collective-permute-done | bytes 196640 | tf_op jit(solution)/shard_map/ppermute | solution.py:275
  32.1 1.5 %collective-permute-done.9.refs_4_ = bf16[48,2048]{1,0:T(8,128)(2,1)S(1)} collective-permute-done((bf16[48,2048]{1,0:T(8,128)(2,1)S(1)}, bf16[48,2048]{1,0:T(8,128)(2,1)S(1)}, u32[]{:S(2)}, u32[]{:S(2)}) %collective-permute-start.9) | collective-permute-done | bytes 196640 | tf_op jit(solution)/shard_map/ppermute | solution.py:244
  34.1 2.1 %collective-permute-start.16 = (bf16[24,2048]{1,0:T(8,128)(2,1)S(1)}, bf16[24,2048]{1,0:T(8,128)(2,1)S(1)}, u32[]{:S(2)}, u32[]{:S(2)}) collective-permute-start(bf16[24,2048]{1,0:T(8,128)(2,1)S(1)} %slice.65), channel_id=1, source_target_pairs={{0,4},{8,0},{16,8},{24,16},{28,24},{20,28},{12,20},{4,12},{1,5},{9... | collective-permute-start | bytes 294920 | tf_op jit(solution)/shard_map/ppermute | solution.py:282
  36.2 2.5 %forward.1 = (bf16[8,48,2048]{2,1,0:T(8,128)(2,1)S(1)}, f32[192,128]{1,0:T(8,128)S(1)}) custom-call(bf16[64,1024]{1,0:T(8,128)(2,1)S(1)} %bitcast.34, bf16[64,2048]{1,0:T(8,128)(2,1)S(1)} %copy-done.1, bf16[512,2048]{1,0:T(8,128)(2,1)S(1)} %get-tuple-element.58.w0_ref, bf16[512,2048]{1,0:T(8,128)(2,1)S(1)} %get-tuple-element.68.w1_ref, ...), custom_call_target="tpu_custom_call" | custom-call | flops 1610612736 | bytes 7045120 | tf_op jit(solution)/shard_map/forward/pallas_call | solution.py:55
  38.8 2.1 %collective-permute-start.14 = (bf16[24,2048]{1,0:T(8,128)(2,1)S(1)}, bf16[24,2048]{1,0:T(8,128)(2,1)S(1)}, u32[]{:S(2)}, u32[]{:S(2)}) collective-permute-start(bf16[24,2048]{1,0:T(8,128)(2,1)S(1)} %get-tuple-element.116), channel_id=1, source_target_pairs={{0,4},{8,0},{16,8},{24,16},{28,24},{20,28},{12,20},{4,12},{1,5},{9... | collective-permute-start | bytes 294920 | tf_op jit(solution)/shard_map/ppermute | solution.py:321
  40.9 2.5 %backward.1 = (f32[96,1152]{1,0:T(8,128)S(1)}, bf16[96,1152]{1,0:T(8,128)(2,1)S(1)}, bf16[192,2048]{1,0:T(8,128)(2,1)S(1)}, bf16[384,192]{1,0:T(8,128)(2,1)S(1)}) custom-call(bf16[64,2048]{1,0:T(8,128)(2,1)S(1)} %copy-done.1, bf16[512,2048]{1,0:T(8,128)(2,1)S(1)} %get-tuple-element.58.w0_ref, bf16[512,2048]{1,0:T(8,128)(2,1)S(1)} %get-tuple-element.68.w1_ref, ...), custom_call_target="tpu_custom_call" | custom-call | flops 805306368 | bytes 7626752 | tf_op jit(solution)/shard_map/backward/pallas_call | solution.py:55
  43.4 2.0 %collective-permute-done.13 = bf16[24,2048]{1,0:T(8,128)(2,1)S(1)} collective-permute-done((bf16[24,2048]{1,0:T(8,128)(2,1)S(1)}, bf16[24,2048]{1,0:T(8,128)(2,1)S(1)}, u32[]{:S(2)}, u32[]{:S(2)}) %collective-permute-start.13) | collective-permute-done | bytes 98336 | tf_op jit(solution)/shard_map/ppermute | solution.py:321
  45.6 2.0 %collective-permute-start.18 = (bf16[48,2048]{1,0:T(8,128)(2,1)S(1)}, bf16[48,2048]{1,0:T(8,128)(2,1)S(1)}, u32[]{:S(2)}, u32[]{:S(2)}) collective-permute-start(bf16[48,2048]{1,0:T(8,128)(2,1)S(1)} %get-tuple-element.90), channel_id=1, source_target_pairs={{0,4},{8,0},{16,8},{24,16},{28,24},{20,28},{12,20},{4,12},{1,5},{9... | collective-permute-start | bytes 589832 | tf_op jit(solution)/shard_map/ppermute | solution.py:437
  48.4 3.2 %collective-permute-done.17 = bf16[48,2048]{1,0:T(8,128)(2,1)S(1)} collective-permute-done((bf16[48,2048]{1,0:T(8,128)(2,1)S(1)}, bf16[48,2048]{1,0:T(8,128)(2,1)S(1)}, u32[]{:S(2)}, u32[]{:S(2)}) %collective-permute-start.17) | collective-permute-done | bytes 196640 | tf_op jit(solution)/shard_map/ppermute | solution.py:436
  51.7 1.0 %collective-permute-done.20.low_across_ref = f32[192,128]{1,0:T(8,128)S(1)} collective-permute-done((f32[192,128]{1,0:T(8,128)S(1)}, f32[192,128]{1,0:T(8,128)S(1)}, u32[]{:S(2)}, u32[]{:S(2)}) %collective-permute-start.20) | collective-permute-done | bytes 98336 | tf_op jit(solution)/shard_map/ppermute | solution.py:322
  53.3 1.3 %collective-permute-start.22 = (bf16[48,2048]{1,0:T(8,128)(2,1)S(1)}, bf16[48,2048]{1,0:T(8,128)(2,1)S(1)}, u32[]{:S(2)}, u32[]{:S(2)}) collective-permute-start(bf16[48,2048]{1,0:T(8,128)(2,1)S(1)} %get-tuple-element.94), channel_id=1, source_target_pairs={{0,4},{8,0},{16,8},{24,16},{28,24},{20,28},{12,20},{4,12},{1,5},{9... | collective-permute-start | bytes 589832 | tf_op jit(solution)/shard_map/ppermute | solution.py:437
  55.1 2.6 %collective-permute-start.27 = (f32[96,128]{1,0:T(8,128)S(1)}, f32[96,128]{1,0:T(8,128)S(1)}, u32[]{:S(2)}, u32[]{:S(2)}) collective-permute-start(f32[96,128]{1,0:T(8,128)S(1)} %compact.1), channel_id=1, source_target_pairs={{0,16},{4,20},{8,24},{12,28},{16,0},{20,4},{24,8},{28,12},{1,17},{... | collective-permute-start | bytes 147464 | tf_op jit(solution)/shard_map/ppermute | solution.py:410
  59.4 2.1 %collective-permute-start.23 = (bf16[48,2048]{1,0:T(8,128)(2,1)S(1)}, bf16[48,2048]{1,0:T(8,128)(2,1)S(1)}, u32[]{:S(2)}, u32[]{:S(2)}) collective-permute-start(bf16[48,2048]{1,0:T(8,128)(2,1)S(1)} %get-tuple-element.95), channel_id=1, source_target_pairs={{0,8},{8,16},{16,24},{24,28},{28,20},{20,12},{12,4},{4,0},{1,9},{9... | collective-permute-start | bytes 589832 | tf_op jit(solution)/shard_map/ppermute | solution.py:436
  61.5 2.3 %collective-permute-done.25.b_ref = bf16[96,1152]{1,0:T(8,128)(2,1)S(1)} collective-permute-done((bf16[96,1152]{1,0:T(8,128)(2,1)S(1)}, bf16[96,1152]{1,0:T(8,128)(2,1)S(1)}, u32[]{:S(2)}, u32[]{:S(2)}) %collective-permute-start.25) | collective-permute-done | bytes 221216 | tf_op jit(solution)/shard_map/ppermute | solution.py:402
  64.2 0.9 %collective-permute-done.23.going_ref = bf16[48,2048]{1,0:T(8,128)(2,1)S(1)} collective-permute-done((bf16[48,2048]{1,0:T(8,128)(2,1)S(1)}, bf16[48,2048]{1,0:T(8,128)(2,1)S(1)}, u32[]{:S(2)}, u32[]{:S(2)}) %collective-permute-start.23) | collective-permute-done | bytes 196640 | tf_op jit(solution)/shard_map/ppermute | solution.py:436
  65.1 3.5 %collective-permute-done.24.coming_ref = bf16[48,2048]{1,0:T(8,128)(2,1)S(1)} collective-permute-done((bf16[48,2048]{1,0:T(8,128)(2,1)S(1)}, bf16[48,2048]{1,0:T(8,128)(2,1)S(1)}, u32[]{:S(2)}, u32[]{:S(2)}) %collective-permute-start.24) | collective-permute-done | bytes 196640 | tf_op jit(solution)/shard_map/ppermute | solution.py:437
  68.6 1.5 %home.1 = (bf16[192,2048]{1,0:T(8,128)(2,1)}, f32[1,48]{1,0:T(1,128)S(1)}) custom-call(s32[1]{0:T(128)S(6)} %copy.17.counts_ref, s32[1,48]{1,0:T(1,128)S(1)} %bitcast.37, f32[1,48]{1,0:T(1,128)S(1)} %bitcast.39, bf16[192,2048]{1,0:T(8,128)(2,1)S(1)} %copy-done, bf16[48,2048]{1,0:T(8,128)(2,1)S(1)} %slice_bitcast_fusion.own_ref, ...), custom_call_target="tpu_custom_call" | custom-call | bytes 2359876 | tf_op jit(solution)/shard_map/home/pallas_call | solution.py:55
  70.1 1.1 %collective-permute-done.29 = f32[1,48]{1,0:T(1,128)S(1)} collective-permute-done((f32[1,48]{1,0:T(1,128)S(1)}, f32[1,48]{1,0:T(1,128)S(1)}, u32[]{:S(2)}, u32[]{:S(2)}) %collective-permute-start.29) | collective-permute-done | bytes 224 | tf_op jit(solution)/shard_map/ppermute | solution.py:468
  71.7 2.0 %collective-permute-start.28 = (f32[96,128]{1,0:T(8,128)S(1)}, f32[96,128]{1,0:T(8,128)S(1)}, u32[]{:S(2)}, u32[]{:S(2)}) collective-permute-start(f32[96,128]{1,0:T(8,128)S(1)} %add.37), channel_id=1, source_target_pairs={{0,8},{4,12},{8,0},{12,4},{16,24},{20,28},{24,16},{28,20},{1,9},{5... | collective-permute-start | bytes 147464 | tf_op jit(solution)/shard_map/ppermute | solution.py:410
  73.7 1.6 %last.1 = (bf16[384,1024]{1,0:T(8,128)(2,1)}, f32[64,1024]{1,0:T(8,128)}) custom-call(bf16[96,1152]{1,0:T(8,128)(2,1)S(1)} %finish.1.a_ref, bf16[96,1152]{1,0:T(8,128)(2,1)S(1)} %collective-permute-done.26.b_ref, bf16[384,192]{1,0:T(8,128)(2,1)S(1)} %get-tuple-element.100.where_ref, bf16[384,256]{1,0:T(8,128)(2,1)S(1)} %join.1.refs_0_, ...), custom_call_target="tpu_custom_call" | custom-call | bytes 2424832 | tf_op jit(solution)/shard_map/last/pallas_call | solution.py:55
  75.8 1.3 %up_gradient.1 = f32[64,2048]{1,0:T(8,128)} custom-call(f32[96,128]{1,0:T(8,128)S(1)} %add.38.low_ref, bf16[192,2048]{1,0:T(8,128)(2,1)S(1)} %get-tuple-element.109.g_ref), custom_call_target="tpu_custom_call" | custom-call | flops 150994944 | bytes 1359872 | tf_op jit(solution)/shard_map/up_gradient/pallas_call | solution.py:55
  (68 shorter events, 7.8 us)
Async XLA Ops:
  2.9 11.5 %collective-permute-start.2 = (bf16[48,2048]{1,0:T(8,128)(2,1)S(1)}, bf16[48,2048]{1,0:T(8,128)(2,1)S(1)}, u32[]{:S(2)}, u32[]{:S(2)}) collective-permute-start(bf16[48,2048]{1,0:T(8,128)(2,1)S(1)} %get-tuple-element.61.refs_0_), channel_id=1, source_target_pairs={{0,4},{8,0},{16,8},{24,16},{28,24},{20,28},{12,20},{4,12},{1,5},{9... | collective-permute-start | bytes 589832 | tf_op jit(solution)/shard_map/ppermute | solution.py:223
  5.9 8.5 %collective-permute-start.1 = (bf16[48,2048]{1,0:T(8,128)(2,1)S(1)}, bf16[48,2048]{1,0:T(8,128)(2,1)S(1)}, u32[]{:S(2)}, u32[]{:S(2)}) collective-permute-start(bf16[48,2048]{1,0:T(8,128)(2,1)S(1)} %get-tuple-element.61.refs_0_), channel_id=1, source_target_pairs={{0,8},{8,16},{16,24},{24,28},{28,20},{20,12},{12,4},{4,0},{1,9},{9... | collective-permute-start | bytes 589832 | tf_op jit(solution)/shard_map/ppermute | solution.py:223
  6.0 8.3 %collective-permute-start = (bf16[4,48,256]{2,1,0:T(8,128)(2,1)S(1)}, bf16[4,48,256]{2,1,0:T(8,128)(2,1)S(1)}, u32[]{:S(2)}, u32[]{:S(2)}) collective-permute-start(bf16[4,48,256]{2,1,0:T(8,128)(2,1)S(1)} %get-tuple-element.60), channel_id=1, source_target_pairs={{0,4},{4,0},{8,12},{12,8},{16,20},{20,16},{24,28},{28,24},{1,5},{5... | collective-permute-start | bytes 294920 | tf_op jit(solution)/shard_map/ppermute | solution.py:222
  14.4 11.9 %collective-permute-start.6 = (bf16[48,2048]{1,0:T(8,128)(2,1)S(1)}, bf16[48,2048]{1,0:T(8,128)(2,1)S(1)}, u32[]{:S(2)}, u32[]{:S(2)}) collective-permute-start(bf16[48,2048]{1,0:T(8,128)(2,1)S(1)} %get-tuple-element.73.refs_6_), channel_id=1, source_target_pairs={{0,8},{8,16},{16,24},{24,28},{28,20},{20,12},{12,4},{4,0},{1,9},{9... | collective-permute-start | bytes 589832 | tf_op jit(solution)/shard_map/ppermute | solution.py:244
  15.2 11.1 %collective-permute-start.7 = (bf16[48,2048]{1,0:T(8,128)(2,1)S(1)}, bf16[48,2048]{1,0:T(8,128)(2,1)S(1)}, u32[]{:S(2)}, u32[]{:S(2)}) collective-permute-start(bf16[48,2048]{1,0:T(8,128)(2,1)S(1)} %get-tuple-element.74.refs_1_), channel_id=1, source_target_pairs={{0,4},{8,0},{16,8},{24,16},{28,24},{20,28},{12,20},{4,12},{1,5},{9... | collective-permute-start | bytes 589832 | tf_op jit(solution)/shard_map/ppermute | solution.py:244
  16.5 9.8 %collective-permute-start.3 = (bf16[2,48,256]{2,1,0:T(8,128)(2,1)S(1)}, bf16[2,48,256]{2,1,0:T(8,128)(2,1)S(1)}, u32[]{:S(2)}, u32[]{:S(2)}) collective-permute-start(bf16[2,48,256]{2,1,0:T(8,128)(2,1)S(1)} %get-tuple-element.70), channel_id=1, source_target_pairs={{0,8},{4,12},{8,0},{12,4},{16,24},{20,28},{24,16},{28,20},{1,9},{5... | collective-permute-start | bytes 147464 | tf_op jit(solution)/shard_map/ppermute | solution.py:264
  17.2 9.1 %collective-permute-start.4 = (bf16[2,48,256]{2,1,0:T(8,128)(2,1)S(1)}, bf16[2,48,256]{2,1,0:T(8,128)(2,1)S(1)}, u32[]{:S(2)}, u32[]{:S(2)}) collective-permute-start(bf16[2,48,256]{2,1,0:T(8,128)(2,1)S(1)} %get-tuple-element.71), channel_id=1, source_target_pairs={{0,16},{4,20},{8,24},{12,28},{16,0},{20,4},{24,8},{28,12},{1,17},{... | collective-permute-start | bytes 147464 | tf_op jit(solution)/shard_map/ppermute | solution.py:264
  19.8 6.5 %collective-permute-start.5 = (bf16[2,48,256]{2,1,0:T(8,128)(2,1)S(1)}, bf16[2,48,256]{2,1,0:T(8,128)(2,1)S(1)}, u32[]{:S(2)}, u32[]{:S(2)}) collective-permute-start(bf16[2,48,256]{2,1,0:T(8,128)(2,1)S(1)} %get-tuple-element.72), channel_id=1, source_target_pairs={{0,24},{4,28},{8,16},{12,20},{16,8},{20,12},{24,0},{28,4},{1,25},{... | collective-permute-start | bytes 147464 | tf_op jit(solution)/shard_map/ppermute | solution.py:264
  20.9 15.3 %copy-start.2 = (bf16[1024,64]{0,1:T(8,128)(2,1)S(1)}, bf16[1024,64]{0,1:T(8,128)(2,1)}, u32[]{:S(2)}) copy-start(bf16[1024,64]{0,1:T(8,128)(2,1)} %param.14) | copy-start | bytes 393220
  26.3 5.7 %collective-permute-start.8 = (bf16[384,256]{1,0:T(8,128)(2,1)S(1)}, bf16[384,256]{1,0:T(8,128)(2,1)S(1)}, u32[]{:S(2)}, u32[]{:S(2)}) collective-permute-start(bf16[384,256]{1,0:T(8,128)(2,1)S(1)} %join.1.refs_0_), channel_id=1, source_target_pairs={{0,2},{1,3},{2,0},{3,1},{4,6},{5,7},{6,4},{7,5},{8,10},{9,11},{10,... | collective-permute-start | bytes 589832 | tf_op jit(solution)/shard_map/ppermute | solution.py:275
  27.9 5.7 %collective-permute-start.9 = (bf16[48,2048]{1,0:T(8,128)(2,1)S(1)}, bf16[48,2048]{1,0:T(8,128)(2,1)S(1)}, u32[]{:S(2)}, u32[]{:S(2)}) collective-permute-start(bf16[48,2048]{1,0:T(8,128)(2,1)S(1)} %collective-permute-done.6.refs_5_), channel_id=1, source_target_pairs={{0,8},{8,16},{16,24},{24,28},{28,20},{20,12},{12,4},{4,0},{1,9},{9... | collective-permute-start | bytes 589832 | tf_op jit(solution)/shard_map/ppermute | solution.py:244
  27.9 5.7 %collective-permute-start.10 = (bf16[48,2048]{1,0:T(8,128)(2,1)S(1)}, bf16[48,2048]{1,0:T(8,128)(2,1)S(1)}, u32[]{:S(2)}, u32[]{:S(2)}) collective-permute-start(bf16[48,2048]{1,0:T(8,128)(2,1)S(1)} %collective-permute-done.7.refs_2_), channel_id=1, source_target_pairs={{0,4},{8,0},{16,8},{24,16},{28,24},{20,28},{12,20},{4,12},{1,5},{9... | collective-permute-start | bytes 589832 | tf_op jit(solution)/shard_map/ppermute | solution.py:244
  33.6 2.6 %collective-permute-start.11 = (bf16[384,256]{1,0:T(8,128)(2,1)S(1)}, bf16[384,256]{1,0:T(8,128)(2,1)S(1)}, u32[]{:S(2)}, u32[]{:S(2)}) collective-permute-start(bf16[384,256]{1,0:T(8,128)(2,1)S(1)} %join.1.refs_0_), channel_id=1, source_target_pairs={{0,1},{1,0},{2,3},{3,2},{4,5},{5,4},{6,7},{7,6},{8,9},{9,8},{10,11... | collective-permute-start | bytes 589832 | tf_op jit(solution)/shard_map/ppermute | solution.py:277
  33.6 2.6 %collective-permute-start.12 = (bf16[384,256]{1,0:T(8,128)(2,1)S(1)}, bf16[384,256]{1,0:T(8,128)(2,1)S(1)}, u32[]{:S(2)}, u32[]{:S(2)}) collective-permute-start(bf16[384,256]{1,0:T(8,128)(2,1)S(1)} %collective-permute-done.8.refs_2_), channel_id=1, source_target_pairs={{0,1},{1,0},{2,3},{3,2},{4,5},{5,4},{6,7},{7,6},{8,9},{9,8},{10,11... | collective-permute-start | bytes 589832 | tf_op jit(solution)/shard_map/ppermute | solution.py:277
  34.1 6.7 %collective-permute-start.16 = (bf16[24,2048]{1,0:T(8,128)(2,1)S(1)}, bf16[24,2048]{1,0:T(8,128)(2,1)S(1)}, u32[]{:S(2)}, u32[]{:S(2)}) collective-permute-start(bf16[24,2048]{1,0:T(8,128)(2,1)S(1)} %slice.65), channel_id=1, source_target_pairs={{0,4},{8,0},{16,8},{24,16},{28,24},{20,28},{12,20},{4,12},{1,5},{9... | collective-permute-start | bytes 294920 | tf_op jit(solution)/shard_map/ppermute | solution.py:282
  36.2 4.6 %collective-permute-start.15 = (bf16[24,2048]{1,0:T(8,128)(2,1)S(1)}, bf16[24,2048]{1,0:T(8,128)(2,1)S(1)}, u32[]{:S(2)}, u32[]{:S(2)}) collective-permute-start(bf16[24,2048]{1,0:T(8,128)(2,1)S(1)} %slice.64), channel_id=1, source_target_pairs={{0,8},{8,16},{16,24},{24,28},{28,20},{20,12},{12,4},{4,0},{1,9},{9... | collective-permute-start | bytes 294920 | tf_op jit(solution)/shard_map/ppermute | solution.py:281
  38.8 4.7 %collective-permute-start.14 = (bf16[24,2048]{1,0:T(8,128)(2,1)S(1)}, bf16[24,2048]{1,0:T(8,128)(2,1)S(1)}, u32[]{:S(2)}, u32[]{:S(2)}) collective-permute-start(bf16[24,2048]{1,0:T(8,128)(2,1)S(1)} %get-tuple-element.116), channel_id=1, source_target_pairs={{0,4},{8,0},{16,8},{24,16},{28,24},{20,28},{12,20},{4,12},{1,5},{9... | collective-permute-start | bytes 294920 | tf_op jit(solution)/shard_map/ppermute | solution.py:321
  40.8 4.6 %collective-permute-start.13 = (bf16[24,2048]{1,0:T(8,128)(2,1)S(1)}, bf16[24,2048]{1,0:T(8,128)(2,1)S(1)}, u32[]{:S(2)}, u32[]{:S(2)}) collective-permute-start(bf16[24,2048]{1,0:T(8,128)(2,1)S(1)} %get-tuple-element.118), channel_id=1, source_target_pairs={{0,8},{8,16},{16,24},{24,28},{28,20},{20,12},{12,4},{4,0},{1,9},{9... | collective-permute-start | bytes 294920 | tf_op jit(solution)/shard_map/ppermute | solution.py:321
  45.5 6.0 %collective-permute-start.17 = (bf16[48,2048]{1,0:T(8,128)(2,1)S(1)}, bf16[48,2048]{1,0:T(8,128)(2,1)S(1)}, u32[]{:S(2)}, u32[]{:S(2)}) collective-permute-start(bf16[48,2048]{1,0:T(8,128)(2,1)S(1)} %get-tuple-element.89), channel_id=1, source_target_pairs={{0,8},{8,16},{16,24},{24,28},{28,20},{20,12},{12,4},{4,0},{1,9},{9... | collective-permute-start | bytes 589832 | tf_op jit(solution)/shard_map/ppermute | solution.py:436
  45.6 6.0 %collective-permute-start.18 = (bf16[48,2048]{1,0:T(8,128)(2,1)S(1)}, bf16[48,2048]{1,0:T(8,128)(2,1)S(1)}, u32[]{:S(2)}, u32[]{:S(2)}) collective-permute-start(bf16[48,2048]{1,0:T(8,128)(2,1)S(1)} %get-tuple-element.90), channel_id=1, source_target_pairs={{0,4},{8,0},{16,8},{24,16},{28,24},{20,28},{12,20},{4,12},{1,5},{9... | collective-permute-start | bytes 589832 | tf_op jit(solution)/shard_map/ppermute | solution.py:437
  47.6 5.0 %collective-permute-start.20 = (f32[192,128]{1,0:T(8,128)S(1)}, f32[192,128]{1,0:T(8,128)S(1)}, u32[]{:S(2)}, u32[]{:S(2)}) collective-permute-start(f32[192,128]{1,0:T(8,128)S(1)} %get-tuple-element.92.low_ref), channel_id=1, source_target_pairs={{0,4},{4,0},{8,12},{12,8},{16,20},{20,16},{24,28},{28,24},{1,5},{5... | collective-permute-start | bytes 294920 | tf_op jit(solution)/shard_map/ppermute | solution.py:322
  48.4 4.2 %collective-permute-start.19 = (bf16[96,1152]{1,0:T(8,128)(2,1)S(1)}, bf16[96,1152]{1,0:T(8,128)(2,1)S(1)}, u32[]{:S(2)}, u32[]{:S(2)}) collective-permute-start(bf16[96,1152]{1,0:T(8,128)(2,1)S(1)} %get-tuple-element.91), channel_id=1, source_target_pairs={{0,1},{1,0},{2,3},{3,2},{4,5},{5,4},{6,7},{7,6},{8,9},{9,8},{10,11... | collective-permute-start | bytes 663560 | tf_op jit(solution)/shard_map/ppermute | solution.py:395
  52.6 5.9 %collective-permute-start.21 = (bf16[48,2048]{1,0:T(8,128)(2,1)S(1)}, bf16[48,2048]{1,0:T(8,128)(2,1)S(1)}, u32[]{:S(2)}, u32[]{:S(2)}) collective-permute-start(bf16[48,2048]{1,0:T(8,128)(2,1)S(1)} %get-tuple-element.93), channel_id=1, source_target_pairs={{0,8},{8,16},{16,24},{24,28},{28,20},{20,12},{12,4},{4,0},{1,9},{9... | collective-permute-start | bytes 589832 | tf_op jit(solution)/shard_map/ppermute | solution.py:436
  53.3 6.0 %collective-permute-start.22 = (bf16[48,2048]{1,0:T(8,128)(2,1)S(1)}, bf16[48,2048]{1,0:T(8,128)(2,1)S(1)}, u32[]{:S(2)}, u32[]{:S(2)}) collective-permute-start(bf16[48,2048]{1,0:T(8,128)(2,1)S(1)} %get-tuple-element.94), channel_id=1, source_target_pairs={{0,4},{8,0},{16,8},{24,16},{28,24},{20,28},{12,20},{4,12},{1,5},{9... | collective-permute-start | bytes 589832 | tf_op jit(solution)/shard_map/ppermute | solution.py:437
  55.1 9.1 %collective-permute-start.27 = (f32[96,128]{1,0:T(8,128)S(1)}, f32[96,128]{1,0:T(8,128)S(1)}, u32[]{:S(2)}, u32[]{:S(2)}) collective-permute-start(f32[96,128]{1,0:T(8,128)S(1)} %compact.1), channel_id=1, source_target_pairs={{0,16},{4,20},{8,24},{12,28},{16,0},{20,4},{24,8},{28,12},{1,17},{... | collective-permute-start | bytes 147464 | tf_op jit(solution)/shard_map/ppermute | solution.py:410
  57.9 6.0 %collective-permute-start.25 = (bf16[96,1152]{1,0:T(8,128)(2,1)S(1)}, bf16[96,1152]{1,0:T(8,128)(2,1)S(1)}, u32[]{:S(2)}, u32[]{:S(2)}) collective-permute-start(bf16[96,1152]{1,0:T(8,128)(2,1)S(1)} %add.60.a_ref), channel_id=1, source_target_pairs={{0,2},{1,3},{2,0},{3,1},{4,6},{5,7},{6,4},{7,5},{8,10},{9,11},{10,... | collective-permute-start | bytes 663560 | tf_op jit(solution)/shard_map/ppermute | solution.py:402
  59.4 5.7 %collective-permute-start.23 = (bf16[48,2048]{1,0:T(8,128)(2,1)S(1)}, bf16[48,2048]{1,0:T(8,128)(2,1)S(1)}, u32[]{:S(2)}, u32[]{:S(2)}) collective-permute-start(bf16[48,2048]{1,0:T(8,128)(2,1)S(1)} %get-tuple-element.95), channel_id=1, source_target_pairs={{0,8},{8,16},{16,24},{24,28},{28,20},{20,12},{12,4},{4,0},{1,9},{9... | collective-permute-start | bytes 589832 | tf_op jit(solution)/shard_map/ppermute | solution.py:436
  61.5 7.1 %collective-permute-start.24 = (bf16[48,2048]{1,0:T(8,128)(2,1)S(1)}, bf16[48,2048]{1,0:T(8,128)(2,1)S(1)}, u32[]{:S(2)}, u32[]{:S(2)}) collective-permute-start(bf16[48,2048]{1,0:T(8,128)(2,1)S(1)} %get-tuple-element.96), channel_id=1, source_target_pairs={{0,4},{8,0},{16,8},{24,16},{28,24},{20,28},{12,20},{4,12},{1,5},{9... | collective-permute-start | bytes 589832 | tf_op jit(solution)/shard_map/ppermute | solution.py:437
  64.1 4.5 %collective-permute-start.26 = (bf16[96,1152]{1,0:T(8,128)(2,1)S(1)}, bf16[96,1152]{1,0:T(8,128)(2,1)S(1)}, u32[]{:S(2)}, u32[]{:S(2)}) collective-permute-start(bf16[96,1152]{1,0:T(8,128)(2,1)S(1)} %finish.1.a_ref), channel_id=1, source_target_pairs={{0,1},{1,0},{2,3},{3,2},{4,5},{5,4},{6,7},{7,6},{8,9},{9,8},{10,11... | collective-permute-start | bytes 663560 | tf_op jit(solution)/shard_map/ppermute | solution.py:404
  70.1 1.1 %collective-permute-start.29 = (f32[1,48]{1,0:T(1,128)S(1)}, f32[1,48]{1,0:T(1,128)S(1)}, u32[]{:S(2)}, u32[]{:S(2)}) collective-permute-start(f32[1,48]{1,0:T(1,128)S(1)} %get-tuple-element.110), channel_id=1, source_target_pairs={{0,1},{1,0},{2,3},{3,2},{4,5},{5,4},{6,7},{7,6},{8,9},{9,8},{10,11... | collective-permute-start | bytes 584 | tf_op jit(solution)/shard_map/ppermute | solution.py:468
  71.2 4.1 %collective-permute-start.30 = (f32[1,48]{1,0:T(1,128)S(1)}, f32[1,48]{1,0:T(1,128)S(1)}, u32[]{:S(2)}, u32[]{:S(2)}) collective-permute-start(f32[1,48]{1,0:T(1,128)S(1)} %add.39), channel_id=1, source_target_pairs={{0,2},{1,3},{2,0},{3,1},{4,6},{5,7},{6,4},{7,5},{8,10},{9,11},{10,... | collective-permute-start | bytes 584 | tf_op jit(solution)/shard_map/ppermute | solution.py:468
  71.7 4.1 %collective-permute-start.28 = (f32[96,128]{1,0:T(8,128)S(1)}, f32[96,128]{1,0:T(8,128)S(1)}, u32[]{:S(2)}, u32[]{:S(2)}) collective-permute-start(f32[96,128]{1,0:T(8,128)S(1)} %add.37), channel_id=1, source_target_pairs={{0,8},{4,12},{8,0},{12,4},{16,24},{20,28},{24,16},{28,20},{1,9},{5... | collective-permute-start | bytes 147464 | tf_op jit(solution)/shard_map/ppermute | solution.py:410
  (5 other events, 55.3 us)

commit v4 on v3

--- a/solution.py
+++ b/solution.py
@@ -381,7 +381,8 @@
             out_ref[:, :heads] = (a[:, :heads].astype(F32) + b[:, :heads].astype(F32)).astype(BF)
             out_ref[:, heads:] = jnp.concatenate(split2(ranks(a, b)), axis=1)
 
-        def finish(a_ref, b_ref, down_ref, out_ref):
+        def finish(a_ref, b_ref, down_ref, low_ref, low_other_ref, out_ref, low_out_ref):
+            low_out_ref[...] = low_ref[...] + low_other_ref[...]
             a, b = a_ref[...], b_ref[...]
             rank_grad = ranks(a, b).astype(BF)
             tail = dot(rank_grad, down_ref[...])
@@ -400,12 +401,15 @@
                 mine = call(add, [shape((some, wide), BF)], mine, recv, name="add")[0]
                 bit *= 2
             recv = yield lax.ppermute(mine, "tp", flip(tp, bit))
-            done = call(finish, [shape((some, wide), BF)], mine, recv, down_t, name="finish")[0]
+            done, low_total = call(
+                finish, [shape((some, wide), BF), shape((live_slots // 2, side), F32)],
+                mine, recv, down_t, *low_terms, name="finish",
+            )
             other_done = yield lax.ppermute(done, "tp", flip(tp, 1))
-            return done, other_done
+            return done, other_done, low_total
 
         def sum_low(total):
-            bit = half
+            bit = half // 2
             while bit > 1:
                 recv = yield lax.ppermute(total, "seq", flip(n, bit))
                 total = total + recv
@@ -439,37 +443,15 @@
                 head_steps, head_value = sum_heads(keep, send), None
             elif step == half - 2:
                 low_live = call(compact, [shape((some, side), F32)], low, low_across, where_live, name="compact")[0]
-                low_steps, low_value = sum_low(low_live), None
-                low_value = low_steps.send(None)
+                low_terms = low_live, lax.ppermute(low_live, "seq", flip(n, half))
             if step >= half - 2:
                 head_value = head_steps.send(head_value)
-        done, other_done = drain(head_steps, head_value)
-        going, coming, other_done, low_value = lax.optimization_barrier((going, coming, other_done, low_value))
-        low_sum = drain(low_steps, low_value)
-
-        def home(counts_ref, selected_ref, gate_ref, res_ref, own_ref, going_ref, coming_ref, up_ref, out_ref, gate_out_ref):
-            chosen = pick(counts_ref, selected_ref)
-            block = own_ref[...].astype(F32) + going_ref[...].astype(F32) + coming_ref[...].astype(F32)
-            gate_out_ref[...] = row_of(jnp.sum(up_ref[...].astype(F32) * block, axis=1, keepdims=True))
-            res = res_ref[...]
-            picked = dot(chosen, res, 0, 0)
-            updated = (picked + column(gate_ref[...]) * block).astype(BF)
-            hit = jnp.sum(chosen.astype(F32), axis=1, keepdims=True) > 0
-            out_ref[...] = jnp.where(hit, dot(chosen, updated), res.astype(F32)).astype(BF)
-
-        outgoing_residual, gate_part = call(
-            home,
-            [shape((tokens, cols), BF), shape((1, cap), F32)],
-            counts, selected_row, gate_row, residual, partial[0], going, coming, upstream,
-            in_specs=[smem] + [vmem] * 7, name="home",
-        )
-        bit = 1
-        while bit < tp:
-            gate_part = gate_part + lax.ppermute(gate_part, "tp", flip(tp, bit))
-            bit *= 2
-
+        done, other_done, low_total = drain(head_steps, head_value)
+        low_steps = sum_low(low_total)
+        low_value = low_steps.send(None)
         def last(a_ref, b_ref, where_ref, *refs):
-            piece_refs, (grad_ref, down_grad_ref, live, rank_ref) = refs[:shares], refs[shares:]
+            piece_refs, (grad_ref, down_grad_ref, token_ref, live, rank_ref) = refs[:shares], refs[shares:]
+            token_ref[...] = jnp.zeros_like(token_ref)
             seq, core = me()
             for ref, at in ((a_ref, core), (b_ref, 1 - core)):
                 live[pl.ds(pl.multiple_of(at * some, 16), some), :] = ref[...]
@@ -482,12 +464,36 @@
                 at = pl.multiple_of((share() ^ j) * sub, 128)
                 down_grad_ref[:, pl.ds(at, sub)] = dot(rank_grad, ref[...], 0, 0)
 
-        attention_output_grad, down_gradient = call(
+        attention_output_grad, down_gradient, mark = call(
             last,
-            [shape((slots, heads), BF), shape((rank, heads), F32)],
+            [shape((slots, heads), BF), shape((rank, heads), F32), shape((8, 128), F32)],
             done, other_done, where_live, *pieces,
             scratch=[pltpu.VMEM((live_slots, wide), BF), pltpu.VMEM((n, cap, side), BF)], name="last",
         )
+
+        going, coming, mark, low_value = lax.optimization_barrier((going, coming, mark, low_value))
+        low_sum = drain(low_steps, low_value)
+
+        def home(counts_ref, selected_ref, gate_ref, res_ref, own_ref, going_ref, coming_ref, up_ref, _, out_ref, gate_out_ref):
+            chosen = pick(counts_ref, selected_ref)
+            block = own_ref[...].astype(F32) + going_ref[...].astype(F32) + coming_ref[...].astype(F32)
+            gate_out_ref[...] = row_of(jnp.sum(up_ref[...].astype(F32) * block, axis=1, keepdims=True))
+            res = res_ref[...]
+            picked = dot(chosen, res, 0, 0)
+            updated = (picked + column(gate_ref[...]) * block).astype(BF)
+            hit = jnp.sum(chosen.astype(F32), axis=1, keepdims=True) > 0
+            out_ref[...] = jnp.where(hit, dot(chosen, updated), res.astype(F32)).astype(BF)
+
+        outgoing_residual, gate_part = call(
+            home,
+            [shape((tokens, cols), BF), shape((1, cap), F32)],
+            counts, selected_row, gate_row, residual, partial[0], going, coming, upstream, mark,
+            in_specs=[smem] + [vmem] * 8, name="home",
+        )
+        bit = 1
+        while bit < tp:
+            gate_part = gate_part + lax.ppermute(gate_part, "tp", flip(tp, bit))
+            bit *= 2
 
         def up_gradient(low_ref, g_ref, out_ref):
             low = jnp.concatenate([low_ref[:, :rank], low_ref[:, rank:]], axis=0)

time: 77.3 us -> 76.1 us (0.984)
  waiting for transfers between devices: 19.4 us -> 18.1 us
    ppermute x3, waiting for transfers between devices: 4.25 us -> 0.8 us  [body(): coming = lax.ppermute(there, 'seq', ring(-1))]
    ppermute x0 -> x1, starting transfers between devices: none -> 2.56 us  [body(): low_terms = (low_live, lax.ppermute(low_live, 'seq', flip(n, half)))]
    ppermute x2 -> x1, starting transfers between devices: 4.59 us -> 2.09 us  [sum_low(): recv = (yield lax.ppermute(total, 'seq', flip(n, bit)))]
    ppermute x2, waiting for transfers between devices: 1.11 us -> 2.67 us  [body(): gate_part = gate_part + lax.ppermute(gate_part, 'tp', flip(tp, bit))]
    ppermute x1, waiting for transfers between devices: 0.01 us -> 1.46 us  [sum_heads(): other_done = (yield lax.ppermute(done, 'tp', flip(tp, 1)))]
    ppermute x3, waiting for transfers between devices: 4.11 us -> 3.19 us  [body(): going = lax.ppermute(here, 'seq', ring(1))]
  transfers between devices with their start and end apart: 31 -> 31, of which waited for: 12 -> 11; matrix products, arithmetic and copies ran while one was open for 1% -> 1% of each run, Pallas kernels for 24% -> 26%
where the time goes in v4:
time: 76.1 us; the launch traced here: 76 us
  starting transfers between devices  32.7 us (43%)
  Pallas kernels  22.6 us (30%)
  waiting for transfers between devices  18.1 us (24%)
  between operations  1.57 us (2%)
  other arithmetic  0.79 us (1%)
    pallas_call x13, Pallas kernels, call(): pl.pallas_call(kernel, out_shape=tuple(outs), in_specs=in_specs or [whole...  22.6 us
    ppermute x3, starting transfers between devices, body(): lax.ppermute(pairs[k], 'seq', flip(n, 2 * k))  4.39 us
    ppermute x2, starting transfers between devices, hop(): lax.ppermute(coming, 'seq', ring(-1))  3.35 us
    ppermute x3, starting transfers between devices, body(): coming = lax.ppermute(there, 'seq', ring(-1))  3.34 us
    ppermute x3, waiting for transfers between devices, body(): going = lax.ppermute(here, 'seq', ring(1))  3.19 us
    ppermute x1, starting transfers between devices, body(): lax.ppermute(grad, 'seq', ring(-1))  2.99 us
    ppermute x3, starting transfers between devices, body(): going = lax.ppermute(here, 'seq', ring(1))  2.88 us
    ppermute x2, waiting for transfers between devices, body(): gate_part = gate_part + lax.ppermute(gate_part, 'tp', flip(tp, bit))  2.67 us
  transfers between devices with their start and end apart: 31, of which 11 were waited for; matrix products, arithmetic and copies ran while one was open for 1% of the time, Pallas kernels for 26%

profile of v4, /device:TPU:0, one launch (start us, length us, event | category | flops | bytes accessed | tf_op | source)
XLA Modules:
  0.0 76.0 jit_solution(14190258965383483487)
XLA Ops:
  1.3 1.6 %prepare.1 = (bf16[4,48,256]{2,1,0:T(8,128)(2,1)S(1)}, bf16[4,48,256]{2,1,0:T(8,128)(2,1)S(1)}, bf16[48,2048]{1,0:T(8,128)(2,1)S(1)}, bf16[48,2048]{1,0:T(8,128)(2,1)S(1)}) custom-call(s32[1]{0:T(128)S(6)} %copy.17.counts_ref, s32[1,48]{1,0:T(1,128)} %bitcast.36, f32[1,48]{1,0:T(1,128)} %bitcast.38, bf16[48,8192]{1,0:T(8,128)(2,1)} %attention_ref.1, ...), custom_call_target="tpu_custom_call" | custom-call | bytes 2163076 | tf_op jit(solution)/shard_map/prepare/pallas_call | solution.py:55
  2.9 3.0 %collective-permute-start.2 = (bf16[48,2048]{1,0:T(8,128)(2,1)S(1)}, bf16[48,2048]{1,0:T(8,128)(2,1)S(1)}, u32[]{:S(2)}, u32[]{:S(2)}) collective-permute-start(bf16[48,2048]{1,0:T(8,128)(2,1)S(1)} %get-tuple-element.64.refs_0_), channel_id=1, source_target_pairs={{0,4},{8,0},{16,8},{24,16},{28,24},{20,28},{12,20},{4,12},{1,5},{9... | collective-permute-start | bytes 589832 | tf_op jit(solution)/shard_map/ppermute | solution.py:223
  6.0 1.9 %collective-permute-start = (bf16[4,48,256]{2,1,0:T(8,128)(2,1)S(1)}, bf16[4,48,256]{2,1,0:T(8,128)(2,1)S(1)}, u32[]{:S(2)}, u32[]{:S(2)}) collective-permute-start(bf16[4,48,256]{2,1,0:T(8,128)(2,1)S(1)} %get-tuple-element.63), channel_id=1, source_target_pairs={{0,4},{4,0},{8,12},{12,8},{16,20},{20,16},{24,28},{28,24},{1,5},{5... | collective-permute-start | bytes 294920 | tf_op jit(solution)/shard_map/ppermute | solution.py:222
  8.1 5.3 %dequantize.2 = (bf16[512,2048]{1,0:T(8,128)(2,1)S(1)}, f32[8,128]{1,0:T(8,128)S(1)}) custom-call(s32[1024,2048]{1,0:T(8,128)} %codes_hbm.3, f32[1024,32]{1,0:T(8,128)S(1)} %copy.15.absmax_ref), custom_call_target="tpu_custom_call" | custom-call | flops 104857600 | bytes 10620928 | tf_op jit(solution)/shard_map/dequantize/pallas_call | solution.py:55
  13.5 0.9 %collective-permute-done.across_ref = bf16[4,48,256]{2,1,0:T(8,128)(2,1)S(1)} collective-permute-done((bf16[4,48,256]{2,1,0:T(8,128)(2,1)S(1)}, bf16[4,48,256]{2,1,0:T(8,128)(2,1)S(1)}, u32[]{:S(2)}, u32[]{:S(2)}) %collective-permute-start) | collective-permute-done | bytes 98336 | tf_op jit(solution)/shard_map/ppermute | solution.py:222
  15.2 1.3 %collective-permute-start.7 = (bf16[48,2048]{1,0:T(8,128)(2,1)S(1)}, bf16[48,2048]{1,0:T(8,128)(2,1)S(1)}, u32[]{:S(2)}, u32[]{:S(2)}) collective-permute-start(bf16[48,2048]{1,0:T(8,128)(2,1)S(1)} %get-tuple-element.77.refs_1_), channel_id=1, source_target_pairs={{0,4},{8,0},{16,8},{24,16},{28,24},{20,28},{12,20},{4,12},{1,5},{9... | collective-permute-start | bytes 589832 | tf_op jit(solution)/shard_map/ppermute | solution.py:244
  17.2 2.6 %collective-permute-start.4 = (bf16[2,48,256]{2,1,0:T(8,128)(2,1)S(1)}, bf16[2,48,256]{2,1,0:T(8,128)(2,1)S(1)}, u32[]{:S(2)}, u32[]{:S(2)}) collective-permute-start(bf16[2,48,256]{2,1,0:T(8,128)(2,1)S(1)} %get-tuple-element.74), channel_id=1, source_target_pairs={{0,16},{4,20},{8,24},{12,28},{16,0},{20,4},{24,8},{28,12},{1,17},{... | collective-permute-start | bytes 147464 | tf_op jit(solution)/shard_map/ppermute | solution.py:264
  19.8 1.1 %collective-permute-start.5 = (bf16[2,48,256]{2,1,0:T(8,128)(2,1)S(1)}, bf16[2,48,256]{2,1,0:T(8,128)(2,1)S(1)}, u32[]{:S(2)}, u32[]{:S(2)}) collective-permute-start(bf16[2,48,256]{2,1,0:T(8,128)(2,1)S(1)} %get-tuple-element.75), channel_id=1, source_target_pairs={{0,24},{4,28},{8,16},{12,20},{16,8},{20,12},{24,0},{28,4},{1,25},{... | collective-permute-start | bytes 147464 | tf_op jit(solution)/shard_map/ppermute | solution.py:264
  20.9 5.4 %dequantize.3 = (bf16[512,2048]{1,0:T(8,128)(2,1)S(1)}, f32[8,128]{1,0:T(8,128)S(1)}) custom-call(s32[1024,2048]{1,0:T(8,128)} %codes_hbm.3, f32[1024,32]{1,0:T(8,128)S(1)} %copy.15.absmax_ref, f32[8,128]{1,0:T(8,128)S(1)} %get-tuple-element.70.refs_0_), custom_call_target="tpu_custom_call" | custom-call | flops 104857600 | bytes 10625024 | tf_op jit(solution)/shard_map/dequantize/pallas_call | solution.py:55
  26.3 1.6 %collective-permute-start.8 = (bf16[384,256]{1,0:T(8,128)(2,1)S(1)}, bf16[384,256]{1,0:T(8,128)(2,1)S(1)}, u32[]{:S(2)}, u32[]{:S(2)}) collective-permute-start(bf16[384,256]{1,0:T(8,128)(2,1)S(1)} %join.1.refs_0_), channel_id=1, source_target_pairs={{0,2},{1,3},{2,0},{3,1},{4,6},{5,7},{6,4},{7,5},{8,10},{9,11},{10,... | collective-permute-start | bytes 589832 | tf_op jit(solution)/shard_map/ppermute | solution.py:275
  27.9 2.0 %collective-permute-start.10 = (bf16[48,2048]{1,0:T(8,128)(2,1)S(1)}, bf16[48,2048]{1,0:T(8,128)(2,1)S(1)}, u32[]{:S(2)}, u32[]{:S(2)}) collective-permute-start(bf16[48,2048]{1,0:T(8,128)(2,1)S(1)} %collective-permute-done.7.refs_2_), channel_id=1, source_target_pairs={{0,4},{8,0},{16,8},{24,16},{28,24},{20,28},{12,20},{4,12},{1,5},{9... | collective-permute-start | bytes 589832 | tf_op jit(solution)/shard_map/ppermute | solution.py:244
  30.0 2.1 %collective-permute-done.8.refs_2_ = bf16[384,256]{1,0:T(8,128)(2,1)S(1)} collective-permute-done((bf16[384,256]{1,0:T(8,128)(2,1)S(1)}, bf16[384,256]{1,0:T(8,128)(2,1)S(1)}, u32[]{:S(2)}, u32[]{:S(2)}) %collective-permute-start.8) | collective-permute-done | bytes 196640 | tf_op jit(solution)/shard_map/ppermute | solution.py:275
  32.1 1.5 %collective-permute-done.9.refs_4_ = bf16[48,2048]{1,0:T(8,128)(2,1)S(1)} collective-permute-done((bf16[48,2048]{1,0:T(8,128)(2,1)S(1)}, bf16[48,2048]{1,0:T(8,128)(2,1)S(1)}, u32[]{:S(2)}, u32[]{:S(2)}) %collective-permute-start.9) | collective-permute-done | bytes 196640 | tf_op jit(solution)/shard_map/ppermute | solution.py:244
  34.1 2.1 %collective-permute-start.16 = (bf16[24,2048]{1,0:T(8,128)(2,1)S(1)}, bf16[24,2048]{1,0:T(8,128)(2,1)S(1)}, u32[]{:S(2)}, u32[]{:S(2)}) collective-permute-start(bf16[24,2048]{1,0:T(8,128)(2,1)S(1)} %slice.65), channel_id=1, source_target_pairs={{0,4},{8,0},{16,8},{24,16},{28,24},{20,28},{12,20},{4,12},{1,5},{9... | collective-permute-start | bytes 294920 | tf_op jit(solution)/shard_map/ppermute | solution.py:282
  36.2 2.5 %forward.1 = (bf16[8,48,2048]{2,1,0:T(8,128)(2,1)S(1)}, f32[192,128]{1,0:T(8,128)S(1)}) custom-call(bf16[64,1024]{1,0:T(8,128)(2,1)S(1)} %bitcast.34, bf16[64,2048]{1,0:T(8,128)(2,1)S(1)} %copy-done.1, bf16[512,2048]{1,0:T(8,128)(2,1)S(1)} %get-tuple-element.61.w0_ref, bf16[512,2048]{1,0:T(8,128)(2,1)S(1)} %get-tuple-element.71.w1_ref, ...), custom_call_target="tpu_custom_call" | custom-call | flops 1610612736 | bytes 7045120 | tf_op jit(solution)/shard_map/forward/pallas_call | solution.py:55
  38.8 2.1 %collective-permute-start.14 = (bf16[24,2048]{1,0:T(8,128)(2,1)S(1)}, bf16[24,2048]{1,0:T(8,128)(2,1)S(1)}, u32[]{:S(2)}, u32[]{:S(2)}) collective-permute-start(bf16[24,2048]{1,0:T(8,128)(2,1)S(1)} %get-tuple-element.122), channel_id=1, source_target_pairs={{0,4},{8,0},{16,8},{24,16},{28,24},{20,28},{12,20},{4,12},{1,5},{9... | collective-permute-start | bytes 294920 | tf_op jit(solution)/shard_map/ppermute | solution.py:321
  40.9 2.5 %backward.1 = (f32[96,1152]{1,0:T(8,128)S(1)}, bf16[96,1152]{1,0:T(8,128)(2,1)S(1)}, bf16[192,2048]{1,0:T(8,128)(2,1)S(1)}, bf16[384,192]{1,0:T(8,128)(2,1)S(1)}) custom-call(bf16[64,2048]{1,0:T(8,128)(2,1)S(1)} %copy-done.1, bf16[512,2048]{1,0:T(8,128)(2,1)S(1)} %get-tuple-element.61.w0_ref, bf16[512,2048]{1,0:T(8,128)(2,1)S(1)} %get-tuple-element.71.w1_ref, ...), custom_call_target="tpu_custom_call" | custom-call | flops 805306368 | bytes 7626752 | tf_op jit(solution)/shard_map/backward/pallas_call | solution.py:55
  43.4 2.0 %collective-permute-done.13 = bf16[24,2048]{1,0:T(8,128)(2,1)S(1)} collective-permute-done((bf16[24,2048]{1,0:T(8,128)(2,1)S(1)}, bf16[24,2048]{1,0:T(8,128)(2,1)S(1)}, u32[]{:S(2)}, u32[]{:S(2)}) %collective-permute-start.13) | collective-permute-done | bytes 98336 | tf_op jit(solution)/shard_map/ppermute | solution.py:321
  45.6 2.0 %collective-permute-start.18 = (bf16[48,2048]{1,0:T(8,128)(2,1)S(1)}, bf16[48,2048]{1,0:T(8,128)(2,1)S(1)}, u32[]{:S(2)}, u32[]{:S(2)}) collective-permute-start(bf16[48,2048]{1,0:T(8,128)(2,1)S(1)} %get-tuple-element.93), channel_id=1, source_target_pairs={{0,4},{8,0},{16,8},{24,16},{28,24},{20,28},{12,20},{4,12},{1,5},{9... | collective-permute-start | bytes 589832 | tf_op jit(solution)/shard_map/ppermute | solution.py:441
  48.4 3.2 %collective-permute-done.17 = bf16[48,2048]{1,0:T(8,128)(2,1)S(1)} collective-permute-done((bf16[48,2048]{1,0:T(8,128)(2,1)S(1)}, bf16[48,2048]{1,0:T(8,128)(2,1)S(1)}, u32[]{:S(2)}, u32[]{:S(2)}) %collective-permute-start.17) | collective-permute-done | bytes 196640 | tf_op jit(solution)/shard_map/ppermute | solution.py:440
  51.7 0.9 %collective-permute-done.20.low_across_ref = f32[192,128]{1,0:T(8,128)S(1)} collective-permute-done((f32[192,128]{1,0:T(8,128)S(1)}, f32[192,128]{1,0:T(8,128)S(1)}, u32[]{:S(2)}, u32[]{:S(2)}) %collective-permute-start.20) | collective-permute-done | bytes 98336 | tf_op jit(solution)/shard_map/ppermute | solution.py:322
  53.3 1.3 %collective-permute-start.22 = (bf16[48,2048]{1,0:T(8,128)(2,1)S(1)}, bf16[48,2048]{1,0:T(8,128)(2,1)S(1)}, u32[]{:S(2)}, u32[]{:S(2)}) collective-permute-start(bf16[48,2048]{1,0:T(8,128)(2,1)S(1)} %get-tuple-element.97), channel_id=1, source_target_pairs={{0,4},{8,0},{16,8},{24,16},{28,24},{20,28},{12,20},{4,12},{1,5},{9... | collective-permute-start | bytes 589832 | tf_op jit(solution)/shard_map/ppermute | solution.py:441
  55.1 2.6 %collective-permute-start.26 = (f32[96,128]{1,0:T(8,128)S(1)}, f32[96,128]{1,0:T(8,128)S(1)}, u32[]{:S(2)}, u32[]{:S(2)}) collective-permute-start(f32[96,128]{1,0:T(8,128)S(1)} %compact.1.low_ref), channel_id=1, source_target_pairs={{0,16},{4,20},{8,24},{12,28},{16,0},{20,4},{24,8},{28,12},{1,17},{... | collective-permute-start | bytes 147464 | tf_op jit(solution)/shard_map/ppermute | solution.py:446
  59.4 2.1 %collective-permute-start.23 = (bf16[48,2048]{1,0:T(8,128)(2,1)S(1)}, bf16[48,2048]{1,0:T(8,128)(2,1)S(1)}, u32[]{:S(2)}, u32[]{:S(2)}) collective-permute-start(bf16[48,2048]{1,0:T(8,128)(2,1)S(1)} %get-tuple-element.98), channel_id=1, source_target_pairs={{0,8},{8,16},{16,24},{24,28},{28,20},{20,12},{12,4},{4,0},{1,9},{9... | collective-permute-start | bytes 589832 | tf_op jit(solution)/shard_map/ppermute | solution.py:440
  61.6 2.3 %collective-permute-done.25.b_ref = bf16[96,1152]{1,0:T(8,128)(2,1)S(1)} collective-permute-done((bf16[96,1152]{1,0:T(8,128)(2,1)S(1)}, bf16[96,1152]{1,0:T(8,128)(2,1)S(1)}, u32[]{:S(2)}, u32[]{:S(2)}) %collective-permute-start.25) | collective-permute-done | bytes 221216 | tf_op jit(solution)/shard_map/ppermute | solution.py:403
  64.2 2.1 %collective-permute-start.28 = (f32[96,128]{1,0:T(8,128)S(1)}, f32[96,128]{1,0:T(8,128)S(1)}, u32[]{:S(2)}, u32[]{:S(2)}) collective-permute-start(f32[96,128]{1,0:T(8,128)S(1)} %get-tuple-element.106), channel_id=1, source_target_pairs={{0,8},{4,12},{8,0},{12,4},{16,24},{20,28},{24,16},{28,20},{1,9},{5... | collective-permute-start | bytes 147464 | tf_op jit(solution)/shard_map/ppermute | solution.py:414
  66.3 1.5 %collective-permute-done.27.b_ref = bf16[96,1152]{1,0:T(8,128)(2,1)S(1)} collective-permute-done((bf16[96,1152]{1,0:T(8,128)(2,1)S(1)}, bf16[96,1152]{1,0:T(8,128)(2,1)S(1)}, u32[]{:S(2)}, u32[]{:S(2)}) %collective-permute-start.27) | collective-permute-done | bytes 221216 | tf_op jit(solution)/shard_map/ppermute | solution.py:408
  67.7 1.6 %last.1 = (bf16[384,1024]{1,0:T(8,128)(2,1)}, f32[64,1024]{1,0:T(8,128)}, f32[8,128]{1,0:T(8,128)S(1)}) custom-call(bf16[96,1152]{1,0:T(8,128)(2,1)S(1)} %get-tuple-element.104.a_ref, bf16[96,1152]{1,0:T(8,128)(2,1)S(1)} %collective-permute-done.27.b_ref, bf16[384,192]{1,0:T(8,128)(2,1)S(1)} %get-tuple-element.103.where_ref, ...), custom_call_target="tpu_custom_call" | custom-call | bytes 2428928 | tf_op jit(solution)/shard_map/last/pallas_call | solution.py:55
  69.3 1.5 %home.1 = (bf16[192,2048]{1,0:T(8,128)(2,1)}, f32[1,48]{1,0:T(1,128)S(1)}) custom-call(s32[1]{0:T(128)S(6)} %copy.17.counts_ref, s32[1,48]{1,0:T(1,128)S(1)} %bitcast.37, f32[1,48]{1,0:T(1,128)S(1)} %bitcast.39, bf16[192,2048]{1,0:T(8,128)(2,1)S(1)} %copy-done, bf16[48,2048]{1,0:T(8,128)(2,1)S(1)} %slice_bitcast_fusion.own_ref, ...), custom_call_target="tpu_custom_call" | custom-call | bytes 2363972 | tf_op jit(solution)/shard_map/home/pallas_call | solution.py:55
  71.0 1.0 %collective-permute-done.29 = f32[1,48]{1,0:T(1,128)S(1)} collective-permute-done((f32[1,48]{1,0:T(1,128)S(1)}, f32[1,48]{1,0:T(1,128)S(1)}, u32[]{:S(2)}, u32[]{:S(2)}) %collective-permute-start.29) | collective-permute-done | bytes 224 | tf_op jit(solution)/shard_map/ppermute | solution.py:495
  72.4 1.3 %up_gradient.1 = f32[64,2048]{1,0:T(8,128)} custom-call(f32[96,128]{1,0:T(8,128)S(1)} %add.34.low_ref, bf16[192,2048]{1,0:T(8,128)(2,1)S(1)} %get-tuple-element.115.g_ref), custom_call_target="tpu_custom_call" | custom-call | flops 150994944 | bytes 1359872 | tf_op jit(solution)/shard_map/up_gradient/pallas_call | solution.py:55
  73.8 1.7 %collective-permute-done.30 = f32[1,48]{1,0:T(1,128)S(1)} collective-permute-done((f32[1,48]{1,0:T(1,128)S(1)}, f32[1,48]{1,0:T(1,128)S(1)}, u32[]{:S(2)}, u32[]{:S(2)}) %collective-permute-start.30) | collective-permute-done | bytes 224 | tf_op jit(solution)/shard_map/ppermute | solution.py:495
  (67 shorter events, 7.9 us)
Async XLA Ops:
  2.9 11.5 %collective-permute-start.2 = (bf16[48,2048]{1,0:T(8,128)(2,1)S(1)}, bf16[48,2048]{1,0:T(8,128)(2,1)S(1)}, u32[]{:S(2)}, u32[]{:S(2)}) collective-permute-start(bf16[48,2048]{1,0:T(8,128)(2,1)S(1)} %get-tuple-element.64.refs_0_), channel_id=1, source_target_pairs={{0,4},{8,0},{16,8},{24,16},{28,24},{20,28},{12,20},{4,12},{1,5},{9... | collective-permute-start | bytes 589832 | tf_op jit(solution)/shard_map/ppermute | solution.py:223
  5.9 8.5 %collective-permute-start.1 = (bf16[48,2048]{1,0:T(8,128)(2,1)S(1)}, bf16[48,2048]{1,0:T(8,128)(2,1)S(1)}, u32[]{:S(2)}, u32[]{:S(2)}) collective-permute-start(bf16[48,2048]{1,0:T(8,128)(2,1)S(1)} %get-tuple-element.64.refs_0_), channel_id=1, source_target_pairs={{0,8},{8,16},{16,24},{24,28},{28,20},{20,12},{12,4},{4,0},{1,9},{9... | collective-permute-start | bytes 589832 | tf_op jit(solution)/shard_map/ppermute | solution.py:223
  6.0 8.3 %collective-permute-start = (bf16[4,48,256]{2,1,0:T(8,128)(2,1)S(1)}, bf16[4,48,256]{2,1,0:T(8,128)(2,1)S(1)}, u32[]{:S(2)}, u32[]{:S(2)}) collective-permute-start(bf16[4,48,256]{2,1,0:T(8,128)(2,1)S(1)} %get-tuple-element.63), channel_id=1, source_target_pairs={{0,4},{4,0},{8,12},{12,8},{16,20},{20,16},{24,28},{28,24},{1,5},{5... | collective-permute-start | bytes 294920 | tf_op jit(solution)/shard_map/ppermute | solution.py:222
  14.4 11.9 %collective-permute-start.6 = (bf16[48,2048]{1,0:T(8,128)(2,1)S(1)}, bf16[48,2048]{1,0:T(8,128)(2,1)S(1)}, u32[]{:S(2)}, u32[]{:S(2)}) collective-permute-start(bf16[48,2048]{1,0:T(8,128)(2,1)S(1)} %get-tuple-element.76.refs_6_), channel_id=1, source_target_pairs={{0,8},{8,16},{16,24},{24,28},{28,20},{20,12},{12,4},{4,0},{1,9},{9... | collective-permute-start | bytes 589832 | tf_op jit(solution)/shard_map/ppermute | solution.py:244
  15.2 11.1 %collective-permute-start.7 = (bf16[48,2048]{1,0:T(8,128)(2,1)S(1)}, bf16[48,2048]{1,0:T(8,128)(2,1)S(1)}, u32[]{:S(2)}, u32[]{:S(2)}) collective-permute-start(bf16[48,2048]{1,0:T(8,128)(2,1)S(1)} %get-tuple-element.77.refs_1_), channel_id=1, source_target_pairs={{0,4},{8,0},{16,8},{24,16},{28,24},{20,28},{12,20},{4,12},{1,5},{9... | collective-permute-start | bytes 589832 | tf_op jit(solution)/shard_map/ppermute | solution.py:244
  16.5 9.8 %collective-permute-start.3 = (bf16[2,48,256]{2,1,0:T(8,128)(2,1)S(1)}, bf16[2,48,256]{2,1,0:T(8,128)(2,1)S(1)}, u32[]{:S(2)}, u32[]{:S(2)}) collective-permute-start(bf16[2,48,256]{2,1,0:T(8,128)(2,1)S(1)} %get-tuple-element.73), channel_id=1, source_target_pairs={{0,8},{4,12},{8,0},{12,4},{16,24},{20,28},{24,16},{28,20},{1,9},{5... | collective-permute-start | bytes 147464 | tf_op jit(solution)/shard_map/ppermute | solution.py:264
  17.2 9.1 %collective-permute-start.4 = (bf16[2,48,256]{2,1,0:T(8,128)(2,1)S(1)}, bf16[2,48,256]{2,1,0:T(8,128)(2,1)S(1)}, u32[]{:S(2)}, u32[]{:S(2)}) collective-permute-start(bf16[2,48,256]{2,1,0:T(8,128)(2,1)S(1)} %get-tuple-element.74), channel_id=1, source_target_pairs={{0,16},{4,20},{8,24},{12,28},{16,0},{20,4},{24,8},{28,12},{1,17},{... | collective-permute-start | bytes 147464 | tf_op jit(solution)/shard_map/ppermute | solution.py:264
  19.8 6.5 %collective-permute-start.5 = (bf16[2,48,256]{2,1,0:T(8,128)(2,1)S(1)}, bf16[2,48,256]{2,1,0:T(8,128)(2,1)S(1)}, u32[]{:S(2)}, u32[]{:S(2)}) collective-permute-start(bf16[2,48,256]{2,1,0:T(8,128)(2,1)S(1)} %get-tuple-element.75), channel_id=1, source_target_pairs={{0,24},{4,28},{8,16},{12,20},{16,8},{20,12},{24,0},{28,4},{1,25},{... | collective-permute-start | bytes 147464 | tf_op jit(solution)/shard_map/ppermute | solution.py:264
  20.9 15.3 %copy-start.2 = (bf16[1024,64]{0,1:T(8,128)(2,1)S(1)}, bf16[1024,64]{0,1:T(8,128)(2,1)}, u32[]{:S(2)}) copy-start(bf16[1024,64]{0,1:T(8,128)(2,1)} %param.14) | copy-start | bytes 393220
  26.3 5.7 %collective-permute-start.8 = (bf16[384,256]{1,0:T(8,128)(2,1)S(1)}, bf16[384,256]{1,0:T(8,128)(2,1)S(1)}, u32[]{:S(2)}, u32[]{:S(2)}) collective-permute-start(bf16[384,256]{1,0:T(8,128)(2,1)S(1)} %join.1.refs_0_), channel_id=1, source_target_pairs={{0,2},{1,3},{2,0},{3,1},{4,6},{5,7},{6,4},{7,5},{8,10},{9,11},{10,... | collective-permute-start | bytes 589832 | tf_op jit(solution)/shard_map/ppermute | solution.py:275
  27.9 5.7 %collective-permute-start.9 = (bf16[48,2048]{1,0:T(8,128)(2,1)S(1)}, bf16[48,2048]{1,0:T(8,128)(2,1)S(1)}, u32[]{:S(2)}, u32[]{:S(2)}) collective-permute-start(bf16[48,2048]{1,0:T(8,128)(2,1)S(1)} %collective-permute-done.6.refs_5_), channel_id=1, source_target_pairs={{0,8},{8,16},{16,24},{24,28},{28,20},{20,12},{12,4},{4,0},{1,9},{9... | collective-permute-start | bytes 589832 | tf_op jit(solution)/shard_map/ppermute | solution.py:244
  27.9 5.7 %collective-permute-start.10 = (bf16[48,2048]{1,0:T(8,128)(2,1)S(1)}, bf16[48,2048]{1,0:T(8,128)(2,1)S(1)}, u32[]{:S(2)}, u32[]{:S(2)}) collective-permute-start(bf16[48,2048]{1,0:T(8,128)(2,1)S(1)} %collective-permute-done.7.refs_2_), channel_id=1, source_target_pairs={{0,4},{8,0},{16,8},{24,16},{28,24},{20,28},{12,20},{4,12},{1,5},{9... | collective-permute-start | bytes 589832 | tf_op jit(solution)/shard_map/ppermute | solution.py:244
  33.6 2.6 %collective-permute-start.11 = (bf16[384,256]{1,0:T(8,128)(2,1)S(1)}, bf16[384,256]{1,0:T(8,128)(2,1)S(1)}, u32[]{:S(2)}, u32[]{:S(2)}) collective-permute-start(bf16[384,256]{1,0:T(8,128)(2,1)S(1)} %join.1.refs_0_), channel_id=1, source_target_pairs={{0,1},{1,0},{2,3},{3,2},{4,5},{5,4},{6,7},{7,6},{8,9},{9,8},{10,11... | collective-permute-start | bytes 589832 | tf_op jit(solution)/shard_map/ppermute | solution.py:277
  33.6 2.6 %collective-permute-start.12 = (bf16[384,256]{1,0:T(8,128)(2,1)S(1)}, bf16[384,256]{1,0:T(8,128)(2,1)S(1)}, u32[]{:S(2)}, u32[]{:S(2)}) collective-permute-start(bf16[384,256]{1,0:T(8,128)(2,1)S(1)} %collective-permute-done.8.refs_2_), channel_id=1, source_target_pairs={{0,1},{1,0},{2,3},{3,2},{4,5},{5,4},{6,7},{7,6},{8,9},{9,8},{10,11... | collective-permute-start | bytes 589832 | tf_op jit(solution)/shard_map/ppermute | solution.py:277
  34.1 6.7 %collective-permute-start.16 = (bf16[24,2048]{1,0:T(8,128)(2,1)S(1)}, bf16[24,2048]{1,0:T(8,128)(2,1)S(1)}, u32[]{:S(2)}, u32[]{:S(2)}) collective-permute-start(bf16[24,2048]{1,0:T(8,128)(2,1)S(1)} %slice.65), channel_id=1, source_target_pairs={{0,4},{8,0},{16,8},{24,16},{28,24},{20,28},{12,20},{4,12},{1,5},{9... | collective-permute-start | bytes 294920 | tf_op jit(solution)/shard_map/ppermute | solution.py:282
  36.2 4.6 %collective-permute-start.15 = (bf16[24,2048]{1,0:T(8,128)(2,1)S(1)}, bf16[24,2048]{1,0:T(8,128)(2,1)S(1)}, u32[]{:S(2)}, u32[]{:S(2)}) collective-permute-start(bf16[24,2048]{1,0:T(8,128)(2,1)S(1)} %slice.64), channel_id=1, source_target_pairs={{0,8},{8,16},{16,24},{24,28},{28,20},{20,12},{12,4},{4,0},{1,9},{9... | collective-permute-start | bytes 294920 | tf_op jit(solution)/shard_map/ppermute | solution.py:281
  38.8 4.7 %collective-permute-start.14 = (bf16[24,2048]{1,0:T(8,128)(2,1)S(1)}, bf16[24,2048]{1,0:T(8,128)(2,1)S(1)}, u32[]{:S(2)}, u32[]{:S(2)}) collective-permute-start(bf16[24,2048]{1,0:T(8,128)(2,1)S(1)} %get-tuple-element.122), channel_id=1, source_target_pairs={{0,4},{8,0},{16,8},{24,16},{28,24},{20,28},{12,20},{4,12},{1,5},{9... | collective-permute-start | bytes 294920 | tf_op jit(solution)/shard_map/ppermute | solution.py:321
  40.8 4.6 %collective-permute-start.13 = (bf16[24,2048]{1,0:T(8,128)(2,1)S(1)}, bf16[24,2048]{1,0:T(8,128)(2,1)S(1)}, u32[]{:S(2)}, u32[]{:S(2)}) collective-permute-start(bf16[24,2048]{1,0:T(8,128)(2,1)S(1)} %get-tuple-element.124), channel_id=1, source_target_pairs={{0,8},{8,16},{16,24},{24,28},{28,20},{20,12},{12,4},{4,0},{1,9},{9... | collective-permute-start | bytes 294920 | tf_op jit(solution)/shard_map/ppermute | solution.py:321
  45.5 6.0 %collective-permute-start.17 = (bf16[48,2048]{1,0:T(8,128)(2,1)S(1)}, bf16[48,2048]{1,0:T(8,128)(2,1)S(1)}, u32[]{:S(2)}, u32[]{:S(2)}) collective-permute-start(bf16[48,2048]{1,0:T(8,128)(2,1)S(1)} %get-tuple-element.92), channel_id=1, source_target_pairs={{0,8},{8,16},{16,24},{24,28},{28,20},{20,12},{12,4},{4,0},{1,9},{9... | collective-permute-start | bytes 589832 | tf_op jit(solution)/shard_map/ppermute | solution.py:440
  45.6 6.0 %collective-permute-start.18 = (bf16[48,2048]{1,0:T(8,128)(2,1)S(1)}, bf16[48,2048]{1,0:T(8,128)(2,1)S(1)}, u32[]{:S(2)}, u32[]{:S(2)}) collective-permute-start(bf16[48,2048]{1,0:T(8,128)(2,1)S(1)} %get-tuple-element.93), channel_id=1, source_target_pairs={{0,4},{8,0},{16,8},{24,16},{28,24},{20,28},{12,20},{4,12},{1,5},{9... | collective-permute-start | bytes 589832 | tf_op jit(solution)/shard_map/ppermute | solution.py:441
  47.6 5.0 %collective-permute-start.20 = (f32[192,128]{1,0:T(8,128)S(1)}, f32[192,128]{1,0:T(8,128)S(1)}, u32[]{:S(2)}, u32[]{:S(2)}) collective-permute-start(f32[192,128]{1,0:T(8,128)S(1)} %get-tuple-element.95.low_ref), channel_id=1, source_target_pairs={{0,4},{4,0},{8,12},{12,8},{16,20},{20,16},{24,28},{28,24},{1,5},{5... | collective-permute-start | bytes 294920 | tf_op jit(solution)/shard_map/ppermute | solution.py:322
  48.4 4.2 %collective-permute-start.19 = (bf16[96,1152]{1,0:T(8,128)(2,1)S(1)}, bf16[96,1152]{1,0:T(8,128)(2,1)S(1)}, u32[]{:S(2)}, u32[]{:S(2)}) collective-permute-start(bf16[96,1152]{1,0:T(8,128)(2,1)S(1)} %get-tuple-element.94), channel_id=1, source_target_pairs={{0,1},{1,0},{2,3},{3,2},{4,5},{5,4},{6,7},{7,6},{8,9},{9,8},{10,11... | collective-permute-start | bytes 663560 | tf_op jit(solution)/shard_map/ppermute | solution.py:396
  52.6 5.9 %collective-permute-start.21 = (bf16[48,2048]{1,0:T(8,128)(2,1)S(1)}, bf16[48,2048]{1,0:T(8,128)(2,1)S(1)}, u32[]{:S(2)}, u32[]{:S(2)}) collective-permute-start(bf16[48,2048]{1,0:T(8,128)(2,1)S(1)} %get-tuple-element.96), channel_id=1, source_target_pairs={{0,8},{8,16},{16,24},{24,28},{28,20},{20,12},{12,4},{4,0},{1,9},{9... | collective-permute-start | bytes 589832 | tf_op jit(solution)/shard_map/ppermute | solution.py:440
  53.3 6.0 %collective-permute-start.22 = (bf16[48,2048]{1,0:T(8,128)(2,1)S(1)}, bf16[48,2048]{1,0:T(8,128)(2,1)S(1)}, u32[]{:S(2)}, u32[]{:S(2)}) collective-permute-start(bf16[48,2048]{1,0:T(8,128)(2,1)S(1)} %get-tuple-element.97), channel_id=1, source_target_pairs={{0,4},{8,0},{16,8},{24,16},{28,24},{20,28},{12,20},{4,12},{1,5},{9... | collective-permute-start | bytes 589832 | tf_op jit(solution)/shard_map/ppermute | solution.py:441
  55.1 6.4 %collective-permute-start.26 = (f32[96,128]{1,0:T(8,128)S(1)}, f32[96,128]{1,0:T(8,128)S(1)}, u32[]{:S(2)}, u32[]{:S(2)}) collective-permute-start(f32[96,128]{1,0:T(8,128)S(1)} %compact.1.low_ref), channel_id=1, source_target_pairs={{0,16},{4,20},{8,24},{12,28},{16,0},{20,4},{24,8},{28,12},{1,17},{... | collective-permute-start | bytes 147464 | tf_op jit(solution)/shard_map/ppermute | solution.py:446
  57.9 6.0 %collective-permute-start.25 = (bf16[96,1152]{1,0:T(8,128)(2,1)S(1)}, bf16[96,1152]{1,0:T(8,128)(2,1)S(1)}, u32[]{:S(2)}, u32[]{:S(2)}) collective-permute-start(bf16[96,1152]{1,0:T(8,128)(2,1)S(1)} %add.56.a_ref), channel_id=1, source_target_pairs={{0,2},{1,3},{2,0},{3,1},{4,6},{5,7},{6,4},{7,5},{8,10},{9,11},{10,... | collective-permute-start | bytes 663560 | tf_op jit(solution)/shard_map/ppermute | solution.py:403
  59.4 9.9 %collective-permute-start.23 = (bf16[48,2048]{1,0:T(8,128)(2,1)S(1)}, bf16[48,2048]{1,0:T(8,128)(2,1)S(1)}, u32[]{:S(2)}, u32[]{:S(2)}) collective-permute-start(bf16[48,2048]{1,0:T(8,128)(2,1)S(1)} %get-tuple-element.98), channel_id=1, source_target_pairs={{0,8},{8,16},{16,24},{24,28},{28,20},{20,12},{12,4},{4,0},{1,9},{9... | collective-permute-start | bytes 589832 | tf_op jit(solution)/shard_map/ppermute | solution.py:440
  61.5 7.8 %collective-permute-start.24 = (bf16[48,2048]{1,0:T(8,128)(2,1)S(1)}, bf16[48,2048]{1,0:T(8,128)(2,1)S(1)}, u32[]{:S(2)}, u32[]{:S(2)}) collective-permute-start(bf16[48,2048]{1,0:T(8,128)(2,1)S(1)} %get-tuple-element.99), channel_id=1, source_target_pairs={{0,4},{8,0},{16,8},{24,16},{28,24},{20,28},{12,20},{4,12},{1,5},{9... | collective-permute-start | bytes 589832 | tf_op jit(solution)/shard_map/ppermute | solution.py:441
  64.2 5.2 %collective-permute-start.28 = (f32[96,128]{1,0:T(8,128)S(1)}, f32[96,128]{1,0:T(8,128)S(1)}, u32[]{:S(2)}, u32[]{:S(2)}) collective-permute-start(f32[96,128]{1,0:T(8,128)S(1)} %get-tuple-element.106), channel_id=1, source_target_pairs={{0,8},{4,12},{8,0},{12,4},{16,24},{20,28},{24,16},{28,20},{1,9},{5... | collective-permute-start | bytes 147464 | tf_op jit(solution)/shard_map/ppermute | solution.py:414
  66.2 1.5 %collective-permute-start.27 = (bf16[96,1152]{1,0:T(8,128)(2,1)S(1)}, bf16[96,1152]{1,0:T(8,128)(2,1)S(1)}, u32[]{:S(2)}, u32[]{:S(2)}) collective-permute-start(bf16[96,1152]{1,0:T(8,128)(2,1)S(1)} %get-tuple-element.104.a_ref), channel_id=1, source_target_pairs={{0,1},{1,0},{2,3},{3,2},{4,5},{5,4},{6,7},{7,6},{8,9},{9,8},{10,11... | collective-permute-start | bytes 663560 | tf_op jit(solution)/shard_map/ppermute | solution.py:408
  70.8 1.1 %collective-permute-start.29 = (f32[1,48]{1,0:T(1,128)S(1)}, f32[1,48]{1,0:T(1,128)S(1)}, u32[]{:S(2)}, u32[]{:S(2)}) collective-permute-start(f32[1,48]{1,0:T(1,128)S(1)} %get-tuple-element.116), channel_id=1, source_target_pairs={{0,1},{1,0},{2,3},{3,2},{4,5},{5,4},{6,7},{7,6},{8,9},{9,8},{10,11... | collective-permute-start | bytes 584 | tf_op jit(solution)/shard_map/ppermute | solution.py:495
  71.9 3.5 %collective-permute-start.30 = (f32[1,48]{1,0:T(1,128)S(1)}, f32[1,48]{1,0:T(1,128)S(1)}, u32[]{:S(2)}, u32[]{:S(2)}) collective-permute-start(f32[1,48]{1,0:T(1,128)S(1)} %add.35), channel_id=1, source_target_pairs={{0,2},{1,3},{2,0},{3,1},{4,6},{5,7},{6,4},{7,5},{8,10},{9,11},{10,... | collective-permute-start | bytes 584 | tf_op jit(solution)/shard_map/ppermute | solution.py:495
  (5 other events, 57.0 us)

commit v5 on v4

--- a/solution.py
+++ b/solution.py
@@ -102,6 +102,7 @@
         copy(i).start()
     token_ref[...] = jnp.zeros_like(token_ref)
     column_block = lax.broadcasted_iota(I32, (block, 128), 1) // per
+    table = tree_levels(lax.broadcasted_iota(I32, (block, 128), 1) % 16)
 
     @pl.loop(0, chunks)
     def _(i):
@@ -109,10 +110,17 @@
         absmax = absmax_ref[pl.ds(pl.multiple_of(first + i * block, block), block), :]
         absmax = jnp.concatenate([absmax] * (128 // blocks), axis=1)
         copy(i).wait()
-        for c in range(cols // 128):
-            part = slice(c * 128, c * 128 + 128)
-            scale = jnp.take_along_axis(absmax, column_block + c * (128 // per), axis=1, mode="promise_in_bounds")
-            weight_ref[rows, part] = (tree_levels(codes[i, :, part]) * scale).astype(BF)
+        for c in range(0, cols // 128, 2):
+            values = []
+            for tile in (c, c + 1):
+                piece = codes[i, :, tile * 128 : (tile + 1) * 128]
+                scale = jnp.take_along_axis(absmax, column_block + tile * (128 // per), axis=1, mode="promise_in_bounds")
+                if tile % 4 == 1:
+                    level = jnp.take_along_axis(table, piece, axis=1, mode="promise_in_bounds")
+                else:
+                    level = tree_levels(piece)
+                values.append((level * scale).astype(BF))
+            weight_ref[rows, c * 128 : (c + 2) * 128] = jnp.concatenate(values, axis=1)
 
 
 def in_hbm(array):

time: 76.1 us -> 75.5 us (level)
  Pallas kernels: 22.6 us -> 21.2 us
  starting transfers between devices: 32.7 us -> 33.6 us
    pallas_call x13, Pallas kernels: 22.6 us -> 21.2 us  [call(): pl.pallas_call(kernel, out_shape=tuple(outs), in_specs=in_specs or [whole...]
    ppermute x1, starting transfers between devices: 0.78 us -> 1.62 us  [body(): low_across = lax.ppermute(low, 'seq', flip(n, 1))]
    ppermute x3, waiting for transfers between devices: 3.19 us -> 2.43 us  [body(): going = lax.ppermute(here, 'seq', ring(1))]
  transfers between devices with their start and end apart: 31 -> 31, of which waited for: 11 -> 12; matrix products, arithmetic and copies ran while one was open for 1% -> 1% of each run, Pallas kernels for 26% -> 24%
where the time goes in v5:
time: 75.5 us; the launch traced here: 75.3 us
  starting transfers between devices  33.6 us (45%)
  Pallas kernels  21.2 us (28%)
  waiting for transfers between devices  17.9 us (24%)
  between operations  1.57 us (2%)
  other arithmetic  0.79 us (1%)
    pallas_call x13, Pallas kernels, call(): pl.pallas_call(kernel, out_shape=tuple(outs), in_specs=in_specs or [whole...  21.2 us
    ppermute x3, starting transfers between devices, body(): lax.ppermute(pairs[k], 'seq', flip(n, 2 * k))  4.39 us
    ppermute x2, starting transfers between devices, hop(): lax.ppermute(coming, 'seq', ring(-1))  4.04 us
    ppermute x3, starting transfers between devices, body(): coming = lax.ppermute(there, 'seq', ring(-1))  3.74 us
    ppermute x1, starting transfers between devices, body(): lax.ppermute(grad, 'seq', ring(-1))  2.99 us
    ppermute x2, waiting for transfers between devices, body(): gate_part = gate_part + lax.ppermute(gate_part, 'tp', flip(tp, bit))  2.67 us
    ppermute x3, starting transfers between devices, body(): going = lax.ppermute(here, 'seq', ring(1))  2.62 us
    ppermute x1, starting transfers between devices, body(): low_terms = (low_live, lax.ppermute(low_live, 'seq', flip(n, half)))  2.53 us
  transfers between devices with their start and end apart: 31, of which 12 were waited for; matrix products, arithmetic and copies ran while one was open for 1% of the time, Pallas kernels for 24%

profile of v5, /device:TPU:0, one launch (start us, length us, event | category | flops | bytes accessed | tf_op | source)
XLA Modules:
  0.0 75.3 jit_solution(1778841740156817081)
XLA Ops:
  1.3 1.6 %prepare.1 = (bf16[4,48,256]{2,1,0:T(8,128)(2,1)S(1)}, bf16[4,48,256]{2,1,0:T(8,128)(2,1)S(1)}, bf16[48,2048]{1,0:T(8,128)(2,1)S(1)}, bf16[48,2048]{1,0:T(8,128)(2,1)S(1)}) custom-call(s32[1]{0:T(128)S(6)} %copy.17.counts_ref, s32[1,48]{1,0:T(1,128)} %bitcast.36, f32[1,48]{1,0:T(1,128)} %bitcast.38, bf16[48,8192]{1,0:T(8,128)(2,1)} %attention_ref.1, ...), custom_call_target="tpu_custom_call" | custom-call | bytes 2163076 | tf_op jit(solution)/shard_map/prepare/pallas_call | solution.py:55
  2.9 3.0 %collective-permute-start.2 = (bf16[48,2048]{1,0:T(8,128)(2,1)S(1)}, bf16[48,2048]{1,0:T(8,128)(2,1)S(1)}, u32[]{:S(2)}, u32[]{:S(2)}) collective-permute-start(bf16[48,2048]{1,0:T(8,128)(2,1)S(1)} %get-tuple-element.64.refs_0_), channel_id=1, source_target_pairs={{0,4},{8,0},{16,8},{24,16},{28,24},{20,28},{12,20},{4,12},{1,5},{9... | collective-permute-start | bytes 589832 | tf_op jit(solution)/shard_map/ppermute | solution.py:231
  6.0 1.9 %collective-permute-start = (bf16[4,48,256]{2,1,0:T(8,128)(2,1)S(1)}, bf16[4,48,256]{2,1,0:T(8,128)(2,1)S(1)}, u32[]{:S(2)}, u32[]{:S(2)}) collective-permute-start(bf16[4,48,256]{2,1,0:T(8,128)(2,1)S(1)} %get-tuple-element.63), channel_id=1, source_target_pairs={{0,4},{4,0},{8,12},{12,8},{16,20},{20,16},{24,28},{28,24},{1,5},{5... | collective-permute-start | bytes 294920 | tf_op jit(solution)/shard_map/ppermute | solution.py:230
  8.1 4.6 %dequantize.2 = (bf16[512,2048]{1,0:T(8,128)(2,1)S(1)}, f32[8,128]{1,0:T(8,128)S(1)}) custom-call(s32[1024,2048]{1,0:T(8,128)} %codes_hbm.3, f32[1024,32]{1,0:T(8,128)S(1)} %copy.15.absmax_ref), custom_call_target="tpu_custom_call" | custom-call | flops 104857600 | bytes 10620928 | tf_op jit(solution)/shard_map/dequantize/pallas_call | solution.py:55
  12.7 1.6 %collective-permute-done.across_ref = bf16[4,48,256]{2,1,0:T(8,128)(2,1)S(1)} collective-permute-done((bf16[4,48,256]{2,1,0:T(8,128)(2,1)S(1)}, bf16[4,48,256]{2,1,0:T(8,128)(2,1)S(1)}, u32[]{:S(2)}, u32[]{:S(2)}) %collective-permute-start) | collective-permute-done | bytes 98336 | tf_op jit(solution)/shard_map/ppermute | solution.py:230
  14.5 2.0 %collective-permute-start.7 = (bf16[48,2048]{1,0:T(8,128)(2,1)S(1)}, bf16[48,2048]{1,0:T(8,128)(2,1)S(1)}, u32[]{:S(2)}, u32[]{:S(2)}) collective-permute-start(bf16[48,2048]{1,0:T(8,128)(2,1)S(1)} %get-tuple-element.77.refs_1_), channel_id=1, source_target_pairs={{0,4},{8,0},{16,8},{24,16},{28,24},{20,28},{12,20},{4,12},{1,5},{9... | collective-permute-start | bytes 589832 | tf_op jit(solution)/shard_map/ppermute | solution.py:252
  16.6 2.9 %collective-permute-start.4 = (bf16[2,48,256]{2,1,0:T(8,128)(2,1)S(1)}, bf16[2,48,256]{2,1,0:T(8,128)(2,1)S(1)}, u32[]{:S(2)}, u32[]{:S(2)}) collective-permute-start(bf16[2,48,256]{2,1,0:T(8,128)(2,1)S(1)} %get-tuple-element.74), channel_id=1, source_target_pairs={{0,16},{4,20},{8,24},{12,28},{16,0},{20,4},{24,8},{28,12},{1,17},{... | collective-permute-start | bytes 147464 | tf_op jit(solution)/shard_map/ppermute | solution.py:272
  19.5 1.4 %collective-permute-start.5 = (bf16[2,48,256]{2,1,0:T(8,128)(2,1)S(1)}, bf16[2,48,256]{2,1,0:T(8,128)(2,1)S(1)}, u32[]{:S(2)}, u32[]{:S(2)}) collective-permute-start(bf16[2,48,256]{2,1,0:T(8,128)(2,1)S(1)} %get-tuple-element.75), channel_id=1, source_target_pairs={{0,24},{4,28},{8,16},{12,20},{16,8},{20,12},{24,0},{28,4},{1,25},{... | collective-permute-start | bytes 147464 | tf_op jit(solution)/shard_map/ppermute | solution.py:272
  20.9 4.6 %dequantize.3 = (bf16[512,2048]{1,0:T(8,128)(2,1)S(1)}, f32[8,128]{1,0:T(8,128)S(1)}) custom-call(s32[1024,2048]{1,0:T(8,128)} %codes_hbm.3, f32[1024,32]{1,0:T(8,128)S(1)} %copy.15.absmax_ref, f32[8,128]{1,0:T(8,128)S(1)} %get-tuple-element.70.refs_0_), custom_call_target="tpu_custom_call" | custom-call | flops 104857600 | bytes 10625024 | tf_op jit(solution)/shard_map/dequantize/pallas_call | solution.py:55
  25.6 1.6 %collective-permute-start.8 = (bf16[384,256]{1,0:T(8,128)(2,1)S(1)}, bf16[384,256]{1,0:T(8,128)(2,1)S(1)}, u32[]{:S(2)}, u32[]{:S(2)}) collective-permute-start(bf16[384,256]{1,0:T(8,128)(2,1)S(1)} %join.1.refs_0_), channel_id=1, source_target_pairs={{0,2},{1,3},{2,0},{3,1},{4,6},{5,7},{6,4},{7,5},{8,10},{9,11},{10,... | collective-permute-start | bytes 589832 | tf_op jit(solution)/shard_map/ppermute | solution.py:283
  27.2 2.0 %collective-permute-start.10 = (bf16[48,2048]{1,0:T(8,128)(2,1)S(1)}, bf16[48,2048]{1,0:T(8,128)(2,1)S(1)}, u32[]{:S(2)}, u32[]{:S(2)}) collective-permute-start(bf16[48,2048]{1,0:T(8,128)(2,1)S(1)} %collective-permute-done.7.refs_2_), channel_id=1, source_target_pairs={{0,4},{8,0},{16,8},{24,16},{28,24},{20,28},{12,20},{4,12},{1,5},{9... | collective-permute-start | bytes 589832 | tf_op jit(solution)/shard_map/ppermute | solution.py:252
  29.2 2.1 %collective-permute-done.8.refs_2_ = bf16[384,256]{1,0:T(8,128)(2,1)S(1)} collective-permute-done((bf16[384,256]{1,0:T(8,128)(2,1)S(1)}, bf16[384,256]{1,0:T(8,128)(2,1)S(1)}, u32[]{:S(2)}, u32[]{:S(2)}) %collective-permute-start.8) | collective-permute-done | bytes 196640 | tf_op jit(solution)/shard_map/ppermute | solution.py:283
  31.4 1.5 %collective-permute-done.9.refs_4_ = bf16[48,2048]{1,0:T(8,128)(2,1)S(1)} collective-permute-done((bf16[48,2048]{1,0:T(8,128)(2,1)S(1)}, bf16[48,2048]{1,0:T(8,128)(2,1)S(1)}, u32[]{:S(2)}, u32[]{:S(2)}) %collective-permute-start.9) | collective-permute-done | bytes 196640 | tf_op jit(solution)/shard_map/ppermute | solution.py:252
  33.4 2.1 %collective-permute-start.16 = (bf16[24,2048]{1,0:T(8,128)(2,1)S(1)}, bf16[24,2048]{1,0:T(8,128)(2,1)S(1)}, u32[]{:S(2)}, u32[]{:S(2)}) collective-permute-start(bf16[24,2048]{1,0:T(8,128)(2,1)S(1)} %slice.65), channel_id=1, source_target_pairs={{0,4},{8,0},{16,8},{24,16},{28,24},{20,28},{12,20},{4,12},{1,5},{9... | collective-permute-start | bytes 294920 | tf_op jit(solution)/shard_map/ppermute | solution.py:290
  35.5 2.5 %forward.1 = (bf16[8,48,2048]{2,1,0:T(8,128)(2,1)S(1)}, f32[192,128]{1,0:T(8,128)S(1)}) custom-call(bf16[64,1024]{1,0:T(8,128)(2,1)S(1)} %bitcast.34, bf16[64,2048]{1,0:T(8,128)(2,1)S(1)} %copy-done.1, bf16[512,2048]{1,0:T(8,128)(2,1)S(1)} %get-tuple-element.61.w0_ref, bf16[512,2048]{1,0:T(8,128)(2,1)S(1)} %get-tuple-element.71.w1_ref, ...), custom_call_target="tpu_custom_call" | custom-call | flops 1610612736 | bytes 7045120 | tf_op jit(solution)/shard_map/forward/pallas_call | solution.py:55
  38.1 2.1 %collective-permute-start.14 = (bf16[24,2048]{1,0:T(8,128)(2,1)S(1)}, bf16[24,2048]{1,0:T(8,128)(2,1)S(1)}, u32[]{:S(2)}, u32[]{:S(2)}) collective-permute-start(bf16[24,2048]{1,0:T(8,128)(2,1)S(1)} %get-tuple-element.122), channel_id=1, source_target_pairs={{0,4},{8,0},{16,8},{24,16},{28,24},{20,28},{12,20},{4,12},{1,5},{9... | collective-permute-start | bytes 294920 | tf_op jit(solution)/shard_map/ppermute | solution.py:329
  40.1 2.5 %backward.1 = (f32[96,1152]{1,0:T(8,128)S(1)}, bf16[96,1152]{1,0:T(8,128)(2,1)S(1)}, bf16[192,2048]{1,0:T(8,128)(2,1)S(1)}, bf16[384,192]{1,0:T(8,128)(2,1)S(1)}) custom-call(bf16[64,2048]{1,0:T(8,128)(2,1)S(1)} %copy-done.1, bf16[512,2048]{1,0:T(8,128)(2,1)S(1)} %get-tuple-element.61.w0_ref, bf16[512,2048]{1,0:T(8,128)(2,1)S(1)} %get-tuple-element.71.w1_ref, ...), custom_call_target="tpu_custom_call" | custom-call | flops 805306368 | bytes 7626752 | tf_op jit(solution)/shard_map/backward/pallas_call | solution.py:55
  42.7 2.0 %collective-permute-done.13 = bf16[24,2048]{1,0:T(8,128)(2,1)S(1)} collective-permute-done((bf16[24,2048]{1,0:T(8,128)(2,1)S(1)}, bf16[24,2048]{1,0:T(8,128)(2,1)S(1)}, u32[]{:S(2)}, u32[]{:S(2)}) %collective-permute-start.13) | collective-permute-done | bytes 98336 | tf_op jit(solution)/shard_map/ppermute | solution.py:329
  44.9 2.0 %collective-permute-start.18 = (bf16[48,2048]{1,0:T(8,128)(2,1)S(1)}, bf16[48,2048]{1,0:T(8,128)(2,1)S(1)}, u32[]{:S(2)}, u32[]{:S(2)}) collective-permute-start(bf16[48,2048]{1,0:T(8,128)(2,1)S(1)} %get-tuple-element.93), channel_id=1, source_target_pairs={{0,4},{8,0},{16,8},{24,16},{28,24},{20,28},{12,20},{4,12},{1,5},{9... | collective-permute-start | bytes 589832 | tf_op jit(solution)/shard_map/ppermute | solution.py:449
  46.9 1.6 %collective-permute-start.20 = (f32[192,128]{1,0:T(8,128)S(1)}, f32[192,128]{1,0:T(8,128)S(1)}, u32[]{:S(2)}, u32[]{:S(2)}) collective-permute-start(f32[192,128]{1,0:T(8,128)S(1)} %get-tuple-element.95.low_ref), channel_id=1, source_target_pairs={{0,4},{4,0},{8,12},{12,8},{16,20},{20,16},{24,28},{28,24},{1,5},{5... | collective-permute-start | bytes 294920 | tf_op jit(solution)/shard_map/ppermute | solution.py:330
  48.5 2.4 %collective-permute-done.17 = bf16[48,2048]{1,0:T(8,128)(2,1)S(1)} collective-permute-done((bf16[48,2048]{1,0:T(8,128)(2,1)S(1)}, bf16[48,2048]{1,0:T(8,128)(2,1)S(1)}, u32[]{:S(2)}, u32[]{:S(2)}) %collective-permute-start.17) | collective-permute-done | bytes 196640 | tf_op jit(solution)/shard_map/ppermute | solution.py:448
  52.3 1.7 %collective-permute-start.22 = (bf16[48,2048]{1,0:T(8,128)(2,1)S(1)}, bf16[48,2048]{1,0:T(8,128)(2,1)S(1)}, u32[]{:S(2)}, u32[]{:S(2)}) collective-permute-start(bf16[48,2048]{1,0:T(8,128)(2,1)S(1)} %get-tuple-element.97), channel_id=1, source_target_pairs={{0,4},{8,0},{16,8},{24,16},{28,24},{20,28},{12,20},{4,12},{1,5},{9... | collective-permute-start | bytes 589832 | tf_op jit(solution)/shard_map/ppermute | solution.py:449
  54.5 2.5 %collective-permute-start.26 = (f32[96,128]{1,0:T(8,128)S(1)}, f32[96,128]{1,0:T(8,128)S(1)}, u32[]{:S(2)}, u32[]{:S(2)}) collective-permute-start(f32[96,128]{1,0:T(8,128)S(1)} %compact.1.low_ref), channel_id=1, source_target_pairs={{0,16},{4,20},{8,24},{12,28},{16,0},{20,4},{24,8},{28,12},{1,17},{... | collective-permute-start | bytes 147464 | tf_op jit(solution)/shard_map/ppermute | solution.py:454
  58.6 2.3 %collective-permute-start.23 = (bf16[48,2048]{1,0:T(8,128)(2,1)S(1)}, bf16[48,2048]{1,0:T(8,128)(2,1)S(1)}, u32[]{:S(2)}, u32[]{:S(2)}) collective-permute-start(bf16[48,2048]{1,0:T(8,128)(2,1)S(1)} %get-tuple-element.98), channel_id=1, source_target_pairs={{0,8},{8,16},{16,24},{24,28},{28,20},{20,12},{12,4},{4,0},{1,9},{9... | collective-permute-start | bytes 589832 | tf_op jit(solution)/shard_map/ppermute | solution.py:448
  61.0 2.3 %collective-permute-done.25.b_ref = bf16[96,1152]{1,0:T(8,128)(2,1)S(1)} collective-permute-done((bf16[96,1152]{1,0:T(8,128)(2,1)S(1)}, bf16[96,1152]{1,0:T(8,128)(2,1)S(1)}, u32[]{:S(2)}, u32[]{:S(2)}) %collective-permute-start.25) | collective-permute-done | bytes 221216 | tf_op jit(solution)/shard_map/ppermute | solution.py:411
  63.5 2.1 %collective-permute-start.28 = (f32[96,128]{1,0:T(8,128)S(1)}, f32[96,128]{1,0:T(8,128)S(1)}, u32[]{:S(2)}, u32[]{:S(2)}) collective-permute-start(f32[96,128]{1,0:T(8,128)S(1)} %get-tuple-element.106), channel_id=1, source_target_pairs={{0,8},{4,12},{8,0},{12,4},{16,24},{20,28},{24,16},{28,20},{1,9},{5... | collective-permute-start | bytes 147464 | tf_op jit(solution)/shard_map/ppermute | solution.py:422
  65.6 1.5 %collective-permute-done.27.b_ref = bf16[96,1152]{1,0:T(8,128)(2,1)S(1)} collective-permute-done((bf16[96,1152]{1,0:T(8,128)(2,1)S(1)}, bf16[96,1152]{1,0:T(8,128)(2,1)S(1)}, u32[]{:S(2)}, u32[]{:S(2)}) %collective-permute-start.27) | collective-permute-done | bytes 221216 | tf_op jit(solution)/shard_map/ppermute | solution.py:416
  67.1 1.6 %last.1 = (bf16[384,1024]{1,0:T(8,128)(2,1)}, f32[64,1024]{1,0:T(8,128)}, f32[8,128]{1,0:T(8,128)S(1)}) custom-call(bf16[96,1152]{1,0:T(8,128)(2,1)S(1)} %get-tuple-element.104.a_ref, bf16[96,1152]{1,0:T(8,128)(2,1)S(1)} %collective-permute-done.27.b_ref, bf16[384,192]{1,0:T(8,128)(2,1)S(1)} %get-tuple-element.103.where_ref, ...), custom_call_target="tpu_custom_call" | custom-call | bytes 2428928 | tf_op jit(solution)/shard_map/last/pallas_call | solution.py:55
  68.7 1.5 %home.1 = (bf16[192,2048]{1,0:T(8,128)(2,1)}, f32[1,48]{1,0:T(1,128)S(1)}) custom-call(s32[1]{0:T(128)S(6)} %copy.17.counts_ref, s32[1,48]{1,0:T(1,128)S(1)} %bitcast.37, f32[1,48]{1,0:T(1,128)S(1)} %bitcast.39, bf16[192,2048]{1,0:T(8,128)(2,1)S(1)} %copy-done, bf16[48,2048]{1,0:T(8,128)(2,1)S(1)} %slice_bitcast_fusion.own_ref, ...), custom_call_target="tpu_custom_call" | custom-call | bytes 2363972 | tf_op jit(solution)/shard_map/home/pallas_call | solution.py:55
  70.3 1.0 %collective-permute-done.29 = f32[1,48]{1,0:T(1,128)S(1)} collective-permute-done((f32[1,48]{1,0:T(1,128)S(1)}, f32[1,48]{1,0:T(1,128)S(1)}, u32[]{:S(2)}, u32[]{:S(2)}) %collective-permute-start.29) | collective-permute-done | bytes 224 | tf_op jit(solution)/shard_map/ppermute | solution.py:503
  71.8 1.3 %up_gradient.1 = f32[64,2048]{1,0:T(8,128)} custom-call(f32[96,128]{1,0:T(8,128)S(1)} %add.34.low_ref, bf16[192,2048]{1,0:T(8,128)(2,1)S(1)} %get-tuple-element.115.g_ref), custom_call_target="tpu_custom_call" | custom-call | flops 150994944 | bytes 1359872 | tf_op jit(solution)/shard_map/up_gradient/pallas_call | solution.py:55
  73.1 1.7 %collective-permute-done.30 = f32[1,48]{1,0:T(1,128)S(1)} collective-permute-done((f32[1,48]{1,0:T(1,128)S(1)}, f32[1,48]{1,0:T(1,128)S(1)}, u32[]{:S(2)}, u32[]{:S(2)}) %collective-permute-start.30) | collective-permute-done | bytes 224 | tf_op jit(solution)/shard_map/ppermute | solution.py:503
  (67 shorter events, 6.3 us)
Async XLA Ops:
  2.9 11.5 %collective-permute-start.2 = (bf16[48,2048]{1,0:T(8,128)(2,1)S(1)}, bf16[48,2048]{1,0:T(8,128)(2,1)S(1)}, u32[]{:S(2)}, u32[]{:S(2)}) collective-permute-start(bf16[48,2048]{1,0:T(8,128)(2,1)S(1)} %get-tuple-element.64.refs_0_), channel_id=1, source_target_pairs={{0,4},{8,0},{16,8},{24,16},{28,24},{20,28},{12,20},{4,12},{1,5},{9... | collective-permute-start | bytes 589832 | tf_op jit(solution)/shard_map/ppermute | solution.py:231
  5.9 8.5 %collective-permute-start.1 = (bf16[48,2048]{1,0:T(8,128)(2,1)S(1)}, bf16[48,2048]{1,0:T(8,128)(2,1)S(1)}, u32[]{:S(2)}, u32[]{:S(2)}) collective-permute-start(bf16[48,2048]{1,0:T(8,128)(2,1)S(1)} %get-tuple-element.64.refs_0_), channel_id=1, source_target_pairs={{0,8},{8,16},{16,24},{24,28},{28,20},{20,12},{12,4},{4,0},{1,9},{9... | collective-permute-start | bytes 589832 | tf_op jit(solution)/shard_map/ppermute | solution.py:231
  6.0 8.3 %collective-permute-start = (bf16[4,48,256]{2,1,0:T(8,128)(2,1)S(1)}, bf16[4,48,256]{2,1,0:T(8,128)(2,1)S(1)}, u32[]{:S(2)}, u32[]{:S(2)}) collective-permute-start(bf16[4,48,256]{2,1,0:T(8,128)(2,1)S(1)} %get-tuple-element.63), channel_id=1, source_target_pairs={{0,4},{4,0},{8,12},{12,8},{16,20},{20,16},{24,28},{28,24},{1,5},{5... | collective-permute-start | bytes 294920 | tf_op jit(solution)/shard_map/ppermute | solution.py:230
  14.4 11.2 %collective-permute-start.6 = (bf16[48,2048]{1,0:T(8,128)(2,1)S(1)}, bf16[48,2048]{1,0:T(8,128)(2,1)S(1)}, u32[]{:S(2)}, u32[]{:S(2)}) collective-permute-start(bf16[48,2048]{1,0:T(8,128)(2,1)S(1)} %get-tuple-element.76.refs_6_), channel_id=1, source_target_pairs={{0,8},{8,16},{16,24},{24,28},{28,20},{20,12},{12,4},{4,0},{1,9},{9... | collective-permute-start | bytes 589832 | tf_op jit(solution)/shard_map/ppermute | solution.py:252
  14.5 11.1 %collective-permute-start.7 = (bf16[48,2048]{1,0:T(8,128)(2,1)S(1)}, bf16[48,2048]{1,0:T(8,128)(2,1)S(1)}, u32[]{:S(2)}, u32[]{:S(2)}) collective-permute-start(bf16[48,2048]{1,0:T(8,128)(2,1)S(1)} %get-tuple-element.77.refs_1_), channel_id=1, source_target_pairs={{0,4},{8,0},{16,8},{24,16},{28,24},{20,28},{12,20},{4,12},{1,5},{9... | collective-permute-start | bytes 589832 | tf_op jit(solution)/shard_map/ppermute | solution.py:252
  16.5 9.1 %collective-permute-start.3 = (bf16[2,48,256]{2,1,0:T(8,128)(2,1)S(1)}, bf16[2,48,256]{2,1,0:T(8,128)(2,1)S(1)}, u32[]{:S(2)}, u32[]{:S(2)}) collective-permute-start(bf16[2,48,256]{2,1,0:T(8,128)(2,1)S(1)} %get-tuple-element.73), channel_id=1, source_target_pairs={{0,8},{4,12},{8,0},{12,4},{16,24},{20,28},{24,16},{28,20},{1,9},{5... | collective-permute-start | bytes 147464 | tf_op jit(solution)/shard_map/ppermute | solution.py:272
  16.6 9.0 %collective-permute-start.4 = (bf16[2,48,256]{2,1,0:T(8,128)(2,1)S(1)}, bf16[2,48,256]{2,1,0:T(8,128)(2,1)S(1)}, u32[]{:S(2)}, u32[]{:S(2)}) collective-permute-start(bf16[2,48,256]{2,1,0:T(8,128)(2,1)S(1)} %get-tuple-element.74), channel_id=1, source_target_pairs={{0,16},{4,20},{8,24},{12,28},{16,0},{20,4},{24,8},{28,12},{1,17},{... | collective-permute-start | bytes 147464 | tf_op jit(solution)/shard_map/ppermute | solution.py:272
  19.5 6.1 %collective-permute-start.5 = (bf16[2,48,256]{2,1,0:T(8,128)(2,1)S(1)}, bf16[2,48,256]{2,1,0:T(8,128)(2,1)S(1)}, u32[]{:S(2)}, u32[]{:S(2)}) collective-permute-start(bf16[2,48,256]{2,1,0:T(8,128)(2,1)S(1)} %get-tuple-element.75), channel_id=1, source_target_pairs={{0,24},{4,28},{8,16},{12,20},{16,8},{20,12},{24,0},{28,4},{1,25},{... | collective-permute-start | bytes 147464 | tf_op jit(solution)/shard_map/ppermute | solution.py:272
  20.9 14.6 %copy-start.2 = (bf16[1024,64]{0,1:T(8,128)(2,1)S(1)}, bf16[1024,64]{0,1:T(8,128)(2,1)}, u32[]{:S(2)}) copy-start(bf16[1024,64]{0,1:T(8,128)(2,1)} %param.14) | copy-start | bytes 393220
  25.6 5.7 %collective-permute-start.8 = (bf16[384,256]{1,0:T(8,128)(2,1)S(1)}, bf16[384,256]{1,0:T(8,128)(2,1)S(1)}, u32[]{:S(2)}, u32[]{:S(2)}) collective-permute-start(bf16[384,256]{1,0:T(8,128)(2,1)S(1)} %join.1.refs_0_), channel_id=1, source_target_pairs={{0,2},{1,3},{2,0},{3,1},{4,6},{5,7},{6,4},{7,5},{8,10},{9,11},{10,... | collective-permute-start | bytes 589832 | tf_op jit(solution)/shard_map/ppermute | solution.py:283
  27.2 5.7 %collective-permute-start.9 = (bf16[48,2048]{1,0:T(8,128)(2,1)S(1)}, bf16[48,2048]{1,0:T(8,128)(2,1)S(1)}, u32[]{:S(2)}, u32[]{:S(2)}) collective-permute-start(bf16[48,2048]{1,0:T(8,128)(2,1)S(1)} %collective-permute-done.6.refs_5_), channel_id=1, source_target_pairs={{0,8},{8,16},{16,24},{24,28},{28,20},{20,12},{12,4},{4,0},{1,9},{9... | collective-permute-start | bytes 589832 | tf_op jit(solution)/shard_map/ppermute | solution.py:252
  27.2 5.7 %collective-permute-start.10 = (bf16[48,2048]{1,0:T(8,128)(2,1)S(1)}, bf16[48,2048]{1,0:T(8,128)(2,1)S(1)}, u32[]{:S(2)}, u32[]{:S(2)}) collective-permute-start(bf16[48,2048]{1,0:T(8,128)(2,1)S(1)} %collective-permute-done.7.refs_2_), channel_id=1, source_target_pairs={{0,4},{8,0},{16,8},{24,16},{28,24},{20,28},{12,20},{4,12},{1,5},{9... | collective-permute-start | bytes 589832 | tf_op jit(solution)/shard_map/ppermute | solution.py:252
  32.9 2.6 %collective-permute-start.11 = (bf16[384,256]{1,0:T(8,128)(2,1)S(1)}, bf16[384,256]{1,0:T(8,128)(2,1)S(1)}, u32[]{:S(2)}, u32[]{:S(2)}) collective-permute-start(bf16[384,256]{1,0:T(8,128)(2,1)S(1)} %join.1.refs_0_), channel_id=1, source_target_pairs={{0,1},{1,0},{2,3},{3,2},{4,5},{5,4},{6,7},{7,6},{8,9},{9,8},{10,11... | collective-permute-start | bytes 589832 | tf_op jit(solution)/shard_map/ppermute | solution.py:285
  32.9 2.6 %collective-permute-start.12 = (bf16[384,256]{1,0:T(8,128)(2,1)S(1)}, bf16[384,256]{1,0:T(8,128)(2,1)S(1)}, u32[]{:S(2)}, u32[]{:S(2)}) collective-permute-start(bf16[384,256]{1,0:T(8,128)(2,1)S(1)} %collective-permute-done.8.refs_2_), channel_id=1, source_target_pairs={{0,1},{1,0},{2,3},{3,2},{4,5},{5,4},{6,7},{7,6},{8,9},{9,8},{10,11... | collective-permute-start | bytes 589832 | tf_op jit(solution)/shard_map/ppermute | solution.py:285
  33.4 6.7 %collective-permute-start.16 = (bf16[24,2048]{1,0:T(8,128)(2,1)S(1)}, bf16[24,2048]{1,0:T(8,128)(2,1)S(1)}, u32[]{:S(2)}, u32[]{:S(2)}) collective-permute-start(bf16[24,2048]{1,0:T(8,128)(2,1)S(1)} %slice.65), channel_id=1, source_target_pairs={{0,4},{8,0},{16,8},{24,16},{28,24},{20,28},{12,20},{4,12},{1,5},{9... | collective-permute-start | bytes 294920 | tf_op jit(solution)/shard_map/ppermute | solution.py:290
  35.5 4.6 %collective-permute-start.15 = (bf16[24,2048]{1,0:T(8,128)(2,1)S(1)}, bf16[24,2048]{1,0:T(8,128)(2,1)S(1)}, u32[]{:S(2)}, u32[]{:S(2)}) collective-permute-start(bf16[24,2048]{1,0:T(8,128)(2,1)S(1)} %slice.64), channel_id=1, source_target_pairs={{0,8},{8,16},{16,24},{24,28},{28,20},{20,12},{12,4},{4,0},{1,9},{9... | collective-permute-start | bytes 294920 | tf_op jit(solution)/shard_map/ppermute | solution.py:289
  38.1 4.7 %collective-permute-start.14 = (bf16[24,2048]{1,0:T(8,128)(2,1)S(1)}, bf16[24,2048]{1,0:T(8,128)(2,1)S(1)}, u32[]{:S(2)}, u32[]{:S(2)}) collective-permute-start(bf16[24,2048]{1,0:T(8,128)(2,1)S(1)} %get-tuple-element.122), channel_id=1, source_target_pairs={{0,4},{8,0},{16,8},{24,16},{28,24},{20,28},{12,20},{4,12},{1,5},{9... | collective-permute-start | bytes 294920 | tf_op jit(solution)/shard_map/ppermute | solution.py:329
  40.1 4.6 %collective-permute-start.13 = (bf16[24,2048]{1,0:T(8,128)(2,1)S(1)}, bf16[24,2048]{1,0:T(8,128)(2,1)S(1)}, u32[]{:S(2)}, u32[]{:S(2)}) collective-permute-start(bf16[24,2048]{1,0:T(8,128)(2,1)S(1)} %get-tuple-element.124), channel_id=1, source_target_pairs={{0,8},{8,16},{16,24},{24,28},{28,20},{20,12},{12,4},{4,0},{1,9},{9... | collective-permute-start | bytes 294920 | tf_op jit(solution)/shard_map/ppermute | solution.py:329
  44.8 6.1 %collective-permute-start.17 = (bf16[48,2048]{1,0:T(8,128)(2,1)S(1)}, bf16[48,2048]{1,0:T(8,128)(2,1)S(1)}, u32[]{:S(2)}, u32[]{:S(2)}) collective-permute-start(bf16[48,2048]{1,0:T(8,128)(2,1)S(1)} %get-tuple-element.92), channel_id=1, source_target_pairs={{0,8},{8,16},{16,24},{24,28},{28,20},{20,12},{12,4},{4,0},{1,9},{9... | collective-permute-start | bytes 589832 | tf_op jit(solution)/shard_map/ppermute | solution.py:448
  44.9 6.0 %collective-permute-start.18 = (bf16[48,2048]{1,0:T(8,128)(2,1)S(1)}, bf16[48,2048]{1,0:T(8,128)(2,1)S(1)}, u32[]{:S(2)}, u32[]{:S(2)}) collective-permute-start(bf16[48,2048]{1,0:T(8,128)(2,1)S(1)} %get-tuple-element.93), channel_id=1, source_target_pairs={{0,4},{8,0},{16,8},{24,16},{28,24},{20,28},{12,20},{4,12},{1,5},{9... | collective-permute-start | bytes 589832 | tf_op jit(solution)/shard_map/ppermute | solution.py:449
  46.9 5.1 %collective-permute-start.20 = (f32[192,128]{1,0:T(8,128)S(1)}, f32[192,128]{1,0:T(8,128)S(1)}, u32[]{:S(2)}, u32[]{:S(2)}) collective-permute-start(f32[192,128]{1,0:T(8,128)S(1)} %get-tuple-element.95.low_ref), channel_id=1, source_target_pairs={{0,4},{4,0},{8,12},{12,8},{16,20},{20,16},{24,28},{28,24},{1,5},{5... | collective-permute-start | bytes 294920 | tf_op jit(solution)/shard_map/ppermute | solution.py:330
  48.5 3.5 %collective-permute-start.19 = (bf16[96,1152]{1,0:T(8,128)(2,1)S(1)}, bf16[96,1152]{1,0:T(8,128)(2,1)S(1)}, u32[]{:S(2)}, u32[]{:S(2)}) collective-permute-start(bf16[96,1152]{1,0:T(8,128)(2,1)S(1)} %get-tuple-element.94), channel_id=1, source_target_pairs={{0,1},{1,0},{2,3},{3,2},{4,5},{5,4},{6,7},{7,6},{8,9},{9,8},{10,11... | collective-permute-start | bytes 663560 | tf_op jit(solution)/shard_map/ppermute | solution.py:404
  52.0 5.9 %collective-permute-start.21 = (bf16[48,2048]{1,0:T(8,128)(2,1)S(1)}, bf16[48,2048]{1,0:T(8,128)(2,1)S(1)}, u32[]{:S(2)}, u32[]{:S(2)}) collective-permute-start(bf16[48,2048]{1,0:T(8,128)(2,1)S(1)} %get-tuple-element.96), channel_id=1, source_target_pairs={{0,8},{8,16},{16,24},{24,28},{28,20},{20,12},{12,4},{4,0},{1,9},{9... | collective-permute-start | bytes 589832 | tf_op jit(solution)/shard_map/ppermute | solution.py:448
  52.3 6.2 %collective-permute-start.22 = (bf16[48,2048]{1,0:T(8,128)(2,1)S(1)}, bf16[48,2048]{1,0:T(8,128)(2,1)S(1)}, u32[]{:S(2)}, u32[]{:S(2)}) collective-permute-start(bf16[48,2048]{1,0:T(8,128)(2,1)S(1)} %get-tuple-element.97), channel_id=1, source_target_pairs={{0,4},{8,0},{16,8},{24,16},{28,24},{20,28},{12,20},{4,12},{1,5},{9... | collective-permute-start | bytes 589832 | tf_op jit(solution)/shard_map/ppermute | solution.py:449
  54.5 6.5 %collective-permute-start.26 = (f32[96,128]{1,0:T(8,128)S(1)}, f32[96,128]{1,0:T(8,128)S(1)}, u32[]{:S(2)}, u32[]{:S(2)}) collective-permute-start(f32[96,128]{1,0:T(8,128)S(1)} %compact.1.low_ref), channel_id=1, source_target_pairs={{0,16},{4,20},{8,24},{12,28},{16,0},{20,4},{24,8},{28,12},{1,17},{... | collective-permute-start | bytes 147464 | tf_op jit(solution)/shard_map/ppermute | solution.py:454
  57.2 6.0 %collective-permute-start.25 = (bf16[96,1152]{1,0:T(8,128)(2,1)S(1)}, bf16[96,1152]{1,0:T(8,128)(2,1)S(1)}, u32[]{:S(2)}, u32[]{:S(2)}) collective-permute-start(bf16[96,1152]{1,0:T(8,128)(2,1)S(1)} %add.56.a_ref), channel_id=1, source_target_pairs={{0,2},{1,3},{2,0},{3,1},{4,6},{5,7},{6,4},{7,5},{8,10},{9,11},{10,... | collective-permute-start | bytes 663560 | tf_op jit(solution)/shard_map/ppermute | solution.py:411
  58.6 10.1 %collective-permute-start.23 = (bf16[48,2048]{1,0:T(8,128)(2,1)S(1)}, bf16[48,2048]{1,0:T(8,128)(2,1)S(1)}, u32[]{:S(2)}, u32[]{:S(2)}) collective-permute-start(bf16[48,2048]{1,0:T(8,128)(2,1)S(1)} %get-tuple-element.98), channel_id=1, source_target_pairs={{0,8},{8,16},{16,24},{24,28},{28,20},{20,12},{12,4},{4,0},{1,9},{9... | collective-permute-start | bytes 589832 | tf_op jit(solution)/shard_map/ppermute | solution.py:448
  60.8 7.8 %collective-permute-start.24 = (bf16[48,2048]{1,0:T(8,128)(2,1)S(1)}, bf16[48,2048]{1,0:T(8,128)(2,1)S(1)}, u32[]{:S(2)}, u32[]{:S(2)}) collective-permute-start(bf16[48,2048]{1,0:T(8,128)(2,1)S(1)} %get-tuple-element.99), channel_id=1, source_target_pairs={{0,4},{8,0},{16,8},{24,16},{28,24},{20,28},{12,20},{4,12},{1,5},{9... | collective-permute-start | bytes 589832 | tf_op jit(solution)/shard_map/ppermute | solution.py:449
  63.5 5.2 %collective-permute-start.28 = (f32[96,128]{1,0:T(8,128)S(1)}, f32[96,128]{1,0:T(8,128)S(1)}, u32[]{:S(2)}, u32[]{:S(2)}) collective-permute-start(f32[96,128]{1,0:T(8,128)S(1)} %get-tuple-element.106), channel_id=1, source_target_pairs={{0,8},{4,12},{8,0},{12,4},{16,24},{20,28},{24,16},{28,20},{1,9},{5... | collective-permute-start | bytes 147464 | tf_op jit(solution)/shard_map/ppermute | solution.py:422
  65.6 1.5 %collective-permute-start.27 = (bf16[96,1152]{1,0:T(8,128)(2,1)S(1)}, bf16[96,1152]{1,0:T(8,128)(2,1)S(1)}, u32[]{:S(2)}, u32[]{:S(2)}) collective-permute-start(bf16[96,1152]{1,0:T(8,128)(2,1)S(1)} %get-tuple-element.104.a_ref), channel_id=1, source_target_pairs={{0,1},{1,0},{2,3},{3,2},{4,5},{5,4},{6,7},{7,6},{8,9},{9,8},{10,11... | collective-permute-start | bytes 663560 | tf_op jit(solution)/shard_map/ppermute | solution.py:416
  70.2 1.1 %collective-permute-start.29 = (f32[1,48]{1,0:T(1,128)S(1)}, f32[1,48]{1,0:T(1,128)S(1)}, u32[]{:S(2)}, u32[]{:S(2)}) collective-permute-start(f32[1,48]{1,0:T(1,128)S(1)} %get-tuple-element.116), channel_id=1, source_target_pairs={{0,1},{1,0},{2,3},{3,2},{4,5},{5,4},{6,7},{7,6},{8,9},{9,8},{10,11... | collective-permute-start | bytes 584 | tf_op jit(solution)/shard_map/ppermute | solution.py:503
  71.3 3.5 %collective-permute-start.30 = (f32[1,48]{1,0:T(1,128)S(1)}, f32[1,48]{1,0:T(1,128)S(1)}, u32[]{:S(2)}, u32[]{:S(2)}) collective-permute-start(f32[1,48]{1,0:T(1,128)S(1)} %add.35), channel_id=1, source_target_pairs={{0,2},{1,3},{2,0},{3,1},{4,6},{5,7},{6,4},{7,5},{8,10},{9,11},{10,... | collective-permute-start | bytes 584 | tf_op jit(solution)/shard_map/ppermute | solution.py:503
  (5 other events, 56.3 us)

commit v6 on v5

--- a/solution.py
+++ b/solution.py
@@ -229,7 +229,7 @@
 
         across = lax.ppermute(send, "seq", flip(n, 1))
         going, coming = lax.ppermute(grad, "seq", ring(1)), lax.ppermute(grad, "seq", ring(-1))
-        block = min(64, wsub)
+        block = min(128, wsub)
 
         def dequantize(part, *after):
             return call(

time: 75.5 us -> 75.3 us (level)
  transfers between devices with their start and end apart: 31 -> 31, of which waited for: 12 -> 14; matrix products, arithmetic and copies ran while one was open for 1% -> 1% of each run, Pallas kernels for 24% -> 24%
where the time goes in v6:
time: 75.3 us; the launch traced here: 75.2 us
  starting transfers between devices  33.5 us (44%)
  Pallas kernels  20.8 us (28%)
  waiting for transfers between devices  18.2 us (24%)
  between operations  1.54 us (2%)
  other arithmetic  0.79 us (1%)
    pallas_call x13, Pallas kernels, call(): pl.pallas_call(kernel, out_shape=tuple(outs), in_specs=in_specs or [whole...  20.8 us
    ppermute x3, starting transfers between devices, body(): lax.ppermute(pairs[k], 'seq', flip(n, 2 * k))  4.39 us
    ppermute x2, starting transfers between devices, hop(): lax.ppermute(coming, 'seq', ring(-1))  3.99 us
    ppermute x3, starting transfers between devices, body(): coming = lax.ppermute(there, 'seq', ring(-1))  3.88 us
    ppermute x1, starting transfers between devices, body(): lax.ppermute(grad, 'seq', ring(-1))  2.99 us
    ppermute x2, waiting for transfers between devices, body(): gate_part = gate_part + lax.ppermute(gate_part, 'tp', flip(tp, bit))  2.69 us
    ppermute x3, waiting for transfers between devices, body(): going = lax.ppermute(here, 'seq', ring(1))  2.6 us
    ppermute x3, starting transfers between devices, body(): going = lax.ppermute(here, 'seq', ring(1))  2.49 us
  transfers between devices with their start and end apart: 31, of which 14 were waited for; matrix products, arithmetic and copies ran while one was open for 1% of the time, Pallas kernels for 24%

profile of v6, /device:TPU:0, one launch (start us, length us, event | category | flops | bytes accessed | tf_op | source)
XLA Modules:
  0.0 75.2 jit_solution(8028268574161203177)
XLA Ops:
  1.3 1.6 %prepare.1 = (bf16[4,48,256]{2,1,0:T(8,128)(2,1)S(1)}, bf16[4,48,256]{2,1,0:T(8,128)(2,1)S(1)}, bf16[48,2048]{1,0:T(8,128)(2,1)S(1)}, bf16[48,2048]{1,0:T(8,128)(2,1)S(1)}) custom-call(s32[1]{0:T(128)S(6)} %copy.17.counts_ref, s32[1,48]{1,0:T(1,128)} %bitcast.36, f32[1,48]{1,0:T(1,128)} %bitcast.38, bf16[48,8192]{1,0:T(8,128)(2,1)} %attention_ref.1, ...), custom_call_target="tpu_custom_call" | custom-call | bytes 2163076 | tf_op jit(solution)/shard_map/prepare/pallas_call | solution.py:55
  2.9 3.0 %collective-permute-start.2 = (bf16[48,2048]{1,0:T(8,128)(2,1)S(1)}, bf16[48,2048]{1,0:T(8,128)(2,1)S(1)}, u32[]{:S(2)}, u32[]{:S(2)}) collective-permute-start(bf16[48,2048]{1,0:T(8,128)(2,1)S(1)} %get-tuple-element.64.refs_0_), channel_id=1, source_target_pairs={{0,4},{8,0},{16,8},{24,16},{28,24},{20,28},{12,20},{4,12},{1,5},{9... | collective-permute-start | bytes 589832 | tf_op jit(solution)/shard_map/ppermute | solution.py:231
  6.0 1.9 %collective-permute-start = (bf16[4,48,256]{2,1,0:T(8,128)(2,1)S(1)}, bf16[4,48,256]{2,1,0:T(8,128)(2,1)S(1)}, u32[]{:S(2)}, u32[]{:S(2)}) collective-permute-start(bf16[4,48,256]{2,1,0:T(8,128)(2,1)S(1)} %get-tuple-element.63), channel_id=1, source_target_pairs={{0,4},{4,0},{8,12},{12,8},{16,20},{20,16},{24,28},{28,24},{1,5},{5... | collective-permute-start | bytes 294920 | tf_op jit(solution)/shard_map/ppermute | solution.py:230
  8.1 4.4 %dequantize.2 = (bf16[512,2048]{1,0:T(8,128)(2,1)S(1)}, f32[8,128]{1,0:T(8,128)S(1)}) custom-call(s32[1024,2048]{1,0:T(8,128)} %codes_hbm.3, f32[1024,32]{1,0:T(8,128)S(1)} %copy.15.absmax_ref), custom_call_target="tpu_custom_call" | custom-call | flops 104857600 | bytes 10620928 | tf_op jit(solution)/shard_map/dequantize/pallas_call | solution.py:55
  12.6 1.8 %collective-permute-done.across_ref = bf16[4,48,256]{2,1,0:T(8,128)(2,1)S(1)} collective-permute-done((bf16[4,48,256]{2,1,0:T(8,128)(2,1)S(1)}, bf16[4,48,256]{2,1,0:T(8,128)(2,1)S(1)}, u32[]{:S(2)}, u32[]{:S(2)}) %collective-permute-start) | collective-permute-done | bytes 98336 | tf_op jit(solution)/shard_map/ppermute | solution.py:230
  14.5 2.0 %collective-permute-start.7 = (bf16[48,2048]{1,0:T(8,128)(2,1)S(1)}, bf16[48,2048]{1,0:T(8,128)(2,1)S(1)}, u32[]{:S(2)}, u32[]{:S(2)}) collective-permute-start(bf16[48,2048]{1,0:T(8,128)(2,1)S(1)} %get-tuple-element.77.refs_1_), channel_id=1, source_target_pairs={{0,4},{8,0},{16,8},{24,16},{28,24},{20,28},{12,20},{4,12},{1,5},{9... | collective-permute-start | bytes 589832 | tf_op jit(solution)/shard_map/ppermute | solution.py:252
  16.6 2.9 %collective-permute-start.4 = (bf16[2,48,256]{2,1,0:T(8,128)(2,1)S(1)}, bf16[2,48,256]{2,1,0:T(8,128)(2,1)S(1)}, u32[]{:S(2)}, u32[]{:S(2)}) collective-permute-start(bf16[2,48,256]{2,1,0:T(8,128)(2,1)S(1)} %get-tuple-element.74), channel_id=1, source_target_pairs={{0,16},{4,20},{8,24},{12,28},{16,0},{20,4},{24,8},{28,12},{1,17},{... | collective-permute-start | bytes 147464 | tf_op jit(solution)/shard_map/ppermute | solution.py:272
  19.5 1.4 %collective-permute-start.5 = (bf16[2,48,256]{2,1,0:T(8,128)(2,1)S(1)}, bf16[2,48,256]{2,1,0:T(8,128)(2,1)S(1)}, u32[]{:S(2)}, u32[]{:S(2)}) collective-permute-start(bf16[2,48,256]{2,1,0:T(8,128)(2,1)S(1)} %get-tuple-element.75), channel_id=1, source_target_pairs={{0,24},{4,28},{8,16},{12,20},{16,8},{20,12},{24,0},{28,4},{1,25},{... | collective-permute-start | bytes 147464 | tf_op jit(solution)/shard_map/ppermute | solution.py:272
  20.9 4.5 %dequantize.3 = (bf16[512,2048]{1,0:T(8,128)(2,1)S(1)}, f32[8,128]{1,0:T(8,128)S(1)}) custom-call(s32[1024,2048]{1,0:T(8,128)} %codes_hbm.3, f32[1024,32]{1,0:T(8,128)S(1)} %copy.15.absmax_ref, f32[8,128]{1,0:T(8,128)S(1)} %get-tuple-element.70.refs_0_), custom_call_target="tpu_custom_call" | custom-call | flops 104857600 | bytes 10625024 | tf_op jit(solution)/shard_map/dequantize/pallas_call | solution.py:55
  25.5 1.6 %collective-permute-start.8 = (bf16[384,256]{1,0:T(8,128)(2,1)S(1)}, bf16[384,256]{1,0:T(8,128)(2,1)S(1)}, u32[]{:S(2)}, u32[]{:S(2)}) collective-permute-start(bf16[384,256]{1,0:T(8,128)(2,1)S(1)} %join.1.refs_0_), channel_id=1, source_target_pairs={{0,2},{1,3},{2,0},{3,1},{4,6},{5,7},{6,4},{7,5},{8,10},{9,11},{10,... | collective-permute-start | bytes 589832 | tf_op jit(solution)/shard_map/ppermute | solution.py:283
  27.2 2.0 %collective-permute-start.10 = (bf16[48,2048]{1,0:T(8,128)(2,1)S(1)}, bf16[48,2048]{1,0:T(8,128)(2,1)S(1)}, u32[]{:S(2)}, u32[]{:S(2)}) collective-permute-start(bf16[48,2048]{1,0:T(8,128)(2,1)S(1)} %collective-permute-done.7.refs_2_), channel_id=1, source_target_pairs={{0,4},{8,0},{16,8},{24,16},{28,24},{20,28},{12,20},{4,12},{1,5},{9... | collective-permute-start | bytes 589832 | tf_op jit(solution)/shard_map/ppermute | solution.py:252
  29.2 2.1 %collective-permute-done.8.refs_2_ = bf16[384,256]{1,0:T(8,128)(2,1)S(1)} collective-permute-done((bf16[384,256]{1,0:T(8,128)(2,1)S(1)}, bf16[384,256]{1,0:T(8,128)(2,1)S(1)}, u32[]{:S(2)}, u32[]{:S(2)}) %collective-permute-start.8) | collective-permute-done | bytes 196640 | tf_op jit(solution)/shard_map/ppermute | solution.py:283
  31.3 1.5 %collective-permute-done.9.refs_4_ = bf16[48,2048]{1,0:T(8,128)(2,1)S(1)} collective-permute-done((bf16[48,2048]{1,0:T(8,128)(2,1)S(1)}, bf16[48,2048]{1,0:T(8,128)(2,1)S(1)}, u32[]{:S(2)}, u32[]{:S(2)}) %collective-permute-start.9) | collective-permute-done | bytes 196640 | tf_op jit(solution)/shard_map/ppermute | solution.py:252
  33.4 2.0 %collective-permute-start.16 = (bf16[24,2048]{1,0:T(8,128)(2,1)S(1)}, bf16[24,2048]{1,0:T(8,128)(2,1)S(1)}, u32[]{:S(2)}, u32[]{:S(2)}) collective-permute-start(bf16[24,2048]{1,0:T(8,128)(2,1)S(1)} %slice.65), channel_id=1, source_target_pairs={{0,4},{8,0},{16,8},{24,16},{28,24},{20,28},{12,20},{4,12},{1,5},{9... | collective-permute-start | bytes 294920 | tf_op jit(solution)/shard_map/ppermute | solution.py:290
  35.5 2.5 %forward.1 = (bf16[8,48,2048]{2,1,0:T(8,128)(2,1)S(1)}, f32[192,128]{1,0:T(8,128)S(1)}) custom-call(bf16[64,1024]{1,0:T(8,128)(2,1)S(1)} %bitcast.34, bf16[64,2048]{1,0:T(8,128)(2,1)S(1)} %copy-done.1, bf16[512,2048]{1,0:T(8,128)(2,1)S(1)} %get-tuple-element.61.w0_ref, bf16[512,2048]{1,0:T(8,128)(2,1)S(1)} %get-tuple-element.71.w1_ref, ...), custom_call_target="tpu_custom_call" | custom-call | flops 1610612736 | bytes 7045120 | tf_op jit(solution)/shard_map/forward/pallas_call | solution.py:55
  38.0 2.0 %collective-permute-start.14 = (bf16[24,2048]{1,0:T(8,128)(2,1)S(1)}, bf16[24,2048]{1,0:T(8,128)(2,1)S(1)}, u32[]{:S(2)}, u32[]{:S(2)}) collective-permute-start(bf16[24,2048]{1,0:T(8,128)(2,1)S(1)} %get-tuple-element.122), channel_id=1, source_target_pairs={{0,4},{8,0},{16,8},{24,16},{28,24},{20,28},{12,20},{4,12},{1,5},{9... | collective-permute-start | bytes 294920 | tf_op jit(solution)/shard_map/ppermute | solution.py:329
  40.1 2.5 %backward.1 = (f32[96,1152]{1,0:T(8,128)S(1)}, bf16[96,1152]{1,0:T(8,128)(2,1)S(1)}, bf16[192,2048]{1,0:T(8,128)(2,1)S(1)}, bf16[384,192]{1,0:T(8,128)(2,1)S(1)}) custom-call(bf16[64,2048]{1,0:T(8,128)(2,1)S(1)} %copy-done.1, bf16[512,2048]{1,0:T(8,128)(2,1)S(1)} %get-tuple-element.61.w0_ref, bf16[512,2048]{1,0:T(8,128)(2,1)S(1)} %get-tuple-element.71.w1_ref, ...), custom_call_target="tpu_custom_call" | custom-call | flops 805306368 | bytes 7626752 | tf_op jit(solution)/shard_map/backward/pallas_call | solution.py:55
  42.7 2.0 %collective-permute-done.13 = bf16[24,2048]{1,0:T(8,128)(2,1)S(1)} collective-permute-done((bf16[24,2048]{1,0:T(8,128)(2,1)S(1)}, bf16[24,2048]{1,0:T(8,128)(2,1)S(1)}, u32[]{:S(2)}, u32[]{:S(2)}) %collective-permute-start.13) | collective-permute-done | bytes 98336 | tf_op jit(solution)/shard_map/ppermute | solution.py:329
  44.8 2.0 %collective-permute-start.18 = (bf16[48,2048]{1,0:T(8,128)(2,1)S(1)}, bf16[48,2048]{1,0:T(8,128)(2,1)S(1)}, u32[]{:S(2)}, u32[]{:S(2)}) collective-permute-start(bf16[48,2048]{1,0:T(8,128)(2,1)S(1)} %get-tuple-element.93), channel_id=1, source_target_pairs={{0,4},{8,0},{16,8},{24,16},{28,24},{20,28},{12,20},{4,12},{1,5},{9... | collective-permute-start | bytes 589832 | tf_op jit(solution)/shard_map/ppermute | solution.py:449
  46.8 1.7 %collective-permute-start.20 = (f32[192,128]{1,0:T(8,128)S(1)}, f32[192,128]{1,0:T(8,128)S(1)}, u32[]{:S(2)}, u32[]{:S(2)}) collective-permute-start(f32[192,128]{1,0:T(8,128)S(1)} %get-tuple-element.95.low_ref), channel_id=1, source_target_pairs={{0,4},{4,0},{8,12},{12,8},{16,20},{20,16},{24,28},{28,24},{1,5},{5... | collective-permute-start | bytes 294920 | tf_op jit(solution)/shard_map/ppermute | solution.py:330
  48.5 2.4 %collective-permute-done.17 = bf16[48,2048]{1,0:T(8,128)(2,1)S(1)} collective-permute-done((bf16[48,2048]{1,0:T(8,128)(2,1)S(1)}, bf16[48,2048]{1,0:T(8,128)(2,1)S(1)}, u32[]{:S(2)}, u32[]{:S(2)}) %collective-permute-start.17) | collective-permute-done | bytes 196640 | tf_op jit(solution)/shard_map/ppermute | solution.py:448
  52.1 1.9 %collective-permute-start.22 = (bf16[48,2048]{1,0:T(8,128)(2,1)S(1)}, bf16[48,2048]{1,0:T(8,128)(2,1)S(1)}, u32[]{:S(2)}, u32[]{:S(2)}) collective-permute-start(bf16[48,2048]{1,0:T(8,128)(2,1)S(1)} %get-tuple-element.97), channel_id=1, source_target_pairs={{0,4},{8,0},{16,8},{24,16},{28,24},{20,28},{12,20},{4,12},{1,5},{9... | collective-permute-start | bytes 589832 | tf_op jit(solution)/shard_map/ppermute | solution.py:449
  54.5 2.4 %collective-permute-start.26 = (f32[96,128]{1,0:T(8,128)S(1)}, f32[96,128]{1,0:T(8,128)S(1)}, u32[]{:S(2)}, u32[]{:S(2)}) collective-permute-start(f32[96,128]{1,0:T(8,128)S(1)} %compact.1.low_ref), channel_id=1, source_target_pairs={{0,16},{4,20},{8,24},{12,28},{16,0},{20,4},{24,8},{28,12},{1,17},{... | collective-permute-start | bytes 147464 | tf_op jit(solution)/shard_map/ppermute | solution.py:454
  58.4 2.3 %collective-permute-start.23 = (bf16[48,2048]{1,0:T(8,128)(2,1)S(1)}, bf16[48,2048]{1,0:T(8,128)(2,1)S(1)}, u32[]{:S(2)}, u32[]{:S(2)}) collective-permute-start(bf16[48,2048]{1,0:T(8,128)(2,1)S(1)} %get-tuple-element.98), channel_id=1, source_target_pairs={{0,8},{8,16},{16,24},{24,28},{28,20},{20,12},{12,4},{4,0},{1,9},{9... | collective-permute-start | bytes 589832 | tf_op jit(solution)/shard_map/ppermute | solution.py:448
  60.8 2.3 %collective-permute-done.25.b_ref = bf16[96,1152]{1,0:T(8,128)(2,1)S(1)} collective-permute-done((bf16[96,1152]{1,0:T(8,128)(2,1)S(1)}, bf16[96,1152]{1,0:T(8,128)(2,1)S(1)}, u32[]{:S(2)}, u32[]{:S(2)}) %collective-permute-start.25) | collective-permute-done | bytes 221216 | tf_op jit(solution)/shard_map/ppermute | solution.py:411
  63.3 2.1 %collective-permute-start.28 = (f32[96,128]{1,0:T(8,128)S(1)}, f32[96,128]{1,0:T(8,128)S(1)}, u32[]{:S(2)}, u32[]{:S(2)}) collective-permute-start(f32[96,128]{1,0:T(8,128)S(1)} %get-tuple-element.106), channel_id=1, source_target_pairs={{0,8},{4,12},{8,0},{12,4},{16,24},{20,28},{24,16},{28,20},{1,9},{5... | collective-permute-start | bytes 147464 | tf_op jit(solution)/shard_map/ppermute | solution.py:422
  65.4 1.5 %collective-permute-done.27.b_ref = bf16[96,1152]{1,0:T(8,128)(2,1)S(1)} collective-permute-done((bf16[96,1152]{1,0:T(8,128)(2,1)S(1)}, bf16[96,1152]{1,0:T(8,128)(2,1)S(1)}, u32[]{:S(2)}, u32[]{:S(2)}) %collective-permute-start.27) | collective-permute-done | bytes 221216 | tf_op jit(solution)/shard_map/ppermute | solution.py:416
  66.9 1.6 %last.1 = (bf16[384,1024]{1,0:T(8,128)(2,1)}, f32[64,1024]{1,0:T(8,128)}, f32[8,128]{1,0:T(8,128)S(1)}) custom-call(bf16[96,1152]{1,0:T(8,128)(2,1)S(1)} %get-tuple-element.104.a_ref, bf16[96,1152]{1,0:T(8,128)(2,1)S(1)} %collective-permute-done.27.b_ref, bf16[384,192]{1,0:T(8,128)(2,1)S(1)} %get-tuple-element.103.where_ref, ...), custom_call_target="tpu_custom_call" | custom-call | bytes 2428928 | tf_op jit(solution)/shard_map/last/pallas_call | solution.py:55
  68.5 1.5 %home.1 = (bf16[192,2048]{1,0:T(8,128)(2,1)}, f32[1,48]{1,0:T(1,128)S(1)}) custom-call(s32[1]{0:T(128)S(6)} %copy.17.counts_ref, s32[1,48]{1,0:T(1,128)S(1)} %bitcast.37, f32[1,48]{1,0:T(1,128)S(1)} %bitcast.39, bf16[192,2048]{1,0:T(8,128)(2,1)S(1)} %copy-done, bf16[48,2048]{1,0:T(8,128)(2,1)S(1)} %slice_bitcast_fusion.own_ref, ...), custom_call_target="tpu_custom_call" | custom-call | bytes 2363972 | tf_op jit(solution)/shard_map/home/pallas_call | solution.py:55
  70.2 1.0 %collective-permute-done.29 = f32[1,48]{1,0:T(1,128)S(1)} collective-permute-done((f32[1,48]{1,0:T(1,128)S(1)}, f32[1,48]{1,0:T(1,128)S(1)}, u32[]{:S(2)}, u32[]{:S(2)}) %collective-permute-start.29) | collective-permute-done | bytes 224 | tf_op jit(solution)/shard_map/ppermute | solution.py:503
  71.6 1.3 %up_gradient.1 = f32[64,2048]{1,0:T(8,128)} custom-call(f32[96,128]{1,0:T(8,128)S(1)} %add.34.low_ref, bf16[192,2048]{1,0:T(8,128)(2,1)S(1)} %get-tuple-element.115.g_ref), custom_call_target="tpu_custom_call" | custom-call | flops 150994944 | bytes 1359872 | tf_op jit(solution)/shard_map/up_gradient/pallas_call | solution.py:55
  72.9 1.7 %collective-permute-done.30 = f32[1,48]{1,0:T(1,128)S(1)} collective-permute-done((f32[1,48]{1,0:T(1,128)S(1)}, f32[1,48]{1,0:T(1,128)S(1)}, u32[]{:S(2)}, u32[]{:S(2)}) %collective-permute-start.30) | collective-permute-done | bytes 224 | tf_op jit(solution)/shard_map/ppermute | solution.py:503
  (67 shorter events, 6.4 us)
Async XLA Ops:
  2.9 11.5 %collective-permute-start.2 = (bf16[48,2048]{1,0:T(8,128)(2,1)S(1)}, bf16[48,2048]{1,0:T(8,128)(2,1)S(1)}, u32[]{:S(2)}, u32[]{:S(2)}) collective-permute-start(bf16[48,2048]{1,0:T(8,128)(2,1)S(1)} %get-tuple-element.64.refs_0_), channel_id=1, source_target_pairs={{0,4},{8,0},{16,8},{24,16},{28,24},{20,28},{12,20},{4,12},{1,5},{9... | collective-permute-start | bytes 589832 | tf_op jit(solution)/shard_map/ppermute | solution.py:231
  5.9 8.5 %collective-permute-start.1 = (bf16[48,2048]{1,0:T(8,128)(2,1)S(1)}, bf16[48,2048]{1,0:T(8,128)(2,1)S(1)}, u32[]{:S(2)}, u32[]{:S(2)}) collective-permute-start(bf16[48,2048]{1,0:T(8,128)(2,1)S(1)} %get-tuple-element.64.refs_0_), channel_id=1, source_target_pairs={{0,8},{8,16},{16,24},{24,28},{28,20},{20,12},{12,4},{4,0},{1,9},{9... | collective-permute-start | bytes 589832 | tf_op jit(solution)/shard_map/ppermute | solution.py:231
  6.0 8.3 %collective-permute-start = (bf16[4,48,256]{2,1,0:T(8,128)(2,1)S(1)}, bf16[4,48,256]{2,1,0:T(8,128)(2,1)S(1)}, u32[]{:S(2)}, u32[]{:S(2)}) collective-permute-start(bf16[4,48,256]{2,1,0:T(8,128)(2,1)S(1)} %get-tuple-element.63), channel_id=1, source_target_pairs={{0,4},{4,0},{8,12},{12,8},{16,20},{20,16},{24,28},{28,24},{1,5},{5... | collective-permute-start | bytes 294920 | tf_op jit(solution)/shard_map/ppermute | solution.py:230
  14.4 11.1 %collective-permute-start.6 = (bf16[48,2048]{1,0:T(8,128)(2,1)S(1)}, bf16[48,2048]{1,0:T(8,128)(2,1)S(1)}, u32[]{:S(2)}, u32[]{:S(2)}) collective-permute-start(bf16[48,2048]{1,0:T(8,128)(2,1)S(1)} %get-tuple-element.76.refs_6_), channel_id=1, source_target_pairs={{0,8},{8,16},{16,24},{24,28},{28,20},{20,12},{12,4},{4,0},{1,9},{9... | collective-permute-start | bytes 589832 | tf_op jit(solution)/shard_map/ppermute | solution.py:252
  14.5 11.0 %collective-permute-start.7 = (bf16[48,2048]{1,0:T(8,128)(2,1)S(1)}, bf16[48,2048]{1,0:T(8,128)(2,1)S(1)}, u32[]{:S(2)}, u32[]{:S(2)}) collective-permute-start(bf16[48,2048]{1,0:T(8,128)(2,1)S(1)} %get-tuple-element.77.refs_1_), channel_id=1, source_target_pairs={{0,4},{8,0},{16,8},{24,16},{28,24},{20,28},{12,20},{4,12},{1,5},{9... | collective-permute-start | bytes 589832 | tf_op jit(solution)/shard_map/ppermute | solution.py:252
  16.5 8.9 %collective-permute-start.3 = (bf16[2,48,256]{2,1,0:T(8,128)(2,1)S(1)}, bf16[2,48,256]{2,1,0:T(8,128)(2,1)S(1)}, u32[]{:S(2)}, u32[]{:S(2)}) collective-permute-start(bf16[2,48,256]{2,1,0:T(8,128)(2,1)S(1)} %get-tuple-element.73), channel_id=1, source_target_pairs={{0,8},{4,12},{8,0},{12,4},{16,24},{20,28},{24,16},{28,20},{1,9},{5... | collective-permute-start | bytes 147464 | tf_op jit(solution)/shard_map/ppermute | solution.py:272
  16.6 8.8 %collective-permute-start.4 = (bf16[2,48,256]{2,1,0:T(8,128)(2,1)S(1)}, bf16[2,48,256]{2,1,0:T(8,128)(2,1)S(1)}, u32[]{:S(2)}, u32[]{:S(2)}) collective-permute-start(bf16[2,48,256]{2,1,0:T(8,128)(2,1)S(1)} %get-tuple-element.74), channel_id=1, source_target_pairs={{0,16},{4,20},{8,24},{12,28},{16,0},{20,4},{24,8},{28,12},{1,17},{... | collective-permute-start | bytes 147464 | tf_op jit(solution)/shard_map/ppermute | solution.py:272
  19.5 6.1 %collective-permute-start.5 = (bf16[2,48,256]{2,1,0:T(8,128)(2,1)S(1)}, bf16[2,48,256]{2,1,0:T(8,128)(2,1)S(1)}, u32[]{:S(2)}, u32[]{:S(2)}) collective-permute-start(bf16[2,48,256]{2,1,0:T(8,128)(2,1)S(1)} %get-tuple-element.75), channel_id=1, source_target_pairs={{0,24},{4,28},{8,16},{12,20},{16,8},{20,12},{24,0},{28,4},{1,25},{... | collective-permute-start | bytes 147464 | tf_op jit(solution)/shard_map/ppermute | solution.py:272
  20.9 14.6 %copy-start.2 = (bf16[1024,64]{0,1:T(8,128)(2,1)S(1)}, bf16[1024,64]{0,1:T(8,128)(2,1)}, u32[]{:S(2)}) copy-start(bf16[1024,64]{0,1:T(8,128)(2,1)} %param.14) | copy-start | bytes 393220
  25.5 5.7 %collective-permute-start.8 = (bf16[384,256]{1,0:T(8,128)(2,1)S(1)}, bf16[384,256]{1,0:T(8,128)(2,1)S(1)}, u32[]{:S(2)}, u32[]{:S(2)}) collective-permute-start(bf16[384,256]{1,0:T(8,128)(2,1)S(1)} %join.1.refs_0_), channel_id=1, source_target_pairs={{0,2},{1,3},{2,0},{3,1},{4,6},{5,7},{6,4},{7,5},{8,10},{9,11},{10,... | collective-permute-start | bytes 589832 | tf_op jit(solution)/shard_map/ppermute | solution.py:283
  27.1 5.7 %collective-permute-start.9 = (bf16[48,2048]{1,0:T(8,128)(2,1)S(1)}, bf16[48,2048]{1,0:T(8,128)(2,1)S(1)}, u32[]{:S(2)}, u32[]{:S(2)}) collective-permute-start(bf16[48,2048]{1,0:T(8,128)(2,1)S(1)} %collective-permute-done.6.refs_5_), channel_id=1, source_target_pairs={{0,8},{8,16},{16,24},{24,28},{28,20},{20,12},{12,4},{4,0},{1,9},{9... | collective-permute-start | bytes 589832 | tf_op jit(solution)/shard_map/ppermute | solution.py:252
  27.2 5.7 %collective-permute-start.10 = (bf16[48,2048]{1,0:T(8,128)(2,1)S(1)}, bf16[48,2048]{1,0:T(8,128)(2,1)S(1)}, u32[]{:S(2)}, u32[]{:S(2)}) collective-permute-start(bf16[48,2048]{1,0:T(8,128)(2,1)S(1)} %collective-permute-done.7.refs_2_), channel_id=1, source_target_pairs={{0,4},{8,0},{16,8},{24,16},{28,24},{20,28},{12,20},{4,12},{1,5},{9... | collective-permute-start | bytes 589832 | tf_op jit(solution)/shard_map/ppermute | solution.py:252
  32.8 2.6 %collective-permute-start.11 = (bf16[384,256]{1,0:T(8,128)(2,1)S(1)}, bf16[384,256]{1,0:T(8,128)(2,1)S(1)}, u32[]{:S(2)}, u32[]{:S(2)}) collective-permute-start(bf16[384,256]{1,0:T(8,128)(2,1)S(1)} %join.1.refs_0_), channel_id=1, source_target_pairs={{0,1},{1,0},{2,3},{3,2},{4,5},{5,4},{6,7},{7,6},{8,9},{9,8},{10,11... | collective-permute-start | bytes 589832 | tf_op jit(solution)/shard_map/ppermute | solution.py:285
  32.8 2.6 %collective-permute-start.12 = (bf16[384,256]{1,0:T(8,128)(2,1)S(1)}, bf16[384,256]{1,0:T(8,128)(2,1)S(1)}, u32[]{:S(2)}, u32[]{:S(2)}) collective-permute-start(bf16[384,256]{1,0:T(8,128)(2,1)S(1)} %collective-permute-done.8.refs_2_), channel_id=1, source_target_pairs={{0,1},{1,0},{2,3},{3,2},{4,5},{5,4},{6,7},{7,6},{8,9},{9,8},{10,11... | collective-permute-start | bytes 589832 | tf_op jit(solution)/shard_map/ppermute | solution.py:285
  33.4 6.7 %collective-permute-start.16 = (bf16[24,2048]{1,0:T(8,128)(2,1)S(1)}, bf16[24,2048]{1,0:T(8,128)(2,1)S(1)}, u32[]{:S(2)}, u32[]{:S(2)}) collective-permute-start(bf16[24,2048]{1,0:T(8,128)(2,1)S(1)} %slice.65), channel_id=1, source_target_pairs={{0,4},{8,0},{16,8},{24,16},{28,24},{20,28},{12,20},{4,12},{1,5},{9... | collective-permute-start | bytes 294920 | tf_op jit(solution)/shard_map/ppermute | solution.py:290
  35.4 4.7 %collective-permute-start.15 = (bf16[24,2048]{1,0:T(8,128)(2,1)S(1)}, bf16[24,2048]{1,0:T(8,128)(2,1)S(1)}, u32[]{:S(2)}, u32[]{:S(2)}) collective-permute-start(bf16[24,2048]{1,0:T(8,128)(2,1)S(1)} %slice.64), channel_id=1, source_target_pairs={{0,8},{8,16},{16,24},{24,28},{28,20},{20,12},{12,4},{4,0},{1,9},{9... | collective-permute-start | bytes 294920 | tf_op jit(solution)/shard_map/ppermute | solution.py:289
  38.0 4.7 %collective-permute-start.14 = (bf16[24,2048]{1,0:T(8,128)(2,1)S(1)}, bf16[24,2048]{1,0:T(8,128)(2,1)S(1)}, u32[]{:S(2)}, u32[]{:S(2)}) collective-permute-start(bf16[24,2048]{1,0:T(8,128)(2,1)S(1)} %get-tuple-element.122), channel_id=1, source_target_pairs={{0,4},{8,0},{16,8},{24,16},{28,24},{20,28},{12,20},{4,12},{1,5},{9... | collective-permute-start | bytes 294920 | tf_op jit(solution)/shard_map/ppermute | solution.py:329
  40.0 4.6 %collective-permute-start.13 = (bf16[24,2048]{1,0:T(8,128)(2,1)S(1)}, bf16[24,2048]{1,0:T(8,128)(2,1)S(1)}, u32[]{:S(2)}, u32[]{:S(2)}) collective-permute-start(bf16[24,2048]{1,0:T(8,128)(2,1)S(1)} %get-tuple-element.124), channel_id=1, source_target_pairs={{0,8},{8,16},{16,24},{24,28},{28,20},{20,12},{12,4},{4,0},{1,9},{9... | collective-permute-start | bytes 294920 | tf_op jit(solution)/shard_map/ppermute | solution.py:329
  44.7 6.2 %collective-permute-start.17 = (bf16[48,2048]{1,0:T(8,128)(2,1)S(1)}, bf16[48,2048]{1,0:T(8,128)(2,1)S(1)}, u32[]{:S(2)}, u32[]{:S(2)}) collective-permute-start(bf16[48,2048]{1,0:T(8,128)(2,1)S(1)} %get-tuple-element.92), channel_id=1, source_target_pairs={{0,8},{8,16},{16,24},{24,28},{28,20},{20,12},{12,4},{4,0},{1,9},{9... | collective-permute-start | bytes 589832 | tf_op jit(solution)/shard_map/ppermute | solution.py:448
  44.8 6.1 %collective-permute-start.18 = (bf16[48,2048]{1,0:T(8,128)(2,1)S(1)}, bf16[48,2048]{1,0:T(8,128)(2,1)S(1)}, u32[]{:S(2)}, u32[]{:S(2)}) collective-permute-start(bf16[48,2048]{1,0:T(8,128)(2,1)S(1)} %get-tuple-element.93), channel_id=1, source_target_pairs={{0,4},{8,0},{16,8},{24,16},{28,24},{20,28},{12,20},{4,12},{1,5},{9... | collective-permute-start | bytes 589832 | tf_op jit(solution)/shard_map/ppermute | solution.py:449
  46.8 5.2 %collective-permute-start.20 = (f32[192,128]{1,0:T(8,128)S(1)}, f32[192,128]{1,0:T(8,128)S(1)}, u32[]{:S(2)}, u32[]{:S(2)}) collective-permute-start(f32[192,128]{1,0:T(8,128)S(1)} %get-tuple-element.95.low_ref), channel_id=1, source_target_pairs={{0,4},{4,0},{8,12},{12,8},{16,20},{20,16},{24,28},{28,24},{1,5},{5... | collective-permute-start | bytes 294920 | tf_op jit(solution)/shard_map/ppermute | solution.py:330
  48.5 3.5 %collective-permute-start.19 = (bf16[96,1152]{1,0:T(8,128)(2,1)S(1)}, bf16[96,1152]{1,0:T(8,128)(2,1)S(1)}, u32[]{:S(2)}, u32[]{:S(2)}) collective-permute-start(bf16[96,1152]{1,0:T(8,128)(2,1)S(1)} %get-tuple-element.94), channel_id=1, source_target_pairs={{0,1},{1,0},{2,3},{3,2},{4,5},{5,4},{6,7},{7,6},{8,9},{9,8},{10,11... | collective-permute-start | bytes 663560 | tf_op jit(solution)/shard_map/ppermute | solution.py:404
  52.0 5.9 %collective-permute-start.21 = (bf16[48,2048]{1,0:T(8,128)(2,1)S(1)}, bf16[48,2048]{1,0:T(8,128)(2,1)S(1)}, u32[]{:S(2)}, u32[]{:S(2)}) collective-permute-start(bf16[48,2048]{1,0:T(8,128)(2,1)S(1)} %get-tuple-element.96), channel_id=1, source_target_pairs={{0,8},{8,16},{16,24},{24,28},{28,20},{20,12},{12,4},{4,0},{1,9},{9... | collective-permute-start | bytes 589832 | tf_op jit(solution)/shard_map/ppermute | solution.py:448
  52.1 6.2 %collective-permute-start.22 = (bf16[48,2048]{1,0:T(8,128)(2,1)S(1)}, bf16[48,2048]{1,0:T(8,128)(2,1)S(1)}, u32[]{:S(2)}, u32[]{:S(2)}) collective-permute-start(bf16[48,2048]{1,0:T(8,128)(2,1)S(1)} %get-tuple-element.97), channel_id=1, source_target_pairs={{0,4},{8,0},{16,8},{24,16},{28,24},{20,28},{12,20},{4,12},{1,5},{9... | collective-permute-start | bytes 589832 | tf_op jit(solution)/shard_map/ppermute | solution.py:449
  54.5 6.3 %collective-permute-start.26 = (f32[96,128]{1,0:T(8,128)S(1)}, f32[96,128]{1,0:T(8,128)S(1)}, u32[]{:S(2)}, u32[]{:S(2)}) collective-permute-start(f32[96,128]{1,0:T(8,128)S(1)} %compact.1.low_ref), channel_id=1, source_target_pairs={{0,16},{4,20},{8,24},{12,28},{16,0},{20,4},{24,8},{28,12},{1,17},{... | collective-permute-start | bytes 147464 | tf_op jit(solution)/shard_map/ppermute | solution.py:454
  57.1 6.0 %collective-permute-start.25 = (bf16[96,1152]{1,0:T(8,128)(2,1)S(1)}, bf16[96,1152]{1,0:T(8,128)(2,1)S(1)}, u32[]{:S(2)}, u32[]{:S(2)}) collective-permute-start(bf16[96,1152]{1,0:T(8,128)(2,1)S(1)} %add.56.a_ref), channel_id=1, source_target_pairs={{0,2},{1,3},{2,0},{3,1},{4,6},{5,7},{6,4},{7,5},{8,10},{9,11},{10,... | collective-permute-start | bytes 663560 | tf_op jit(solution)/shard_map/ppermute | solution.py:411
  58.4 10.1 %collective-permute-start.23 = (bf16[48,2048]{1,0:T(8,128)(2,1)S(1)}, bf16[48,2048]{1,0:T(8,128)(2,1)S(1)}, u32[]{:S(2)}, u32[]{:S(2)}) collective-permute-start(bf16[48,2048]{1,0:T(8,128)(2,1)S(1)} %get-tuple-element.98), channel_id=1, source_target_pairs={{0,8},{8,16},{16,24},{24,28},{28,20},{20,12},{12,4},{4,0},{1,9},{9... | collective-permute-start | bytes 589832 | tf_op jit(solution)/shard_map/ppermute | solution.py:448
  60.7 7.8 %collective-permute-start.24 = (bf16[48,2048]{1,0:T(8,128)(2,1)S(1)}, bf16[48,2048]{1,0:T(8,128)(2,1)S(1)}, u32[]{:S(2)}, u32[]{:S(2)}) collective-permute-start(bf16[48,2048]{1,0:T(8,128)(2,1)S(1)} %get-tuple-element.99), channel_id=1, source_target_pairs={{0,4},{8,0},{16,8},{24,16},{28,24},{20,28},{12,20},{4,12},{1,5},{9... | collective-permute-start | bytes 589832 | tf_op jit(solution)/shard_map/ppermute | solution.py:449
  63.3 5.2 %collective-permute-start.28 = (f32[96,128]{1,0:T(8,128)S(1)}, f32[96,128]{1,0:T(8,128)S(1)}, u32[]{:S(2)}, u32[]{:S(2)}) collective-permute-start(f32[96,128]{1,0:T(8,128)S(1)} %get-tuple-element.106), channel_id=1, source_target_pairs={{0,8},{4,12},{8,0},{12,4},{16,24},{20,28},{24,16},{28,20},{1,9},{5... | collective-permute-start | bytes 147464 | tf_op jit(solution)/shard_map/ppermute | solution.py:422
  65.4 1.5 %collective-permute-start.27 = (bf16[96,1152]{1,0:T(8,128)(2,1)S(1)}, bf16[96,1152]{1,0:T(8,128)(2,1)S(1)}, u32[]{:S(2)}, u32[]{:S(2)}) collective-permute-start(bf16[96,1152]{1,0:T(8,128)(2,1)S(1)} %get-tuple-element.104.a_ref), channel_id=1, source_target_pairs={{0,1},{1,0},{2,3},{3,2},{4,5},{5,4},{6,7},{7,6},{8,9},{9,8},{10,11... | collective-permute-start | bytes 663560 | tf_op jit(solution)/shard_map/ppermute | solution.py:416
  70.0 1.1 %collective-permute-start.29 = (f32[1,48]{1,0:T(1,128)S(1)}, f32[1,48]{1,0:T(1,128)S(1)}, u32[]{:S(2)}, u32[]{:S(2)}) collective-permute-start(f32[1,48]{1,0:T(1,128)S(1)} %get-tuple-element.116), channel_id=1, source_target_pairs={{0,1},{1,0},{2,3},{3,2},{4,5},{5,4},{6,7},{7,6},{8,9},{9,8},{10,11... | collective-permute-start | bytes 584 | tf_op jit(solution)/shard_map/ppermute | solution.py:503
  71.1 3.5 %collective-permute-start.30 = (f32[1,48]{1,0:T(1,128)S(1)}, f32[1,48]{1,0:T(1,128)S(1)}, u32[]{:S(2)}, u32[]{:S(2)}) collective-permute-start(f32[1,48]{1,0:T(1,128)S(1)} %add.35), channel_id=1, source_target_pairs={{0,2},{1,3},{2,0},{3,1},{4,6},{5,7},{6,4},{7,5},{8,10},{9,11},{10,... | collective-permute-start | bytes 584 | tf_op jit(solution)/shard_map/ppermute | solution.py:503
  (5 other events, 56.3 us)
